TPU v7x, 512 devices: a whole 4x8x8 slice. The times are simulated.
512 devices in a mesh: img: 16 (over y_lo, x), blk: 32 (over y_hi, z, core).
Axes of the slice: x: 4, y: 8 (y_hi: 2, y_lo: 4; y = y_hi * 4 + y_lo), z: 8, core: 2. Of those that a mesh axis runs over, the one named last changes fastest.
Arguments:
- jac_cam: bfloat16 [16, 32, 1536, 128], P('img', 'blk')
- jac_tex: bfloat16 [16, 32, 1536, 256], P('img', 'blk')
- residual: bfloat16 [16, 32, 1536], P('img', 'blk'), may hold values from -6 to 6
- obs_slot: int32 [16, 32, 192], P('img', 'blk'), may hold values from 0 to 15, never falling along the last dimension, each value on 1 to 36 neighbouring positions
- col_ids: int32 [512], P('blk'), may hold values from 0 to 511, each once
- block_pattern: int32 [512], replicated, may hold values from 0 to 3, as said below
- damping: float32 [], replicated, may hold values from 0.1 to 1
Outputs:
- reduced_blocks: float32 [32, 16, 128, 128], P('blk', 'img')
- reduced_gradient: float32 [32, 16, 128], P('blk', 'img')
- coupling_factor: float32 [32, 16, 128, 256], P('blk', 'img')
- texture_factor: float32 [256, 256], replicated
Inputs may be any that keep to these rules, and one draw needn't show every extreme that they name: `obs_slot`: Non-decreasing along each device's observations; every slot 0 to 15 has 1 to 36 observations on every device, and some slot exactly 36. `col_ids`: each global block column appears once. `block_pattern`: bit 0 marks coupling with texture panel 0, bit 1 with panel 1; exactly 128 columns carry code 1, exactly 128 carry code 2, exactly 2 carry code 0, and all others code 3.
All inputs are finite; a program needn't handle non-finite values.
Results may differ from a plain program's by a relative error of at most 0.00095.
Values sent between devices are 32-bit elements; how exact they have to be, the bound alone decides.
No kernel may reach another device: no remote copies, remote signals or barrier semaphores. Data moves between devices by JAX's collectives and lax.ppermute only.
A program may use at most 64 MiB of HBM per device.

v0:
```python
import jax
import jax.numpy as jnp
from jax import lax
from jax.sharding import PartitionSpec as P

BLOCK = 128
MOST = 36


def exact_dot(left, right):
    return jnp.dot(left, right, precision=lax.Precision.HIGHEST, preferred_element_type=jnp.float32)


def tri_inverse(lower_factor):
    identity = jnp.eye(lower_factor.shape[0], dtype=jnp.float32)
    return lax.linalg.triangular_solve(lower_factor, identity, left_side=True, lower=True)


def device_partial(jac_cam, jac_tex, residual, obs_slot, slot_codes):
    row_count = jac_cam.shape[0]
    repeat_count = row_count // obs_slot.shape[0]
    slot_count = slot_codes.shape[0]
    slot_range = jnp.arange(slot_count)
    row_slot = jnp.repeat(obs_slot, repeat_count)
    onehot = row_slot[:, None] == slot_range[None, :]
    row_code = jnp.sum(jnp.where(onehot, slot_codes[None, :], 0), axis=1)
    half_cols = jac_tex.shape[1] // 2
    keep_first = row_code % 2 == 1
    keep_second = row_code // 2 == 1
    col_first = jnp.arange(jac_tex.shape[1]) < half_cols
    keep = jnp.where(col_first[None, :], keep_first[:, None], keep_second[:, None])
    masked_tex = jnp.where(keep, jac_tex, jnp.zeros_like(jac_tex))
    tex_hess = jnp.dot(masked_tex.T, masked_tex, preferred_element_type=jnp.float32)
    tex_grad = jnp.dot(residual, masked_tex, preferred_element_type=jnp.float32)
    starts = (
        jnp.sum((obs_slot[None, :] < slot_range[:, None]).astype(jnp.int32), axis=1) * repeat_count
    )
    window_rows = min(MOST * repeat_count, row_count)

    def one_slot(slot_index):
        window_start = jnp.minimum(starts[slot_index], row_count - window_rows)
        cam_rows = lax.dynamic_slice_in_dim(jac_cam, window_start, window_rows, 0)
        tex_rows = lax.dynamic_slice_in_dim(masked_tex, window_start, window_rows, 0)
        res_rows = lax.dynamic_slice_in_dim(residual, window_start, window_rows, 0)
        row_match = lax.dynamic_slice_in_dim(row_slot, window_start, window_rows, 0) == slot_index
        picked = jnp.where(row_match[:, None], cam_rows, jnp.zeros_like(cam_rows))
        cam_hess = jnp.dot(picked.T, cam_rows, preferred_element_type=jnp.float32)
        cam_cross = jnp.dot(picked.T, tex_rows, preferred_element_type=jnp.float32)
        cam_grad = jnp.dot(res_rows, picked, preferred_element_type=jnp.float32)
        return (cam_hess, cam_cross, cam_grad)

    cam_hess, cam_cross, cam_grad = lax.map(one_slot, slot_range)
    return (cam_hess, cam_cross, cam_grad, tex_hess, tex_grad)


def first_panel(damped, tex_grad):
    half_cols = damped.shape[0] // 2
    low_first = jnp.linalg.cholesky(damped[:half_cols, :half_cols])
    inv_first = tri_inverse(low_first)
    low_cross = exact_dot(damped[half_cols:, :half_cols], inv_first.T)
    sol_first = exact_dot(inv_first, tex_grad[:half_cols])
    return (low_first, low_cross, inv_first, sol_first)


def second_panel(damped, tex_grad, low_cross, inv_first, sol_first):
    half_cols = damped.shape[0] // 2
    updated = damped[half_cols:, half_cols:] - exact_dot(low_cross, low_cross.T)
    low_second = jnp.linalg.cholesky(updated)
    inv_second = tri_inverse(low_second)
    inv_cross = -exact_dot(inv_second, exact_dot(low_cross, inv_first))
    sol_second = exact_dot(inv_second, tex_grad[half_cols:] - exact_dot(low_cross, sol_first))
    return (low_second, inv_second, inv_cross, sol_second)


def shards(jac_cam, jac_tex, residual, obs_slot, col_ids, block_pattern, damping):
    slot_count = col_ids.shape[0]
    block_range = jnp.arange(block_pattern.shape[0])
    matches = col_ids[:, None] == block_range[None, :]
    slot_codes = jnp.sum(jnp.where(matches, block_pattern[None, :], 0), axis=1)
    cam_hess, cam_cross, cam_grad, tex_hess, tex_grad = device_partial(
        jac_cam[0, 0], jac_tex[0, 0], residual[0, 0], obs_slot[0, 0], slot_codes
    )
    tex_hess, tex_grad = lax.psum((tex_hess, tex_grad), ("img", "blk"))
    share_count = slot_count // lax.axis_size("img")
    cam_hess, cam_cross, cam_grad = lax.psum((cam_hess, cam_cross, cam_grad), "img")
    first_slot = lax.axis_index("img") * share_count
    cam_hess = lax.dynamic_slice_in_dim(cam_hess, first_slot, share_count, 0)
    cam_cross = lax.dynamic_slice_in_dim(cam_cross, first_slot, share_count, 0)
    cam_grad = lax.dynamic_slice_in_dim(cam_grad, first_slot, share_count, 0)
    damped = tex_hess + damping * jnp.diag(jnp.diagonal(tex_hess))
    low_first, low_cross, inv_first, sol_first = first_panel(damped, tex_grad)
    low_second, inv_second, inv_cross, sol_second = second_panel(
        damped, tex_grad, low_cross, inv_first, sol_first
    )
    blank = jnp.zeros((BLOCK, BLOCK), jnp.float32)
    texture_factor = jnp.concatenate(
        [jnp.concatenate([low_first, blank], 1), jnp.concatenate([low_cross, low_second], 1)], 0
    )
    inverse = jnp.concatenate(
        [jnp.concatenate([inv_first, blank], 1), jnp.concatenate([inv_cross, inv_second], 1)], 0
    )
    solution = jnp.concatenate([sol_first, sol_second], 0)
    coupling = jnp.einsum("abp,qp->abq", cam_cross, inverse, precision=lax.Precision.HIGHEST)
    identity = jnp.eye(BLOCK, dtype=jnp.float32)
    reduced = (
        cam_hess
        + damping * (cam_hess * identity)
        - jnp.einsum("abp,acp->abc", coupling, coupling, precision=lax.Precision.HIGHEST)
    )
    gradient = cam_grad - jnp.einsum(
        "abp,p->ab", coupling, solution, precision=lax.Precision.HIGHEST
    )
    return (reduced[None], gradient[None], coupling[None], texture_factor)


def solution(mesh):
    return jax.shard_map(
        shards,
        mesh=mesh,
        in_specs=(
            P("img", "blk", None, None),
            P("img", "blk", None, None),
            P("img", "blk", None),
            P("img", "blk", None),
            P("blk"),
            P(),
            P(),
        ),
        out_specs=(
            P("blk", "img", None, None),
            P("blk", "img", None),
            P("blk", "img", None, None),
            P(),
        ),
        check_vma=False,
    )
```

profile of v0, /device:TPU:1, one launch (start us, length us, event | category | flops | bytes accessed | tf_op | source)
XLA Modules:
  0.0 467.1 jit_solution(272058278508938352)
XLA Ops:
  7.2 0.8 broadcast_in_dim.138
  8.2 0.9 select_reduce_fusion.3
  9.2 2.0 fusion.27
  11.2 1.1 fusion.63
  12.4 1.0 select_select_fusion.1
  13.6 107.8 %while.14 = (s32[]{:T(128)}, f32[16,128,128]{2,1,0:T(8,128)}, f32[16,128,256]{2,1,0:T(8,128)}, f32[16,128]{1,0:T(8,128)S(1)}, s32[16]{0:T(128)S(1)}, /*index=5*/...) while((s32[]{:T(128)}, f32[16,128,128]{2,1,0:T(8,128)}, ...), condition=%wide.region_4.5_spmd, body=%wide.region_3.4_spmd.sunk | while | flops 28496168 | bytes 650665 | solution.py:52
  17.4 0.7 dynamic-slice_compare_fusion.2
  18.2 1.0 fusion.100
  19.1 0.9 fusion.99
  24.2 0.7 dynamic-slice_compare_fusion.2
  24.9 1.0 fusion.100
  25.9 0.9 fusion.99
  30.9 0.7 dynamic-slice_compare_fusion.2
  31.6 1.0 fusion.100
  32.6 0.9 fusion.99
  38.4 1.0 fusion.100
  39.3 0.9 fusion.99
  44.4 0.7 dynamic-slice_compare_fusion.2
  45.1 1.0 fusion.100
  46.1 0.9 fusion.99
  51.1 0.7 dynamic-slice_compare_fusion.2
  51.9 1.0 fusion.100
  52.8 0.9 fusion.99
  57.9 0.7 dynamic-slice_compare_fusion.2
  58.6 1.0 fusion.100
  59.6 0.9 fusion.99
  64.6 0.7 dynamic-slice_compare_fusion.2
  65.3 1.0 fusion.100
  66.3 0.9 fusion.99
  71.4 0.7 dynamic-slice_compare_fusion.2
  72.1 1.0 fusion.100
  73.1 0.9 fusion.99
  78.1 0.7 dynamic-slice_compare_fusion.2
  78.8 1.0 fusion.100
  79.8 0.9 fusion.99
  85.6 1.0 fusion.100
  86.5 0.9 fusion.99
  91.6 0.7 dynamic-slice_compare_fusion.2
  92.3 1.0 fusion.100
  93.3 0.9 fusion.99
  98.3 0.7 dynamic-slice_compare_fusion.2
  99.0 1.0 fusion.100
  100.0 0.9 fusion.99
  105.0 0.7 dynamic-slice_compare_fusion.2
  105.8 1.0 fusion.100
  106.7 0.9 fusion.99
  111.8 0.7 dynamic-slice_compare_fusion.2
  112.5 1.0 fusion.100
  113.5 0.9 fusion.99
  119.2 1.0 fusion.100
  120.2 0.9 fusion.99
  122.4 107.1 %psum.39 = f32[256]{0:T(256)S(1)} all-reduce(f32[256]{0:T(256)S(1)} %bitcast.107), channel_id=1, replica_groups=mesh['img'=16,'blk'=32] {'img','blk'}, use_global_device_ids=true, to_apply=%region_11.14 | all-reduce | flops 256 | bytes 2048 | tf_op jit(solution)/shard_map/psum | solution.py:83
  229.5 34.5 %psum.38 = f32[16,128]{1,0:T(8,128)S(1)} all-reduce(f32[16,128]{1,0:T(8,128)S(1)} %get-tuple-element.62), channel_id=1, replica_groups=mesh['img'=16,'blk'=32] {'img'}, use_global_device_ids=true, to_apply=%region_10.13 | all-reduce | flops 2048 | bytes 16384 | tf_op jit(solution)/shard_map/psum | solution.py:85
  264.1 22.7 %all-reduce.6.cloned.1.call-done = f32[256,256]{0,1:T(8,128)} async-done(((f32[256,256]{0,1:T(8,128)}), f32[256,256]{0,1:T(8,128)}) %all-reduce.6.cloned.1.call-update) | async-done | bytes 262160 | tf_op jit(solution)/shard_map/psum | solution.py:83
  286.7 2.6 gather_fusion
  289.3 1.0 multiply_add_fusion
  290.5 11.7 %cholesky.44 = f32[128,128]{1,0:T(8,128)S(1)} custom-call(f32[128,128]{1,0:T(8,128)S(1)} %fusion.46), custom_call_target="Cholesky" | custom-call | tf_op jit(solution)/shard_map/jit(cholesky)/cholesky | solution.py:58
  303.5 9.8 %custom-call.8 = f32[1,128,128]{1,2,0:T(8,128)S(1)} custom-call(f32[1,128,128]{2,1,0:T(8,128)S(1)} %get-tuple-element.87), custom_call_target="InvertDiagBlocksLowerTriangular" | custom-call | tf_op jit(solution)/shard_map/triangular_solve/custom-call.0 | solution.py:16
  314.3 11.7 %cholesky.55 = f32[128,128]{1,0:T(8,128)S(1)} custom-call(f32[128,128]{1,0:T(8,128)S(1)} %fusion.44), custom_call_target="Cholesky" | custom-call | tf_op jit(solution)/shard_map/jit(cholesky)/cholesky | solution.py:68
  327.4 10.0 %custom-call.9 = f32[1,128,128]{1,2,0:T(8,128)S(1)} custom-call(f32[1,128,128]{2,1,0:T(8,128)S(1)} %get-tuple-element.85), custom_call_target="InvertDiagBlocksLowerTriangular" | custom-call | tf_op jit(solution)/shard_map/triangular_solve/custom-call.0 | solution.py:16
  339.6 116.8 %all-reduce.8.cloned.1.call-done = (f32[16,128,256]{2,1,0:T(8,128)}, f32[16,128,128]{2,1,0:T(8,128)}) async-done(((f32[16,128,256]{2,1,0:T(8,128)}, f32[16,128,128]{2,1,0:T(8,128)}), (f32[16,128,256]{2,1,0:T(8,128)}, f32[16,128,128]{2,1,0:T(8,128)})) %all-reduce.8.cloned.1.call-update) | async-done | bytes 3145744 | tf_op jit(solution)/shard_map/psum | solution.py:85
  456.4 1.3 fusion.28
  457.7 1.8 fusion.23
  459.5 0.7 fusion.26
  (150 shorter events, 33.0 us)
Async XLA Ops:
  7.2 5.2 %copy-start = (bf16[1,1,1536,256]{3,2,1,0:T(8,128)(2,1)S(1)}, bf16[1,1,1536,256]{3,2,1,0:T(8,128)(2,1)}, u32[]{:S(2)}) copy-start(bf16[1,1,1536,256]{3,2,1,0:T(8,128)(2,1)} %param.13) | copy-start | bytes 2359300
  7.2 279.6 %all-reduce.6.cloned.1.call-start = ((), (), s32[]{:S(2)}) async-start(), calls=%async_computation | async-start | bytes 524288 | tf_op jit(solution)/shard_map/psum | solution.py:83
  11.2 2.3 copy-start.4
  11.2 2.4 copy-start.3
  11.2 2.4 copy-start.2
  12.4 444.1 %all-reduce.8.cloned.1.call-start = ((), (), s32[]{:S(2)}) async-start(), calls=%async_computation.1 | async-start | bytes 6291456 | tf_op jit(solution)/shard_map/psum | solution.py:85
  457.7 2.5 copy-start.1
Sparse Core Ops, SparseCore 0:
  13.6 273.1 all-reduce.5
  290.1 166.3 all-reduce.7
where the time goes:
time: 475 us; the launch traced here: 467 us
  blocking collectives  142 us (30%)
  waiting for transfers between devices  139 us (29%)
  other arithmetic  63.4 us (13%)
  loops' own time  41.9 us (9%)
  matrix products  41.1 us (9%)
  local copies, waits for them, and re-layouts  24.5 us (5%)
  between operations  15 us (3%)
    psum x1, waiting for transfers between devices, shards(): lax.psum((cam_hess, cam_cross, cam_grad), 'img')  117 us
    psum x1, blocking collectives, shards(): tex_hess, tex_grad = lax.psum((tex_hess, tex_grad), ('img', 'blk'))  107 us
    another operation x1, loops' own time, device_partial(): cam_hess, cam_cross, cam_grad = lax.map(one_slot, slot_range)  41.9 us
    psum x1, blocking collectives, shards(): lax.psum((cam_hess, cam_cross, cam_grad), 'img')  34.5 us
    psum x1, waiting for transfers between devices, shards(): tex_hess, tex_grad = lax.psum((tex_hess, tex_grad), ('img', 'blk'))  22.7 us
    another operation x4, other arithmetic, tri_inverse(): lax.linalg.triangular_solve(lower_factor, identity, left_side=True, lower...  21.1 us
    dot_general x16, matrix products, one_slot(): cam_cross = jnp.dot(picked.T, tex_rows, preferred_element_type=jnp.float32)  15.6 us
    dot_general x16, matrix products, one_slot(): cam_hess = jnp.dot(picked.T, cam_rows, preferred_element_type=jnp.float32)  14.7 us
  transfers between devices with their start and end apart: 2, of which 2 were waited for; matrix products, arithmetic and copies ran while one was open for 26% of the time, Pallas kernels for 0%

commit v1 on v0

v1 whole, which is shorter than its diff:
```python
import functools

import jax
import jax.numpy as jnp
from jax import lax
from jax.experimental import pallas as pl
from jax.experimental.pallas import tpu as pltpu
from jax.sharding import Mesh, PartitionSpec as P

BLOCK = 128
TEX_W = 256
ROWS = 1536
OBS = 192
PER = 8
SLOTS = 16
PIECE = 328
F32 = jnp.float32
VMEM = pl.BlockSpec(memory_space=pltpu.VMEM)
SMEM = pl.BlockSpec(memory_space=pltpu.SMEM)


def col_dot(left, right):
    return lax.dot_general(left, right, (((0,), (0,)), ((), ())), preferred_element_type=F32)


def exact_dot(left, right, dims=((1,), (0,))):
    return lax.dot_general(
        left, right, (dims, ((), ())), precision=lax.Precision.HIGHEST, preferred_element_type=F32
    )


def iota(shape, dim):
    return lax.broadcasted_iota(jnp.int32, shape, dim)


def find_starts(obs_ref, starts):
    starts[SLOTS] = OBS

    def step(i, carry):
        j = OBS - 1 - i
        starts[obs_ref[j]] = j
        return carry

    lax.fori_loop(0, OBS, step, 0, unroll=8)


def tex_kernel(tex_ref, res_ref, obs_ref, ids_ref, pattern_ref, out_ref, starts):
    find_starts(obs_ref, starts)
    obs_index = iota((OBS, BLOCK), 0)
    masks = []
    for bit in range(2):
        keep = jnp.zeros((OBS, BLOCK), jnp.int32)
        before = jnp.int32(0)
        for s in range(SLOTS):
            now = (pattern_ref[ids_ref[s]] >> bit) & 1
            keep = jnp.where(obs_index >= starts[s], now, keep)
            before = now
        keep = keep.astype(F32)
        rows = jnp.broadcast_to(keep[:, None, :], (OBS, PER, BLOCK)).reshape(ROWS, BLOCK)
        masks.append(rows.astype(jnp.bfloat16))
    masked = tex_ref[...] * jnp.concatenate(masks, axis=1)
    hess = col_dot(masked, masked)
    grad = jnp.dot(res_ref[...], masked, preferred_element_type=F32)
    h00, h10, h11 = hess[:BLOCK, :BLOCK], hess[BLOCK:, :BLOCK], hess[BLOCK:, BLOCK:]
    row, col = iota((BLOCK, BLOCK), 0), iota((BLOCK, BLOCK), 1)
    mixed = jnp.where(row >= col, h00, h11)
    diag = jnp.sum(jnp.where(row == col, h11, 0.0), axis=0, keepdims=True)
    out_ref[...] = jnp.zeros(out_ref.shape, F32)
    out_ref[:16, :8, :] = mixed.reshape(16, 8, BLOCK)
    out_ref[16:, :8, :] = h10.reshape(16, 8, BLOCK)
    out_ref[0, 8:9, :] = grad[:, :BLOCK]
    out_ref[1, 8:9, :] = grad[:, BLOCK:]
    out_ref[2, 8:9, :] = diag


def cam_kernel(cam_ref, tex_ref, res_ref, obs_ref, ids_ref, pattern_ref, place_ref, *rest):
    outs, starts = rest[:4], rest[4]
    find_starts(obs_ref, starts)
    my_yl, my_x = place_ref[0], place_ref[1]
    row64, lane64 = iota((64, BLOCK), 0), iota((64, BLOCK), 1)
    row256 = iota((256, BLOCK), 0)
    row48 = iota((48, BLOCK), 0)
    sub = iota((SLOTS, BLOCK), 0)
    first = jnp.zeros((SLOTS, BLOCK), jnp.int32)
    last = jnp.zeros((SLOTS, BLOCK), jnp.int32)
    for k in range(4):
        for j in range(4):
            out = outs[k]
            base = j * PIECE
            slot = ((my_yl + j) & 3) * 4 + ((my_x + k) & 3)
            lo, hi = starts[slot] * PER, starts[slot + 1] * PER
            code = pattern_ref[ids_ref[slot]]
            first = jnp.where(sub == k * 4 + j, lo, first)
            last = jnp.where(sub == k * 4 + j, hi, last)
            begin = jnp.minimum((lo >> 4) << 4, ROWS - 256)
            begin = pl.multiple_of(begin, 16)

            def part(begin, low, rows, count):
                cam = cam_ref[pl.ds(begin, count), :]
                tex = tex_ref[pl.ds(begin, count), :]
                where = rows + begin
                keep = ((where >= low) & (where < hi)).astype(F32).astype(jnp.bfloat16)
                picked = cam * keep
                return col_dot(picked, cam), col_dot(picked, tex)

            hess, cross = part(begin, lo, row256, 256)
            keep0, keep1 = (code & 1) == 1, (code >> 1) == 1
            zero = jnp.zeros((BLOCK, BLOCK), F32)

            def packed(hess):
                low, high = hess[64:, :], hess[:64, :]
                turned = pltpu.roll(high, 64, 1)
                pair = jnp.where((lane64 >= 64) & (row64 >= lane64 - 64), turned, low)
                diag = jnp.sum(jnp.where(row64 == lane64 - 64, low, 0.0), axis=0, keepdims=True)
                return pair, diag

            pair, diag = packed(hess)
            out[base : base + 128, :] = jnp.where(keep0, cross[:, :BLOCK], zero)
            out[base + 128 : base + 256, :] = jnp.where(keep1, cross[:, BLOCK:], zero)
            out[base + 256 : base + 320, :] = pair
            out[base + 320 : base + 328, :] = jnp.broadcast_to(diag, (8, BLOCK))

            @pl.when(hi > begin + 256)
            def _():
                second = jnp.minimum(begin + 256, ROWS - 48)
                second = pl.multiple_of(second, 16)
                hess, cross = part(second, begin + 256, row48, 48)
                pair, diag = packed(hess)
                out[base : base + 128, :] += jnp.where(keep0, cross[:, :BLOCK], zero)
                out[base + 128 : base + 256, :] += jnp.where(keep1, cross[:, BLOCK:], zero)
                out[base + 256 : base + 320, :] += pair
                out[base + 320 : base + 328, :] += jnp.broadcast_to(diag, (8, BLOCK))

    lane = iota((SLOTS, ROWS), 1)
    first = jnp.tile(first, (1, ROWS // BLOCK))
    last = jnp.tile(last, (1, ROWS // BLOCK))
    res = jnp.broadcast_to(res_ref[...].astype(F32), (SLOTS, ROWS))
    spread = jnp.where((lane >= first) & (lane < last), res, 0.0).astype(jnp.bfloat16)
    grad = jnp.dot(spread, cam_ref[...], preferred_element_type=F32)
    for k in range(4):
        for j in range(4):
            base = j * PIECE
            outs[k][base + 320 : base + 321, :] = grad[k * 4 + j : k * 4 + j + 1, :]


def add_kernel(a_ref, b_ref, c_ref, d_ref, *outs):
    for j in range(4):
        rows = slice(j * PIECE, (j + 1) * PIECE)
        outs[j][...] = (a_ref[rows, :] + b_ref[rows, :]) + (c_ref[rows, :] + d_ref[rows, :])


def factor(a):
    row, col = iota((BLOCK, BLOCK), 0), iota((BLOCK, BLOCK), 1)
    eye = (row == col).astype(F32)

    def step(j, carry):
        a, b, low = carry
        pick = col == j
        column = jnp.sum(jnp.where(pick, a, 0.0), axis=1, keepdims=True)
        here = row[:, :1] == j
        pivot = jnp.sum(jnp.where(here, column, 0.0), axis=0, keepdims=True)
        scale = lax.rsqrt(pivot)
        arow = jnp.sum(jnp.where(row == j, a, 0.0), axis=0, keepdims=True) * scale
        brow = jnp.sum(jnp.where(row == j, b, 0.0), axis=0, keepdims=True) * scale
        column = jnp.where(row[:, :1] >= j, column, 0.0) * scale
        low = jnp.where(pick, column, low)
        under = jnp.where(here, 0.0, column)
        a = a - under * arow
        b = jnp.where(row == j, brow, b - under * brow)
        return a, b, low

    a, b, low = lax.fori_loop(0, BLOCK, step, (a, eye, jnp.zeros((BLOCK, BLOCK), F32)))
    return low, b


def panel_kernel(sums_ref, damping_ref, factor_ref, inv_ref, sol_ref):
    damping = damping_ref[0]
    sums = sums_ref[...]
    both = sums[:, :8, :].reshape(TEX_W, BLOCK)
    mixed, h10 = both[:BLOCK], both[BLOCK:]
    g0, g1, diag = sums[0, 8:9, :], sums[1, 8:9, :], sums[2, 8:9, :]
    row, col = iota((BLOCK, BLOCK), 0), iota((BLOCK, BLOCK), 1)
    flipped = mixed.T
    h00 = jnp.where(row >= col, mixed, flipped)
    h11 = jnp.where(row < col, mixed, jnp.where(row == col, diag, flipped))
    h00 = jnp.where(row == col, h00 + damping * h00, h00)
    h11 = jnp.where(row == col, h11 + damping * h11, h11)
    l00, w00 = factor(h00)
    l10 = exact_dot(h10, w00, ((1,), (1,)))
    y0 = exact_dot(g0, w00, ((1,), (1,)))
    l11, w11 = factor(h11 - exact_dot(l10, l10, ((1,), (1,))))
    w10 = -exact_dot(w11, exact_dot(l10, w00))
    y1 = exact_dot(g1 - exact_dot(y0, l10, ((1,), (1,))), w11, ((1,), (1,)))
    zero = jnp.zeros((BLOCK, BLOCK), F32)
    factor_ref[:BLOCK, :BLOCK] = l00
    factor_ref[:BLOCK, BLOCK:] = zero
    factor_ref[BLOCK:, :BLOCK] = l10
    factor_ref[BLOCK:, BLOCK:] = l11
    inv_ref[:BLOCK, :BLOCK] = w00
    inv_ref[:BLOCK, BLOCK:] = zero
    inv_ref[BLOCK:, :BLOCK] = w10
    inv_ref[BLOCK:, BLOCK:] = w11
    sol_ref[:, :BLOCK] = y0
    sol_ref[:, BLOCK:] = y1


def last_kernel(a_ref, b_ref, c_ref, d_ref, inv_ref, sol_ref, damping_ref, red_ref, grad_ref, coup_ref):
    damping = damping_ref[0]
    total = (a_ref[...] + b_ref[...]) + (c_ref[...] + d_ref[...])
    cross = jnp.concatenate([total[:128], total[128:256]], axis=1)
    pair, grad, diag = total[256:320], total[320:321], total[321:322]
    row, col = iota((BLOCK, BLOCK), 0), iota((BLOCK, BLOCK), 1)
    row64, lane64 = iota((64, BLOCK), 0), iota((64, BLOCK), 1)
    turned = pltpu.roll(pair, 64, 1)
    top = jnp.where(lane64 < 64, turned, 0.0)
    square = jnp.concatenate([top, pair], axis=0)
    other = square.T
    lower = jnp.where((row >= 64) & (col >= 64), other, square)
    lower = jnp.where(row > col, lower, 0.0)
    main = jnp.where(row == col, jnp.where(row < 64, square, diag), 0.0)
    hess = lower + lower.T + main + damping * main
    coupling = exact_dot(cross, inv_ref[...], ((1,), (1,)))
    coup_ref[...] = coupling
    red_ref[...] = hess - exact_dot(coupling, coupling, ((1,), (1,)))
    grad_ref[...] = grad - exact_dot(sol_ref[...], coupling, ((1,), (1,)))


def call(kernel, name, outs, specs, scratch=()):
    return pl.pallas_call(
        kernel,
        out_shape=[jax.ShapeDtypeStruct(s, F32) for s in outs],
        in_specs=specs,
        out_specs=[VMEM] * len(outs),
        scratch_shapes=scratch,
        name=name,
        compiler_params=pltpu.CompilerParams(vmem_limit_bytes=24 * 2**20),
    )


def spread_sum(value, axes):
    count = lax.axis_size(axes)
    copies = jnp.broadcast_to(value[None], (count, *value.shape))
    return jnp.sum(lax.all_to_all(copies, axes, 0, 0), axis=0)


def shift(value, axis, by):
    n = lax.axis_size(axis)
    return lax.ppermute(value, axis, [(i, (i + by) % n) for i in range(n)])


FAR = ("x", "z")
NEAR = ("yl", "yh", "c")


def shards(jac_cam, jac_tex, residual, obs_slot, col_ids, block_pattern, damping):
    cam, tex = jac_cam[0, 0], jac_tex[0, 0]
    res, obs = residual[0], obs_slot[0, 0]
    damping = damping.reshape(1)
    starts = [pltpu.SMEM((SLOTS + 1,), jnp.int32)]
    place = jnp.stack([lax.axis_index("yl"), lax.axis_index("x")]).astype(jnp.int32)

    (tex_part,) = call(
        tex_kernel, "tex", [(32, 16, BLOCK)], [VMEM, VMEM, SMEM, SMEM, SMEM], starts
    )(tex, res, obs, col_ids, block_pattern)
    share = jnp.sum(lax.all_to_all(tex_part, FAR, 0, 0), axis=0)
    share = spread_sum(share, NEAR)
    copies = jnp.broadcast_to(share[None], (32, *share.shape))
    tex_sums = lax.all_to_all(copies, FAR, 0, 0)

    pieces = call(
        cam_kernel,
        "cam",
        [(4 * PIECE, BLOCK)] * 4,
        [VMEM, VMEM, VMEM, SMEM, SMEM, SMEM, SMEM],
        starts,
    )(cam, tex, res, obs, col_ids, block_pattern, place)
    moved = [pieces[0]] + [shift(pieces[k], "x", k) for k in (1, 2, 3)]
    pieces = call(add_kernel, "add", [(PIECE, BLOCK)] * 4, [VMEM] * 4)(*moved)
    moved = [pieces[0]] + [shift(pieces[j], "yl", j) for j in (1, 2, 3)]

    texture_factor, inverse, sol = call(
        panel_kernel, "panel", [(TEX_W, TEX_W), (TEX_W, TEX_W), (1, TEX_W)], [VMEM, SMEM]
    )(tex_sums, damping)
    reduced, gradient, coupling = call(
        last_kernel,
        "last",
        [(BLOCK, BLOCK), (1, BLOCK), (BLOCK, TEX_W)],
        [VMEM] * 6 + [SMEM],
    )(*moved, inverse, sol, damping)
    return (reduced[None, None], gradient[None], coupling[None, None], texture_factor)


def solution(mesh):
    fine = Mesh(mesh.devices.reshape(4, 4, 2, 8, 2), ("yl", "x", "yh", "z", "c"))
    img, blk = ("yl", "x"), ("yh", "z", "c")
    return jax.shard_map(
        shards,
        mesh=fine,
        in_specs=(
            P(img, blk, None, None),
            P(img, blk, None, None),
            P(img, blk, None),
            P(img, blk, None),
            P(blk),
            P(),
            P(),
        ),
        out_specs=(
            P(blk, img, None, None),
            P(blk, img, None),
            P(blk, img, None, None),
            P(),
        ),
        check_vma=False,
    )
```

time: 475 us -> 116 us (0.24)
  the two profiles are of different devices: /device:TPU:1 before, /device:TPU:114 now
where the time goes in v1:
time: 116 us
  Pallas kernels  48.5 us (42%)
  starting transfers between devices  43.1 us (37%)
  blocking collectives  13.1 us (11%)
  waiting for transfers between devices  4.54 us (4%)
  local copies, waits for them, and re-layouts  3.84 us (3%)
  between operations  1.43 us (1%)
    pallas_call x1, Pallas kernels, shards(): call(panel_kernel, 'panel', [(TEX_W, TEX_W), (TEX_W, TEX_W), (1, TEX_W)],...  36.4 us
    ppermute x6, starting transfers between devices, shift(): return lax.ppermute(value, axis, [(i, (i + by) % n) for i in range(n)])  21.9 us
    all_to_all x1, blocking collectives, spread_sum(): return jnp.sum(lax.all_to_all(copies, axes, 0, 0), axis=0)  13.1 us
    all_to_all x1, starting transfers between devices, shards(): share = jnp.sum(lax.all_to_all(tex_part, FAR, 0, 0), axis=0)  12.7 us
    all_to_all x1, starting transfers between devices, shards(): tex_sums = lax.all_to_all(copies, FAR, 0, 0)  8.48 us
    pallas_call x1, Pallas kernels, shards(): call(cam_kernel, 'cam', [(4 * PIECE, BLOCK)] * 4, [VMEM, VMEM, VMEM, SMEM...  7.18 us
    ppermute x6, waiting for transfers between devices, shift(): return lax.ppermute(value, axis, [(i, (i + by) % n) for i in range(n)])  4.53 us
    unnamed x16, local copies, waits for them, and re-layouts  3.11 us
  transfers between devices with their start and end apart: 8, of which 1 were waited for; matrix products, arithmetic and copies ran while one was open for 2% of the time, Pallas kernels for 38%

profile of v1, /device:TPU:114, one launch (start us, length us, event | category | flops | bytes accessed | tf_op | source)
XLA Modules:
  0.0 115.6 jit_solution(16700624377143641319)
XLA Ops:
  0.6 0.0 copy-start.5
  0.6 0.0 copy-start.6
  0.7 0.0 copy-start.7
  0.7 0.7 copy-done.5
  1.3 0.0 copy-done.6
  1.3 0.0 copy-done.7
  1.3 0.0 copy-start
  1.3 1.1 copy-done
  2.5 0.0 copy-start.3
  2.5 0.7 copy-done.3
  3.2 0.0 copy-start.1
  3.2 2.3 %tex.1 = f32[32,16,128]{2,1,0:T(8,128)} custom-call(bf16[1536,256]{1,0:T(8,128)(2,1)S(1)} %bitcast.12, bf16[1,1536]{1,0:T(2,128)(2,1)S(1)} %bitcast.15, s32[192]{0:T(256)S(1)} %bitcast.17, s32[16]{0:T(128)S(1)} %copy-done.7, s32[512]{0:T(512)S(1)} %copy-done.5), custom_call_target="tpu_custom_call" | custom-call | tf_op jit(solution)/shard_map/tex/pallas_call | solution.py:262
  5.5 0.0 copy-start.2
  5.5 12.7 %all-to-all-start = ((f32[32,16,128]{2,1,0:T(8,128)}), f32[32,16,128]{2,1,0:T(8,128)}, u32[]{:S(2)}, u32[]{:S(2)}) async-start(f32[32,16,128]{2,1,0:T(8,128)} %tex.1), calls=%async_computation | async-start | bytes 524288 | tf_op jit(solution)/shard_map/all_to_all | solution.py:265
  18.2 0.0 copy-start.4
  18.2 0.1 pad_add_fusion.place_ref
  18.3 0.0 copy-done.1
  18.3 0.0 copy-done.2
  18.3 0.6 copy-done.4
  18.9 7.2 %cam.1 = (f32[1312,128]{1,0:T(8,128)S(1)}, f32[1312,128]{1,0:T(8,128)}, f32[1312,128]{1,0:T(8,128)}, f32[1312,128]{1,0:T(8,128)}) custom-call(bf16[1536,128]{1,0:T(8,128)(2,1)S(1)} %bitcast.14, bf16[1536,256]{1,0:T(8,128)(2,1)S(1)} %bitcast.13, bf16[1,1536]{1,0:T(2,128)(2,1)S(1)} %bitcast.16, s32[192]{0:T(256)S(1)} %bitcast.18, s32[16]{0:T(128)S(1)} %copy-done.7, ...), custom_call_target="tpu_custom_call" | custom-call | tf_op jit(solution)/shard_map/cam/pallas_call | solution.py:270
  26.1 3.4 %collective-permute-start = (f32[1312,128]{1,0:T(8,128)}, f32[1312,128]{1,0:T(8,128)S(1)}, u32[]{:S(2)}, u32[]{:S(2)}) collective-permute-start(f32[1312,128]{1,0:T(8,128)} %get-tuple-element.19), channel_id=1, source_target_pairs={{0,32},{32,64},{64,96},{96,0},{1,33},{33,65},{65,97},{97,1},{2,34}... | collective-permute-start | bytes 2015240 | tf_op jit(solution)/shard_map/ppermute | solution.py:248
  29.5 3.1 %collective-permute-start.1 = (f32[1312,128]{1,0:T(8,128)}, f32[1312,128]{1,0:T(8,128)S(1)}, u32[]{:S(2)}, u32[]{:S(2)}) collective-permute-start(f32[1312,128]{1,0:T(8,128)} %get-tuple-element.20), channel_id=1, source_target_pairs={{0,64},{32,96},{64,0},{96,32},{1,65},{33,97},{65,1},{97,33},{2,66}... | collective-permute-start | bytes 2015240 | tf_op jit(solution)/shard_map/ppermute | solution.py:248
  32.5 4.0 %collective-permute-start.2 = (f32[1312,128]{1,0:T(8,128)}, f32[1312,128]{1,0:T(8,128)S(1)}, u32[]{:S(2)}, u32[]{:S(2)}) collective-permute-start(f32[1312,128]{1,0:T(8,128)} %get-tuple-element.21), channel_id=1, source_target_pairs={{0,96},{32,0},{64,32},{96,64},{1,97},{33,1},{65,33},{97,65},{2,98}... | collective-permute-start | bytes 2015240 | tf_op jit(solution)/shard_map/ppermute | solution.py:248
  36.6 0.0 all-to-all-done
  36.6 1.0 reduce_sum.18
  37.6 13.1 %all_to_all.15 = f32[16,16,128]{2,1,0:T(8,128)S(1)} all-to-all(f32[16,16,128]{2,1,0:T(8,128)S(1)} %broadcast_in_dim.10), channel_id=1, replica_groups=mesh['yl'=4,'x'=4,'yh'=2,'z'=8,'c'=2] {'yl','yh','c'}, dimensions={0} | all-to-all | bytes 262144 | tf_op jit(solution)/shard_map/all_to_all | solution.py:243
  50.8 0.7 broadcast_in_dim.22
  51.5 8.5 %all-to-all-start.2 = ((f32[32,16,128]{2,1,0:T(8,128)}), f32[32,16,128]{2,1,0:T(8,128)S(1)}, u32[]{:S(2)}, u32[]{:S(2)}) async-start(f32[32,16,128]{2,1,0:T(8,128)} %broadcast_in_dim.22), calls=%async_computation.2 | async-start | bytes 524288 | tf_op jit(solution)/shard_map/all_to_all | solution.py:268
  60.0 0.0 collective-permute-done.b_ref
  60.0 0.0 collective-permute-done.1.c_ref
  60.0 4.5 %collective-permute-done.2.d_ref = f32[1312,128]{1,0:T(8,128)S(1)} collective-permute-done((f32[1312,128]{1,0:T(8,128)}, f32[1312,128]{1,0:T(8,128)S(1)}, u32[]{:S(2)}, u32[]{:S(2)}) %collective-permute-start.2) | collective-permute-done | bytes 671776 | tf_op jit(solution)/shard_map/ppermute | solution.py:248
  64.5 0.9 add.3
  65.4 2.0 %collective-permute-start.3 = (f32[328,128]{1,0:T(8,128)}, f32[328,128]{1,0:T(8,128)S(1)}, u32[]{:S(2)}, u32[]{:S(2)}) collective-permute-start(f32[328,128]{1,0:T(8,128)} %get-tuple-element.23), channel_id=1, source_target_pairs={{0,128},{128,256},{256,384},{384,0},{1,129},{129,257},{257,385},{3... | collective-permute-start | bytes 503816 | tf_op jit(solution)/shard_map/ppermute | solution.py:248
  67.4 4.9 %collective-permute-start.4 = (f32[328,128]{1,0:T(8,128)}, f32[328,128]{1,0:T(8,128)S(1)}, u32[]{:S(2)}, u32[]{:S(2)}) collective-permute-start(f32[328,128]{1,0:T(8,128)} %get-tuple-element.24), channel_id=1, source_target_pairs={{0,256},{128,384},{256,0},{384,128},{1,257},{129,385},{257,1},{385... | collective-permute-start | bytes 503816 | tf_op jit(solution)/shard_map/ppermute | solution.py:248
  72.3 4.5 %collective-permute-start.5 = (f32[328,128]{1,0:T(8,128)}, f32[328,128]{1,0:T(8,128)S(1)}, u32[]{:S(2)}, u32[]{:S(2)}) collective-permute-start(f32[328,128]{1,0:T(8,128)} %get-tuple-element.25), channel_id=1, source_target_pairs={{0,384},{128,0},{256,128},{384,256},{1,385},{129,1},{257,129},{385... | collective-permute-start | bytes 503816 | tf_op jit(solution)/shard_map/ppermute | solution.py:248
  77.5 0.0 all-to-all-done.2.sums_ref
  77.5 36.4 %panel.1 = (f32[256,256]{1,0:T(8,128)}, f32[256,256]{1,0:T(8,128)S(1)}, f32[1,256]{1,0:T(1,128)S(1)}) custom-call(f32[32,16,128]{2,1,0:T(8,128)S(1)} %all-to-all-done.2.sums_ref, f32[1]{0:T(128)} %bitcast.10.damping_ref), custom_call_target="tpu_custom_call" | custom-call | tf_op jit(solution)/shard_map/panel/pallas_call | solution.py:281
  113.8 0.0 collective-permute-done.3.b_ref
  113.8 0.0 collective-permute-done.4.c_ref
  113.8 0.0 collective-permute-done.5.d_ref
  113.8 1.7 %last.1 = (f32[128,128]{1,0:T(8,128)}, f32[1,128]{1,0:T(1,128)}, f32[128,256]{1,0:T(8,128)}) custom-call(f32[328,128]{1,0:T(8,128)S(1)} %get-tuple-element.22.a_ref, f32[328,128]{1,0:T(8,128)S(1)} %collective-permute-done.3.b_ref, f32[328,128]{1,0:T(8,128)S(1)} %collective-permute-done.4.c_ref, f32[328,128]{1,0:T(8,128)S(1)} %collective-permute-done.5.d_ref, ...), custom_call_target="tpu_custom_call" | custom-call | tf_op jit(solution)/shard_map/last/pallas_call | solution.py:284
  (2 shorter events, 0.0 us)
Async XLA Ops:
  0.6 0.7 copy-start.5
  0.6 0.7 copy-start.6
  0.7 0.7 copy-start.7
  1.3 1.1 copy-start
  2.5 0.7 copy-start.3
  3.2 15.2 %copy-start.1 = (bf16[1,1,1536,256]{3,2,1,0:T(8,128)(2,1)S(1)}, bf16[1,1,1536,256]{3,2,1,0:T(8,128)(2,1)}, u32[]{:S(2)}) copy-start(bf16[1,1,1536,256]{3,2,1,0:T(8,128)(2,1)} %param.8) | copy-start | bytes 2359300
  5.5 12.9 %copy-start.2 = (bf16[1,1,1536,128]{3,2,1,0:T(8,128)(2,1)S(1)}, bf16[1,1,1536,128]{3,2,1,0:T(8,128)(2,1)}, u32[]{:S(2)}) copy-start(bf16[1,1,1536,128]{3,2,1,0:T(8,128)(2,1)} %param.7) | copy-start | bytes 1179652
  5.5 31.1 %all-to-all-start = ((f32[32,16,128]{2,1,0:T(8,128)}), f32[32,16,128]{2,1,0:T(8,128)}, u32[]{:S(2)}, u32[]{:S(2)}) async-start(f32[32,16,128]{2,1,0:T(8,128)} %tex.1), calls=%async_computation | async-start | bytes 524288 | tf_op jit(solution)/shard_map/all_to_all | solution.py:265
  18.2 0.7 copy-start.4
  26.1 33.9 %collective-permute-start = (f32[1312,128]{1,0:T(8,128)}, f32[1312,128]{1,0:T(8,128)S(1)}, u32[]{:S(2)}, u32[]{:S(2)}) collective-permute-start(f32[1312,128]{1,0:T(8,128)} %get-tuple-element.19), channel_id=1, source_target_pairs={{0,32},{32,64},{64,96},{96,0},{1,33},{33,65},{65,97},{97,1},{2,34}... | collective-permute-start | bytes 2015240 | tf_op jit(solution)/shard_map/ppermute | solution.py:248
  29.5 30.5 %collective-permute-start.1 = (f32[1312,128]{1,0:T(8,128)}, f32[1312,128]{1,0:T(8,128)S(1)}, u32[]{:S(2)}, u32[]{:S(2)}) collective-permute-start(f32[1312,128]{1,0:T(8,128)} %get-tuple-element.20), channel_id=1, source_target_pairs={{0,64},{32,96},{64,0},{96,32},{1,65},{33,97},{65,1},{97,33},{2,66}... | collective-permute-start | bytes 2015240 | tf_op jit(solution)/shard_map/ppermute | solution.py:248
  32.5 32.0 %collective-permute-start.2 = (f32[1312,128]{1,0:T(8,128)}, f32[1312,128]{1,0:T(8,128)S(1)}, u32[]{:S(2)}, u32[]{:S(2)}) collective-permute-start(f32[1312,128]{1,0:T(8,128)} %get-tuple-element.21), channel_id=1, source_target_pairs={{0,96},{32,0},{64,32},{96,64},{1,97},{33,1},{65,33},{97,65},{2,98}... | collective-permute-start | bytes 2015240 | tf_op jit(solution)/shard_map/ppermute | solution.py:248
  51.5 26.0 %all-to-all-start.2 = ((f32[32,16,128]{2,1,0:T(8,128)}), f32[32,16,128]{2,1,0:T(8,128)S(1)}, u32[]{:S(2)}, u32[]{:S(2)}) async-start(f32[32,16,128]{2,1,0:T(8,128)} %broadcast_in_dim.22), calls=%async_computation.2 | async-start | bytes 524288 | tf_op jit(solution)/shard_map/all_to_all | solution.py:268
  65.4 48.5 %collective-permute-start.3 = (f32[328,128]{1,0:T(8,128)}, f32[328,128]{1,0:T(8,128)S(1)}, u32[]{:S(2)}, u32[]{:S(2)}) collective-permute-start(f32[328,128]{1,0:T(8,128)} %get-tuple-element.23), channel_id=1, source_target_pairs={{0,128},{128,256},{256,384},{384,0},{1,129},{129,257},{257,385},{3... | collective-permute-start | bytes 503816 | tf_op jit(solution)/shard_map/ppermute | solution.py:248
  67.4 46.5 %collective-permute-start.4 = (f32[328,128]{1,0:T(8,128)}, f32[328,128]{1,0:T(8,128)S(1)}, u32[]{:S(2)}, u32[]{:S(2)}) collective-permute-start(f32[328,128]{1,0:T(8,128)} %get-tuple-element.24), channel_id=1, source_target_pairs={{0,256},{128,384},{256,0},{384,128},{1,257},{129,385},{257,1},{385... | collective-permute-start | bytes 503816 | tf_op jit(solution)/shard_map/ppermute | solution.py:248
  72.3 41.5 %collective-permute-start.5 = (f32[328,128]{1,0:T(8,128)}, f32[328,128]{1,0:T(8,128)S(1)}, u32[]{:S(2)}, u32[]{:S(2)}) collective-permute-start(f32[328,128]{1,0:T(8,128)} %get-tuple-element.25), channel_id=1, source_target_pairs={{0,384},{128,0},{256,128},{384,256},{1,385},{129,1},{257,129},{385... | collective-permute-start | bytes 503816 | tf_op jit(solution)/shard_map/ppermute | solution.py:248

commit v2 on v1

v2 whole, which is shorter than its diff:
```python
import functools

import jax
import jax.numpy as jnp
from jax import lax
from jax.experimental import pallas as pl
from jax.experimental.pallas import tpu as pltpu
from jax.sharding import Mesh, PartitionSpec as P

BLOCK = 128
TEX_W = 256
ROWS = 1536
OBS = 192
PER = 8
SLOTS = 16
PIECE = 328
F32 = jnp.float32
VMEM = pl.BlockSpec(memory_space=pltpu.VMEM)
HBM = pl.BlockSpec(memory_space=pltpu.HBM)
SMEM = pl.BlockSpec(memory_space=pltpu.SMEM)


def col_dot(left, right):
    return lax.dot_general(left, right, (((0,), (0,)), ((), ())), preferred_element_type=F32)


def exact_dot(left, right, dims=((1,), (0,))):
    return lax.dot_general(
        left, right, (dims, ((), ())), precision=lax.Precision.HIGHEST, preferred_element_type=F32
    )


def iota(shape, dim):
    return lax.broadcasted_iota(jnp.int32, shape, dim)


def find_starts(obs_ref, starts):
    starts[SLOTS] = OBS

    def step(i, carry):
        j = OBS - 1 - i
        starts[obs_ref[j]] = j
        return carry

    lax.fori_loop(0, OBS, step, 0, unroll=8)


def tex_sums(tex_ref, res_ref, ids_ref, pattern_ref, starts, out_ref):
    obs_index = iota((OBS, BLOCK), 0)
    masks = []
    for bit in range(2):
        keep = jnp.zeros((OBS, BLOCK), jnp.int32)
        for s in range(SLOTS):
            keep = jnp.where(obs_index >= starts[s], (pattern_ref[ids_ref[s]] >> bit) & 1, keep)
        rows = jnp.broadcast_to(keep.astype(F32)[:, None, :], (OBS, PER, BLOCK))
        masks.append(rows.reshape(ROWS, BLOCK).astype(jnp.bfloat16))
    masked = tex_ref[...] * jnp.concatenate(masks, axis=1)
    hess = col_dot(masked, masked)
    grad = jnp.dot(res_ref[...], masked, preferred_element_type=F32)
    h00, h10, h11 = hess[:BLOCK, :BLOCK], hess[BLOCK:, :BLOCK], hess[BLOCK:, BLOCK:]
    row, col = iota((BLOCK, BLOCK), 0), iota((BLOCK, BLOCK), 1)
    mixed = jnp.where(row >= col, h00, h11)
    diag = jnp.sum(jnp.where(row == col, h11, 0.0), axis=0, keepdims=True)
    out_ref[:, 8:, :] = jnp.zeros((32, 8, BLOCK), F32)
    out_ref[:16, :8, :] = mixed.reshape(16, 8, BLOCK)
    out_ref[16:, :8, :] = h10.reshape(16, 8, BLOCK)
    out_ref[0, 8:9, :] = grad[:, :BLOCK]
    out_ref[1, 8:9, :] = grad[:, BLOCK:]
    out_ref[2, 8:9, :] = diag


def packed(hess):
    row, lane = iota((64, BLOCK), 0), iota((64, BLOCK), 1)
    low, high = hess[64:, :], hess[:64, :]
    turned = pltpu.roll(high, 64, 1)
    pair = jnp.where((lane >= 64) & (row >= lane - 64), turned, low)
    return pair, jnp.sum(jnp.where(row == lane - 64, low, 0.0), axis=0, keepdims=True)


def local_kernel(
    cam_any, tex_any, res_any, obs_any, ids_any, pattern_any, out, tex_out,
    starts, cam_ref, tex_ref, res_ref, obs_ref, ids_ref, pattern_ref, sems, small,
):
    near = [
        pltpu.make_async_copy(src, dst, small.at[i])
        for i, (src, dst) in enumerate(
            ((obs_any, obs_ref), (ids_any, ids_ref), (pattern_any, pattern_ref), (res_any, res_ref))
        )
    ]
    for copy in near:
        copy.start()
    copies = []
    for i, (src, dst) in enumerate(((cam_any, cam_ref), (tex_any, tex_ref))):
        for n in range(4):
            rows = pl.ds(n * (ROWS // 4), ROWS // 4)
            copies.append(pltpu.make_async_copy(src.at[rows, :], dst.at[rows, :], sems.at[i * 4 + n]))
    for copy in copies:
        copy.start()
    for copy in near:
        copy.wait()
    find_starts(obs_ref, starts)
    sub = iota((SLOTS, BLOCK), 0)
    first = jnp.zeros((SLOTS, BLOCK), jnp.int32)
    last = jnp.zeros((SLOTS, BLOCK), jnp.int32)
    for copy in copies:
        copy.wait()
    tex_sums(tex_ref, res_ref, ids_ref, pattern_ref, starts, tex_out)

    def bounds(k, j):
        slot = j * 4 + k
        lo, hi = starts[slot] * PER, starts[slot + 1] * PER
        begin = pl.multiple_of(jnp.minimum((lo >> 4) << 4, ROWS - 256), 16)
        code = pattern_ref[ids_ref[slot]]
        return lo, hi, begin, (code & 1) == 1, (code >> 1) == 1

    def part(begin, lo, hi, count):
        cam = cam_ref[pl.ds(begin, count), :]
        both = jnp.concatenate([cam, tex_ref[pl.ds(begin, count), :]], axis=1)
        where = iota((count, BLOCK), 0) + begin
        keep = ((where >= lo) & (where < hi)).astype(F32).astype(jnp.bfloat16)
        return col_dot(cam * keep, both)

    zero = jnp.zeros((BLOCK, BLOCK), F32)
    for k in range(4):
        for j in range(4):
            base = (k * 4 + j) * PIECE
            lo, hi, begin, keep0, keep1 = bounds(k, j)
            first = jnp.where(sub == k * 4 + j, lo, first)
            last = jnp.where(sub == k * 4 + j, hi, last)
            sums = part(begin, lo, hi, 256)
            pair, diag = packed(sums[:, :BLOCK])
            out[base : base + 128, :] = jnp.where(keep0, sums[:, BLOCK : 2 * BLOCK], zero)
            out[base + 128 : base + 256, :] = jnp.where(keep1, sums[:, 2 * BLOCK :], zero)
            out[base + 256 : base + 320, :] = pair
            out[base + 320 : base + 328, :] = jnp.broadcast_to(diag, (8, BLOCK))

    lane = iota((SLOTS, ROWS), 1)
    first = jnp.tile(first, (1, ROWS // BLOCK))
    last = jnp.tile(last, (1, ROWS // BLOCK))
    res = jnp.broadcast_to(res_ref[...].astype(F32), (SLOTS, ROWS))
    spread = jnp.where((lane >= first) & (lane < last), res, 0.0).astype(jnp.bfloat16)
    grad = jnp.dot(spread, cam_ref[...], preferred_element_type=F32)
    for i in range(SLOTS):
        out[i * PIECE + 320 : i * PIECE + 321, :] = grad[i : i + 1, :]

    for k in range(4):
        for j in range(4):
            base = (k * 4 + j) * PIECE
            lo, hi, begin, keep0, keep1 = bounds(k, j)

            @pl.when(hi > begin + 256)
            def _():
                second = pl.multiple_of(jnp.minimum(begin + 256, ROWS - 48), 16)
                sums = part(second, begin + 256, hi, 48)
                pair, diag = packed(sums[:, :BLOCK])
                out[base : base + 128, :] += jnp.where(keep0, sums[:, BLOCK : 2 * BLOCK], zero)
                out[base + 128 : base + 256, :] += jnp.where(keep1, sums[:, 2 * BLOCK :], zero)
                out[base + 256 : base + 320, :] += pair
                out[base + 321 : base + 322, :] += diag


def split3(value):
    high = value.astype(jnp.bfloat16)
    return high, (value - high.astype(F32)).astype(jnp.bfloat16)


def near_dot(left, right, dims=((1,), (0,))):
    (lk,), (rk,) = dims
    lh, ll = split3(left)
    rh, rl = split3(right)
    return lax.dot_general(
        jnp.concatenate([lh, lh, ll], axis=lk),
        jnp.concatenate([rh, rl, rh], axis=rk),
        (dims, ((), ())),
        preferred_element_type=F32,
    )


def lanes(value, k):
    return jnp.broadcast_to(value[:, k : k + 1], (8, BLOCK))


def subs(value, j):
    return jnp.broadcast_to(value[j : j + 1, :], (8, BLOCK))


def factor(ab, upper, block):
    row, col = iota((BLOCK, BLOCK), 0), iota((BLOCK, BLOCK), 1)
    sub = iota((8, BLOCK), 0)
    ab[:, :BLOCK] = block
    ab[:, BLOCK:] = (row == col).astype(F32)
    cur = [block[:8], ab[:8, BLOCK:]]
    for b in range(16):
        more = b < 15
        heads = [lanes(cur[0], 8 * b + k) for k in range(8)]
        if more:
            rows = slice(8 * (b + 1), 8 * (b + 2))
            below = [ab[rows, :BLOCK], ab[rows, BLOCK:]]
            tails = [lanes(below[0], 8 * b + k) for k in range(8)]
        for j in range(8):
            scale = lax.rsqrt(subs(heads[j], j))
            head = jnp.where(sub > j, heads[j] * scale, 0.0)
            for k in range(j + 1, 8):
                pick = subs(heads[k], j) * scale
                heads[k] = heads[k] - head * pick
                if more:
                    if k == j + 1:
                        tail = tails[j] * scale
                    tails[k] = tails[k] - tail * pick
            if more and j == 7:
                tail = tails[j] * scale
            for part in range(2):
                pivot = subs(cur[part], j) * scale
                cur[part] = jnp.where(sub == j, pivot, cur[part] - head * pivot)
                if more:
                    below[part] = below[part] - tail * pivot
        done = jnp.concatenate(cur, axis=1)
        upper[8 * b : 8 * b + 8, :] = done
        if b < 14:
            high, low = split3(done)
            update = col_dot(
                jnp.concatenate([high[:, :BLOCK], high[:, :BLOCK], low[:, :BLOCK]], axis=0),
                jnp.concatenate([high, low, high], axis=0),
            )
            ab[8 * (b + 2) :, :] -= update[8 * (b + 2) :, :]
        if more:
            cur = below
    return jnp.where(row >= col, upper[:, :BLOCK].T, 0.0), upper[:, BLOCK:]


def panel_kernel(sums_ref, damping_ref, factor_ref, inv_ref, sol_ref, ab, upper):
    damping = damping_ref[0]
    sums = sums_ref[...]
    both = sums[:, :8, :].reshape(TEX_W, BLOCK)
    mixed, h10 = both[:BLOCK], both[BLOCK:]
    g0, g1, diag = sums[0, 8:9, :], sums[1, 8:9, :], sums[2, 8:9, :]
    row, col = iota((BLOCK, BLOCK), 0), iota((BLOCK, BLOCK), 1)
    flipped = mixed.T
    h00 = jnp.where(row >= col, mixed, flipped)
    h11 = jnp.where(row < col, mixed, jnp.where(row == col, diag, flipped))
    h00 = jnp.where(row == col, h00 + damping * h00, h00)
    h11 = jnp.where(row == col, h11 + damping * h11, h11)
    across = ((1,), (1,))
    l00, w00 = factor(ab, upper, h00)
    l10 = near_dot(h10, w00, across)
    y0 = near_dot(g0, w00, across)
    zero = jnp.zeros((BLOCK, BLOCK), F32)
    factor_ref[:BLOCK, :BLOCK] = l00
    factor_ref[:BLOCK, BLOCK:] = zero
    factor_ref[BLOCK:, :BLOCK] = l10
    inv_ref[:BLOCK, :BLOCK] = w00
    inv_ref[:BLOCK, BLOCK:] = zero
    lw = near_dot(l10, w00)
    l11, w11 = factor(ab, upper, h11 - near_dot(l10, l10, across))
    factor_ref[BLOCK:, BLOCK:] = l11
    inv_ref[BLOCK:, :BLOCK] = -near_dot(w11, lw)
    inv_ref[BLOCK:, BLOCK:] = w11
    sol_ref[:, :BLOCK] = y0
    sol_ref[:, BLOCK:] = near_dot(g1 - near_dot(y0, l10, across), w11, across)


def last_kernel(parts_ref, inv_ref, sol_ref, damping_ref, red_ref, grad_ref, coup_ref):
    damping = damping_ref[0]
    total = (parts_ref[0] + parts_ref[1]) + (parts_ref[2] + parts_ref[3])
    cross = jnp.concatenate([total[:128], total[128:256]], axis=1)
    pair, grad, diag = total[256:320], total[320:321], total[321:322]
    row, col = iota((BLOCK, BLOCK), 0), iota((BLOCK, BLOCK), 1)
    row64, lane64 = iota((64, BLOCK), 0), iota((64, BLOCK), 1)
    turned = pltpu.roll(pair, 64, 1)
    top = jnp.where(lane64 < 64, turned, 0.0)
    square = jnp.concatenate([top, pair], axis=0)
    other = square.T
    lower = jnp.where((row >= 64) & (col >= 64), other, square)
    lower = jnp.where(row > col, lower, 0.0)
    main = jnp.where(row == col, jnp.where(row < 64, square, diag), 0.0)
    hess = lower + lower.T + main + damping * main
    coupling = exact_dot(cross, inv_ref[...], ((1,), (1,)))
    coup_ref[...] = coupling
    red_ref[...] = hess - exact_dot(coupling, coupling, ((1,), (1,)))
    grad_ref[...] = grad - exact_dot(sol_ref[...], coupling, ((1,), (1,)))


LOCAL_SCRATCH = [
    pltpu.SMEM((SLOTS + 1,), jnp.int32),
    pltpu.VMEM((ROWS, BLOCK), jnp.bfloat16),
    pltpu.VMEM((ROWS, TEX_W), jnp.bfloat16),
    pltpu.VMEM((1, ROWS), jnp.bfloat16),
    pltpu.SMEM((OBS,), jnp.int32),
    pltpu.SMEM((SLOTS,), jnp.int32),
    pltpu.SMEM((512,), jnp.int32),
    pltpu.SemaphoreType.DMA((8,)),
    pltpu.SemaphoreType.DMA((4,)),
]
PANEL = [pltpu.VMEM((BLOCK, TEX_W), F32), pltpu.VMEM((BLOCK, TEX_W), F32)]


def call(kernel, name, outs, specs, scratch=(), room=24):
    return pl.pallas_call(
        kernel,
        out_shape=[jax.ShapeDtypeStruct(s, F32) for s in outs],
        in_specs=specs,
        out_specs=[VMEM] * len(outs),
        scratch_shapes=scratch,
        name=name,
        compiler_params=pltpu.CompilerParams(vmem_limit_bytes=room * 2**20),
    )


def spread_sum(value, axes):
    count = lax.axis_size(axes)
    copies = jnp.broadcast_to(value[None], (count, *value.shape))
    return jnp.sum(lax.all_to_all(copies, axes, 0, 0), axis=0)


FAR = ("x", "z")
NEAR = ("yl", "yh", "c")


def shards(jac_cam, jac_tex, residual, obs_slot, col_ids, block_pattern, damping):
    cam, tex = jac_cam[0, 0], jac_tex[0, 0]
    res, obs = residual[0], obs_slot[0, 0]
    damping = damping.reshape(1)

    cam_part, tex_part = call(
        local_kernel, "local", [(16 * PIECE, BLOCK), (32, 16, BLOCK)], [HBM] * 6, LOCAL_SCRATCH, 60
    )(cam, tex, res, obs, col_ids, block_pattern)

    share = jnp.sum(lax.all_to_all(tex_part, FAR, 0, 0), axis=0)
    share = spread_sum(share, NEAR)
    copies = jnp.broadcast_to(share[None], (32, *share.shape))
    tex_sums = lax.all_to_all(copies, FAR, 0, 0)

    pieces = lax.psum_scatter(cam_part, "x", scatter_dimension=0, tiled=True)
    parts = lax.all_to_all(pieces.reshape(4, PIECE, BLOCK), "yl", 0, 0)

    texture_factor, inverse, sol = call(
        panel_kernel, "panel", [(TEX_W, TEX_W), (TEX_W, TEX_W), (1, TEX_W)], [VMEM, SMEM], PANEL
    )(tex_sums, damping)
    reduced, gradient, coupling = call(
        last_kernel,
        "last",
        [(BLOCK, BLOCK), (1, BLOCK), (BLOCK, TEX_W)],
        [VMEM] * 3 + [SMEM],
    )(parts, inverse, sol, damping)
    return (reduced[None, None], gradient[None], coupling[None, None], texture_factor)


def solution(mesh):
    fine = Mesh(mesh.devices.reshape(4, 4, 2, 8, 2), ("yl", "x", "yh", "z", "c"))
    img, blk = ("yl", "x"), ("yh", "z", "c")
    return jax.shard_map(
        shards,
        mesh=fine,
        in_specs=(
            P(img, blk, None, None),
            P(img, blk, None, None),
            P(img, blk, None),
            P(img, blk, None),
            P(blk),
            P(),
            P(),
        ),
        out_specs=(
            P(blk, img, None, None),
            P(blk, img, None),
            P(blk, img, None, None),
            P(),
        ),
        check_vma=False,
    )
```

time: 116 us -> 101 us (0.87)
  the two profiles are of different devices: /device:TPU:114 before, /device:TPU:1 now
where the time goes in v2:
time: 101 us; the launch traced here: 100 us
  blocking collectives  57.4 us (57%)
  Pallas kernels  15.9 us (16%)
  between operations  14.7 us (15%)
  waiting for transfers between devices  7.49 us (7%)
  starting transfers between devices  3.52 us (3%)
    all_to_all x1, blocking collectives, shards(): share = jnp.sum(lax.all_to_all(tex_part, FAR, 0, 0), axis=0)  23.4 us
    all_to_all x1, blocking collectives, spread_sum(): return jnp.sum(lax.all_to_all(copies, axes, 0, 0), axis=0)  19.6 us
    all_to_all x1, blocking collectives, shards(): tex_sums = lax.all_to_all(copies, FAR, 0, 0)  14.4 us
    pallas_call x1, Pallas kernels, shards(): call(panel_kernel, 'panel', [(TEX_W, TEX_W), (TEX_W, TEX_W), (1, TEX_W)],...  8.98 us
    all_to_all x1, waiting for transfers between devices, shards(): parts = lax.all_to_all(pieces.reshape(4, PIECE, BLOCK), 'yl', 0, 0)  7.47 us
    pallas_call x1, Pallas kernels, shards(): call(local_kernel, 'local', [(16 * PIECE, BLOCK), (32, 16, BLOCK)], [HBM]...  5.19 us
    all_to_all x1, starting transfers between devices, shards(): parts = lax.all_to_all(pieces.reshape(4, PIECE, BLOCK), 'yl', 0, 0)  3.48 us
  transfers between devices with their start and end apart: 2, of which 1 were waited for; matrix products, arithmetic and copies ran while one was open for 0% of the time, Pallas kernels for 9%

profile of v2, /device:TPU:1, one launch (start us, length us, event | category | flops | bytes accessed | tf_op | source)
XLA Modules:
  0.0 100.1 jit_solution(9892334524803919422)
XLA Ops:
  7.2 0.0 reduce-scatter.2.cloned.1.call-start
  7.2 5.2 %local.1 = (f32[5248,128]{1,0:T(8,128)}, f32[32,16,128]{2,1,0:T(8,128)}) custom-call(bf16[1536,128]{1,0:T(8,128)(2,1)} %bitcast.13, bf16[1536,256]{1,0:T(8,128)(2,1)} %bitcast.11, bf16[1,1536]{1,0:T(2,128)(2,1)} %bitcast.14, s32[192]{0:T(256)} %bitcast.15, s32[16]{0:T(128)} %ids_any.1, s32[512]{0:T(512)} %pattern_any.1), custom_call_target="tpu_custom_call" | custom-call | tf_op jit(solution)/shard_map/local/pallas_call | solution.py:324
  12.4 0.0 copy-start
  12.4 0.0 reduce-scatter.2.cloned.1.call-update
  12.4 0.9 copy-done
  13.4 23.4 %all_to_all.20 = f32[32,16,128]{2,1,0:T(8,128)S(1)} all-to-all(f32[32,16,128]{2,1,0:T(8,128)S(1)} %copy-done), channel_id=1, replica_groups=mesh['yl'=4,'x'=4,'yh'=2,'z'=8,'c'=2] {'x','z'}, dimensions={0} | all-to-all | bytes 524288 | tf_op jit(solution)/shard_map/all_to_all | solution.py:328
  36.8 19.6 %all_to_all.21 = f32[16,16,128]{2,1,0:T(8,128)S(1)} all-to-all(f32[16,16,128]{2,1,0:T(8,128)S(1)} %broadcast_in_dim.10), channel_id=1, replica_groups=mesh['yl'=4,'x'=4,'yh'=2,'z'=8,'c'=2] {'yl','yh','c'}, dimensions={0} | all-to-all | bytes 262144 | tf_op jit(solution)/shard_map/all_to_all | solution.py:312
  56.5 14.4 %all_to_all.22.sums_ref = f32[32,16,128]{2,1,0:T(8,128)S(1)} all-to-all(f32[32,16,128]{2,1,0:T(8,128)S(1)} %broadcast_in_dim.22), channel_id=1, replica_groups=mesh['yl'=4,'x'=4,'yh'=2,'z'=8,'c'=2] {'x','z'}, dimensions={0} | all-to-all | bytes 524288 | tf_op jit(solution)/shard_map/all_to_all | solution.py:331
  70.9 0.0 reduce-scatter.2.cloned.1.call-done
  70.9 3.5 %all-to-all-start = ((f32[4,328,128]{2,1,0:T(8,128)}), f32[4,328,128]{2,1,0:T(8,128)S(1)}, u32[]{:S(2)}, u32[]{:S(2)}) async-start(f32[4,328,128]{2,1,0:T(8,128)} %bitcast.12), calls=%async_computation.1 | async-start | bytes 1343488 | tf_op jit(solution)/shard_map/all_to_all | solution.py:334
  75.0 9.0 %panel.1 = (f32[256,256]{1,0:T(8,128)}, f32[256,256]{1,0:T(8,128)S(1)}, f32[1,256]{1,0:T(1,128)S(1)}) custom-call(f32[32,16,128]{2,1,0:T(8,128)S(1)} %all_to_all.22.sums_ref, f32[1]{0:T(128)} %bitcast.9.damping_ref), custom_call_target="tpu_custom_call" | custom-call | tf_op jit(solution)/shard_map/panel/pallas_call | solution.py:336
  84.0 7.5 %all-to-all-done.parts_ref = f32[4,328,128]{2,1,0:T(8,128)S(1)} async-done(((f32[4,328,128]{2,1,0:T(8,128)}), f32[4,328,128]{2,1,0:T(8,128)S(1)}, u32[]{:S(2)}, u32[]{:S(2)}) %all-to-all-start) | async-done | bytes 671776 | tf_op jit(solution)/shard_map/all_to_all | solution.py:334
  91.5 1.7 %last.1 = (f32[128,128]{1,0:T(8,128)}, f32[1,128]{1,0:T(1,128)}, f32[128,256]{1,0:T(8,128)}) custom-call(f32[4,328,128]{2,1,0:T(8,128)S(1)} %all-to-all-done.parts_ref, f32[256,256]{1,0:T(8,128)S(1)} %get-tuple-element.14.inv_ref, f32[1,256]{1,0:T(1,128)S(1)} %get-tuple-element.15.sol_ref, f32[1]{0:T(128)} %bitcast.10.damping_ref), custom_call_target="tpu_custom_call" | custom-call | tf_op jit(solution)/shard_map/last/pallas_call | solution.py:339
  (4 shorter events, 0.1 us)
Async XLA Ops:
  7.2 63.7 %reduce-scatter.2.cloned.1.call-start = ((), (), s32[]{:S(2)}) async-start(), calls=%async_computation.5 | async-start | bytes 3358720 | tf_op jit(solution)/shard_map/reduce_scatter | solution.py:333
  12.4 1.0 copy-start
  70.9 20.6 %all-to-all-start = ((f32[4,328,128]{2,1,0:T(8,128)}), f32[4,328,128]{2,1,0:T(8,128)S(1)}, u32[]{:S(2)}, u32[]{:S(2)}) async-start(f32[4,328,128]{2,1,0:T(8,128)} %bitcast.12), calls=%async_computation.1 | async-start | bytes 1343488 | tf_op jit(solution)/shard_map/all_to_all | solution.py:334
Sparse Core Ops, SparseCore 0:
  12.6 46.9 reduce-scatter.1

commit v3 on v2

--- a/solution.py
+++ b/solution.py
@@ -61,12 +61,12 @@
     row, col = iota((BLOCK, BLOCK), 0), iota((BLOCK, BLOCK), 1)
     mixed = jnp.where(row >= col, h00, h11)
     diag = jnp.sum(jnp.where(row == col, h11, 0.0), axis=0, keepdims=True)
-    out_ref[:, 8:, :] = jnp.zeros((32, 8, BLOCK), F32)
-    out_ref[:16, :8, :] = mixed.reshape(16, 8, BLOCK)
-    out_ref[16:, :8, :] = h10.reshape(16, 8, BLOCK)
-    out_ref[0, 8:9, :] = grad[:, :BLOCK]
-    out_ref[1, 8:9, :] = grad[:, BLOCK:]
-    out_ref[2, 8:9, :] = diag
+    out_ref[:, 16:, :] = jnp.zeros((16, 8, BLOCK), F32)
+    out_ref[:8, :16, :] = mixed.reshape(8, 16, BLOCK)
+    out_ref[8:, :16, :] = h10.reshape(8, 16, BLOCK)
+    out_ref[0, 16:17, :] = grad[:, :BLOCK]
+    out_ref[1, 16:17, :] = grad[:, BLOCK:]
+    out_ref[2, 16:17, :] = diag
 
 
 def packed(hess):
@@ -78,9 +78,10 @@
 
 
 def local_kernel(
-    cam_any, tex_any, res_any, obs_any, ids_any, pattern_any, out, tex_out,
+    cam_any, tex_any, res_any, obs_any, ids_any, pattern_any, out0, out1, out2, out3, tex_out,
     starts, cam_ref, tex_ref, res_ref, obs_ref, ids_ref, pattern_ref, sems, small,
 ):
+    outs, my_x = (out0, out1, out2, out3), lax.axis_index("x")
     near = [
         pltpu.make_async_copy(src, dst, small.at[i])
         for i, (src, dst) in enumerate(
@@ -107,7 +108,7 @@
     tex_sums(tex_ref, res_ref, ids_ref, pattern_ref, starts, tex_out)
 
     def bounds(k, j):
-        slot = j * 4 + k
+        slot = j * 4 + ((my_x + k) & 3)
         lo, hi = starts[slot] * PER, starts[slot + 1] * PER
         begin = pl.multiple_of(jnp.minimum((lo >> 4) << 4, ROWS - 256), 16)
         code = pattern_ref[ids_ref[slot]]
@@ -123,7 +124,7 @@
     zero = jnp.zeros((BLOCK, BLOCK), F32)
     for k in range(4):
         for j in range(4):
-            base = (k * 4 + j) * PIECE
+            out, base = outs[k], j * PIECE
             lo, hi, begin, keep0, keep1 = bounds(k, j)
             first = jnp.where(sub == k * 4 + j, lo, first)
             last = jnp.where(sub == k * 4 + j, hi, last)
@@ -141,11 +142,12 @@
     spread = jnp.where((lane >= first) & (lane < last), res, 0.0).astype(jnp.bfloat16)
     grad = jnp.dot(spread, cam_ref[...], preferred_element_type=F32)
     for i in range(SLOTS):
-        out[i * PIECE + 320 : i * PIECE + 321, :] = grad[i : i + 1, :]
+        base = (i % 4) * PIECE
+        outs[i // 4][base + 320 : base + 321, :] = grad[i : i + 1, :]
 
     for k in range(4):
         for j in range(4):
-            base = (k * 4 + j) * PIECE
+            out, base = outs[k], j * PIECE
             lo, hi, begin, keep0, keep1 = bounds(k, j)
 
             @pl.when(hi > begin + 256)
@@ -157,6 +159,10 @@
                 out[base + 128 : base + 256, :] += jnp.where(keep1, sums[:, 2 * BLOCK :], zero)
                 out[base + 256 : base + 320, :] += pair
                 out[base + 321 : base + 322, :] += diag
+
+
+def add_kernel(a_ref, b_ref, c_ref, d_ref, out_ref):
+    out_ref[...] = (a_ref[...] + b_ref[...]) + (c_ref[...] + d_ref[...])
 
 
 def split3(value):
@@ -231,9 +237,9 @@
 def panel_kernel(sums_ref, damping_ref, factor_ref, inv_ref, sol_ref, ab, upper):
     damping = damping_ref[0]
     sums = sums_ref[...]
-    both = sums[:, :8, :].reshape(TEX_W, BLOCK)
+    both = sums[:, :16, :].reshape(TEX_W, BLOCK)
     mixed, h10 = both[:BLOCK], both[BLOCK:]
-    g0, g1, diag = sums[0, 8:9, :], sums[1, 8:9, :], sums[2, 8:9, :]
+    g0, g1, diag = sums[0, 16:17, :], sums[1, 16:17, :], sums[2, 16:17, :]
     row, col = iota((BLOCK, BLOCK), 0), iota((BLOCK, BLOCK), 1)
     flipped = mixed.T
     h00 = jnp.where(row >= col, mixed, flipped)
@@ -306,14 +312,19 @@
     )
 
 
+def shift(value, axis, by):
+    n = lax.axis_size(axis)
+    return lax.ppermute(value, axis, [(i, (i + by) % n) for i in range(n)])
+
+
 def spread_sum(value, axes):
     count = lax.axis_size(axes)
     copies = jnp.broadcast_to(value[None], (count, *value.shape))
     return jnp.sum(lax.all_to_all(copies, axes, 0, 0), axis=0)
 
 
-FAR = ("x", "z")
-NEAR = ("yl", "yh", "c")
+FAR = ("z", "c")
+NEAR = ("yl", "x", "yh")
 
 
 def shards(jac_cam, jac_tex, residual, obs_slot, col_ids, block_pattern, damping):
@@ -321,17 +332,24 @@
     res, obs = residual[0], obs_slot[0, 0]
     damping = damping.reshape(1)
 
-    cam_part, tex_part = call(
-        local_kernel, "local", [(16 * PIECE, BLOCK), (32, 16, BLOCK)], [HBM] * 6, LOCAL_SCRATCH, 60
+    *pieces, tex_part = call(
+        local_kernel,
+        "local",
+        [(4 * PIECE, BLOCK)] * 4 + [(16, 24, BLOCK)],
+        [HBM] * 6,
+        LOCAL_SCRATCH,
+        60,
     )(cam, tex, res, obs, col_ids, block_pattern)
+
+    moved = [pieces[0]] + [shift(pieces[k], "x", k) for k in (1, 2, 3)]
+    (own,) = call(add_kernel, "add", [(4 * PIECE, BLOCK)], [VMEM] * 4)(*moved)
 
     share = jnp.sum(lax.all_to_all(tex_part, FAR, 0, 0), axis=0)
     share = spread_sum(share, NEAR)
-    copies = jnp.broadcast_to(share[None], (32, *share.shape))
+    share, own = lax.optimization_barrier((share, own))
+    copies = jnp.broadcast_to(share[None], (16, *share.shape))
     tex_sums = lax.all_to_all(copies, FAR, 0, 0)
-
-    pieces = lax.psum_scatter(cam_part, "x", scatter_dimension=0, tiled=True)
-    parts = lax.all_to_all(pieces.reshape(4, PIECE, BLOCK), "yl", 0, 0)
+    parts = lax.all_to_all(own.reshape(4, PIECE, BLOCK), "yl", 0, 0)
 
     texture_factor, inverse, sol = call(
         panel_kernel, "panel", [(TEX_W, TEX_W), (TEX_W, TEX_W), (1, TEX_W)], [VMEM, SMEM], PANEL

time: 101 us -> 116 us (1.15)
  waiting for transfers between devices: 7.49 us -> 36.4 us
  blocking collectives: 57.4 us -> 35.8 us
  starting transfers between devices: 3.52 us -> 24.3 us
  between operations: 14.7 us -> 1.35 us
  Pallas kernels: 15.9 us -> 17.1 us
    ppermute x0 -> x3, waiting for transfers between devices: none -> 28.2 us  [shift(): return lax.ppermute(value, axis, [(i, (i + by) % n) for i in range(n)])]
    all_to_all x1 -> x0, blocking collectives: 19.6 us -> none  [spread_sum(): return jnp.sum(lax.all_to_all(copies, axes, 0, 0), axis=0)]
    ppermute x0 -> x3, starting transfers between devices: none -> 10.5 us  [shift(): return lax.ppermute(value, axis, [(i, (i + by) % n) for i in range(n)])]
    all_to_all x1 -> x2, starting transfers between devices: 3.48 us -> 13.8 us  [the longest x1 9.65 us: spread_sum(): return jnp.sum(lax.all_to_all(copies, axes, 0, 0), axis=0)]
    all_to_all x1, blocking collectives: 23.4 us -> 22.1 us  [shards(): share = jnp.sum(lax.all_to_all(tex_part, FAR, 0, 0), axis=0)]
    pallas_call x1 -> x2, Pallas kernels: 5.19 us -> 6.42 us  [the longest x1 5.45 us: shards(): call(local_kernel, 'local', [(4 * PIECE, BLOCK)] * 4 + [(16, 24, BLOCK)],...]
    all_to_all x1 -> x2, waiting for transfers between devices: 7.47 us -> 8.24 us  [the longest x1 8.24 us: shards(): parts = lax.all_to_all(own.reshape(4, PIECE, BLOCK), 'yl', 0, 0)]
  transfers between devices with their start and end apart: 2 -> 5, of which waited for: 1 -> 3; matrix products, arithmetic and copies ran while one was open for 0% -> 0% of each run, Pallas kernels for 9% -> 9%
where the time goes in v3:
time: 116 us
  waiting for transfers between devices  36.4 us (31%)
  blocking collectives  35.8 us (31%)
  starting transfers between devices  24.3 us (21%)
  Pallas kernels  17.1 us (15%)
  between operations  1.35 us (1%)
    ppermute x3, waiting for transfers between devices, shift(): return lax.ppermute(value, axis, [(i, (i + by) % n) for i in range(n)])  28.2 us
    all_to_all x1, blocking collectives, shards(): share = jnp.sum(lax.all_to_all(tex_part, FAR, 0, 0), axis=0)  22.1 us
    all_to_all x1, blocking collectives, shards(): tex_sums = lax.all_to_all(copies, FAR, 0, 0)  13.7 us
    ppermute x3, starting transfers between devices, shift(): return lax.ppermute(value, axis, [(i, (i + by) % n) for i in range(n)])  10.5 us
    all_to_all x1, starting transfers between devices, spread_sum(): return jnp.sum(lax.all_to_all(copies, axes, 0, 0), axis=0)  9.65 us
    pallas_call x1, Pallas kernels, shards(): call(panel_kernel, 'panel', [(TEX_W, TEX_W), (TEX_W, TEX_W), (1, TEX_W)],...  8.98 us
    all_to_all x1, waiting for transfers between devices, shards(): parts = lax.all_to_all(own.reshape(4, PIECE, BLOCK), 'yl', 0, 0)  8.24 us
    pallas_call x1, Pallas kernels, shards(): call(local_kernel, 'local', [(4 * PIECE, BLOCK)] * 4 + [(16, 24, BLOCK)],...  5.45 us
  transfers between devices with their start and end apart: 5, of which 3 were waited for; matrix products, arithmetic and copies ran while one was open for 0% of the time, Pallas kernels for 9%

profile of v3, /device:TPU:1, one launch (start us, length us, event | category | flops | bytes accessed | tf_op | source)
XLA Modules:
  0.0 115.9 jit_solution(11415736324738121740)
XLA Ops:
  0.6 5.4 %local.1 = (f32[1312,128]{1,0:T(8,128)}, f32[1312,128]{1,0:T(8,128)}, f32[1312,128]{1,0:T(8,128)}, f32[1312,128]{1,0:T(8,128)}, f32[16,24,128]{2,1,0:T(8,128)}) custom-call(bf16[1536,128]{1,0:T(8,128)(2,1)} %bitcast.12, bf16[1536,256]{1,0:T(8,128)(2,1)} %bitcast.11, bf16[1,1536]{1,0:T(2,128)(2,1)} %bitcast.13, s32[192]{0:T(256)} %bitcast.14, s32[16]{0:T(128)} %ids_any.1, ...), custom_call_target="tpu_custom_call" | custom-call | tf_op jit(solution)/shard_map/local/pallas_call | solution.py:335
  6.1 22.1 %all_to_all.20 = f32[16,24,128]{2,1,0:T(8,128)S(1)} all-to-all(f32[16,24,128]{2,1,0:T(8,128)} %get-tuple-element.17), channel_id=1, replica_groups=mesh['yl'=4,'x'=4,'yh'=2,'z'=8,'c'=2] {'z','c'}, dimensions={0} | all-to-all | bytes 393216 | tf_op jit(solution)/shard_map/all_to_all | solution.py:347
  28.2 0.0 copy-start.1
  28.2 0.0 copy-start
  28.2 0.8 broadcast_in_dim.10
  29.0 9.6 %all-to-all-start.1 = ((f32[32,24,128]{2,1,0:T(8,128)}), f32[32,24,128]{2,1,0:T(8,128)S(1)}, u32[]{:S(2)}, u32[]{:S(2)}) async-start(f32[32,24,128]{2,1,0:T(8,128)} %broadcast_in_dim.10), calls=%async_computation.1 | async-start | bytes 786432 | tf_op jit(solution)/shard_map/all_to_all | solution.py:323
  38.7 3.1 %collective-permute-start = (f32[1312,128]{1,0:T(8,128)}, f32[1312,128]{1,0:T(8,128)S(1)}, u32[]{:S(2)}, u32[]{:S(2)}) collective-permute-start(f32[1312,128]{1,0:T(8,128)} %get-tuple-element.19), channel_id=1, source_target_pairs={{0,32},{32,64},{64,96},{96,0},{1,33},{33,65},{65,97},{97,1},{2,34}... | collective-permute-start | bytes 2015240 | tf_op jit(solution)/shard_map/ppermute | solution.py:317
  41.8 4.3 %collective-permute-start.1 = (f32[1312,128]{1,0:T(8,128)}, f32[1312,128]{1,0:T(8,128)S(1)}, u32[]{:S(2)}, u32[]{:S(2)}) collective-permute-start(f32[1312,128]{1,0:T(8,128)} %get-tuple-element.20), channel_id=1, source_target_pairs={{0,64},{32,96},{64,0},{96,32},{1,65},{33,97},{65,1},{97,33},{2,66}... | collective-permute-start | bytes 2015240 | tf_op jit(solution)/shard_map/ppermute | solution.py:317
  46.1 0.0 copy-done.1
  46.1 3.1 %collective-permute-start.2 = (f32[1312,128]{1,0:T(8,128)S(1)}, f32[1312,128]{1,0:T(8,128)S(1)}, u32[]{:S(2)}, u32[]{:S(2)}) collective-permute-start(f32[1312,128]{1,0:T(8,128)S(1)} %copy-done.1), channel_id=1, source_target_pairs={{0,96},{32,0},{64,32},{96,64},{1,97},{33,1},{65,33},{97,65},{2,98}... | collective-permute-start | bytes 2015240 | tf_op jit(solution)/shard_map/ppermute | solution.py:317
  49.2 13.2 %collective-permute-done.b_ref = f32[1312,128]{1,0:T(8,128)S(1)} collective-permute-done((f32[1312,128]{1,0:T(8,128)}, f32[1312,128]{1,0:T(8,128)S(1)}, u32[]{:S(2)}, u32[]{:S(2)}) %collective-permute-start) | collective-permute-done | bytes 671776 | tf_op jit(solution)/shard_map/ppermute | solution.py:317
  62.4 15.0 %collective-permute-done.1.c_ref = f32[1312,128]{1,0:T(8,128)S(1)} collective-permute-done((f32[1312,128]{1,0:T(8,128)}, f32[1312,128]{1,0:T(8,128)S(1)}, u32[]{:S(2)}, u32[]{:S(2)}) %collective-permute-start.1) | collective-permute-done | bytes 671776 | tf_op jit(solution)/shard_map/ppermute | solution.py:317
  77.4 0.0 collective-permute-done.2.d_ref
  77.4 0.0 copy-done
  77.5 1.0 add.1
  78.4 0.0 all-to-all-done.1
  78.5 13.7 %all_to_all.21.sums_ref = f32[16,24,128]{2,1,0:T(8,128)S(1)} all-to-all(f32[16,24,128]{2,1,0:T(8,128)S(1)} %broadcast_in_dim.22), channel_id=1, replica_groups=mesh['yl'=4,'x'=4,'yh'=2,'z'=8,'c'=2] {'z','c'}, dimensions={0} | all-to-all | bytes 393216 | tf_op jit(solution)/shard_map/all_to_all | solution.py:351
  92.2 4.1 %all-to-all-start.2 = ((f32[4,328,128]{2,1,0:T(8,128)}), f32[4,328,128]{2,1,0:T(8,128)S(1)}, u32[]{:S(2)}, u32[]{:S(2)}) async-start(f32[4,328,128]{2,1,0:T(8,128)} %bitcast.4), calls=%async_computation.2 | async-start | bytes 1343488 | tf_op jit(solution)/shard_map/all_to_all | solution.py:352
  96.9 9.0 %panel.1 = (f32[256,256]{1,0:T(8,128)}, f32[256,256]{1,0:T(8,128)S(1)}, f32[1,256]{1,0:T(1,128)S(1)}) custom-call(f32[16,24,128]{2,1,0:T(8,128)S(1)} %all_to_all.21.sums_ref, f32[1]{0:T(128)} %bitcast.9.damping_ref), custom_call_target="tpu_custom_call" | custom-call | tf_op jit(solution)/shard_map/panel/pallas_call | solution.py:354
  105.9 8.2 %all-to-all-done.2.parts_ref = f32[4,328,128]{2,1,0:T(8,128)S(1)} async-done(((f32[4,328,128]{2,1,0:T(8,128)}), f32[4,328,128]{2,1,0:T(8,128)S(1)}, u32[]{:S(2)}, u32[]{:S(2)}) %all-to-all-start.2) | async-done | bytes 671776 | tf_op jit(solution)/shard_map/all_to_all | solution.py:352
  114.2 1.7 %last.1 = (f32[128,128]{1,0:T(8,128)}, f32[1,128]{1,0:T(1,128)}, f32[128,256]{1,0:T(8,128)}) custom-call(f32[4,328,128]{2,1,0:T(8,128)S(1)} %all-to-all-done.2.parts_ref, f32[256,256]{1,0:T(8,128)S(1)} %get-tuple-element.24.inv_ref, f32[1,256]{1,0:T(1,128)S(1)} %get-tuple-element.25.sol_ref, f32[1]{0:T(128)} %bitcast.10.damping_ref), custom_call_target="tpu_custom_call" | custom-call | tf_op jit(solution)/shard_map/last/pallas_call | solution.py:357
  (3 shorter events, 0.1 us)
Async XLA Ops:
  28.2 17.9 %copy-start.1 = (f32[1312,128]{1,0:T(8,128)S(1)}, f32[1312,128]{1,0:T(8,128)}, u32[]{:S(2)}) copy-start(f32[1312,128]{1,0:T(8,128)} %get-tuple-element.21) | copy-start | bytes 2015236
  28.2 49.2 %copy-start = (f32[1312,128]{1,0:T(8,128)S(1)}, f32[1312,128]{1,0:T(8,128)}, u32[]{:S(2)}) copy-start(f32[1312,128]{1,0:T(8,128)} %get-tuple-element.18.a_ref) | copy-start | bytes 2015236
  29.0 49.4 %all-to-all-start.1 = ((f32[32,24,128]{2,1,0:T(8,128)}), f32[32,24,128]{2,1,0:T(8,128)S(1)}, u32[]{:S(2)}, u32[]{:S(2)}) async-start(f32[32,24,128]{2,1,0:T(8,128)} %broadcast_in_dim.10), calls=%async_computation.1 | async-start | bytes 786432 | tf_op jit(solution)/shard_map/all_to_all | solution.py:323
  38.7 23.8 %collective-permute-start = (f32[1312,128]{1,0:T(8,128)}, f32[1312,128]{1,0:T(8,128)S(1)}, u32[]{:S(2)}, u32[]{:S(2)}) collective-permute-start(f32[1312,128]{1,0:T(8,128)} %get-tuple-element.19), channel_id=1, source_target_pairs={{0,32},{32,64},{64,96},{96,0},{1,33},{33,65},{65,97},{97,1},{2,34}... | collective-permute-start | bytes 2015240 | tf_op jit(solution)/shard_map/ppermute | solution.py:317
  41.8 35.6 %collective-permute-start.1 = (f32[1312,128]{1,0:T(8,128)}, f32[1312,128]{1,0:T(8,128)S(1)}, u32[]{:S(2)}, u32[]{:S(2)}) collective-permute-start(f32[1312,128]{1,0:T(8,128)} %get-tuple-element.20), channel_id=1, source_target_pairs={{0,64},{32,96},{64,0},{96,32},{1,65},{33,97},{65,1},{97,33},{2,66}... | collective-permute-start | bytes 2015240 | tf_op jit(solution)/shard_map/ppermute | solution.py:317
  46.1 31.3 %collective-permute-start.2 = (f32[1312,128]{1,0:T(8,128)S(1)}, f32[1312,128]{1,0:T(8,128)S(1)}, u32[]{:S(2)}, u32[]{:S(2)}) collective-permute-start(f32[1312,128]{1,0:T(8,128)S(1)} %copy-done.1), channel_id=1, source_target_pairs={{0,96},{32,0},{64,32},{96,64},{1,97},{33,1},{65,33},{97,65},{2,98}... | collective-permute-start | bytes 2015240 | tf_op jit(solution)/shard_map/ppermute | solution.py:317
  92.2 22.0 %all-to-all-start.2 = ((f32[4,328,128]{2,1,0:T(8,128)}), f32[4,328,128]{2,1,0:T(8,128)S(1)}, u32[]{:S(2)}, u32[]{:S(2)}) async-start(f32[4,328,128]{2,1,0:T(8,128)} %bitcast.4), calls=%async_computation.2 | async-start | bytes 1343488 | tf_op jit(solution)/shard_map/all_to_all | solution.py:352

commit v4 on v2

--- a/solution.py
+++ b/solution.py
@@ -45,7 +45,37 @@
     lax.fori_loop(0, OBS, step, 0, unroll=8)
 
 
-def tex_sums(tex_ref, res_ref, ids_ref, pattern_ref, starts, out_ref):
+def fetch(pairs, sems):
+    copies = []
+    for src, dst in pairs:
+        step = dst.shape[0] // 4 if dst.shape[0] == ROWS else dst.shape[0]
+        for n in range(0, dst.shape[0], step):
+            part = pl.ds(n, step)
+            copies.append(pltpu.make_async_copy(src.at[part], dst.at[part], sems.at[len(copies)]))
+    for copy in copies:
+        copy.start()
+    return copies
+
+
+def tex_kernel(
+    tex_any, res_any, obs_any, ids_any, pattern_any, out_ref,
+    starts, tex_ref, res_ref, obs_ref, ids_ref, pattern_ref, sems,
+):
+    copies = fetch(
+        (
+            (obs_any, obs_ref),
+            (ids_any, ids_ref),
+            (pattern_any, pattern_ref),
+            (res_any, res_ref),
+            (tex_any, tex_ref),
+        ),
+        sems,
+    )
+    for copy in copies[:4]:
+        copy.wait()
+    find_starts(obs_ref, starts)
+    for copy in copies[4:]:
+        copy.wait()
     obs_index = iota((OBS, BLOCK), 0)
     masks = []
     for bit in range(2):
@@ -77,37 +107,33 @@
     return pair, jnp.sum(jnp.where(row == lane - 64, low, 0.0), axis=0, keepdims=True)
 
 
-def local_kernel(
-    cam_any, tex_any, res_any, obs_any, ids_any, pattern_any, out, tex_out,
-    starts, cam_ref, tex_ref, res_ref, obs_ref, ids_ref, pattern_ref, sems, small,
+def cam_kernel(
+    cam_any, tex_any, res_any, obs_any, ids_any, pattern_any, out0, out1, out2, out3,
+    starts, cam_ref, tex_ref, res_ref, obs_ref, ids_ref, pattern_ref, sems,
 ):
-    near = [
-        pltpu.make_async_copy(src, dst, small.at[i])
-        for i, (src, dst) in enumerate(
-            ((obs_any, obs_ref), (ids_any, ids_ref), (pattern_any, pattern_ref), (res_any, res_ref))
-        )
-    ]
-    for copy in near:
-        copy.start()
-    copies = []
-    for i, (src, dst) in enumerate(((cam_any, cam_ref), (tex_any, tex_ref))):
-        for n in range(4):
-            rows = pl.ds(n * (ROWS // 4), ROWS // 4)
-            copies.append(pltpu.make_async_copy(src.at[rows, :], dst.at[rows, :], sems.at[i * 4 + n]))
-    for copy in copies:
-        copy.start()
-    for copy in near:
+    outs, my_x, my_yl = (out0, out1, out2, out3), lax.axis_index("x"), lax.axis_index("yl")
+    copies = fetch(
+        (
+            (obs_any, obs_ref),
+            (ids_any, ids_ref),
+            (pattern_any, pattern_ref),
+            (res_any, res_ref),
+            (cam_any, cam_ref),
+            (tex_any, tex_ref),
+        ),
+        sems,
+    )
+    for copy in copies[:4]:
         copy.wait()
     find_starts(obs_ref, starts)
     sub = iota((SLOTS, BLOCK), 0)
     first = jnp.zeros((SLOTS, BLOCK), jnp.int32)
     last = jnp.zeros((SLOTS, BLOCK), jnp.int32)
-    for copy in copies:
+    for copy in copies[4:]:
         copy.wait()
-    tex_sums(tex_ref, res_ref, ids_ref, pattern_ref, starts, tex_out)
 
     def bounds(k, j):
-        slot = j * 4 + k
+        slot = ((my_yl + j) & 3) * 4 + ((my_x + k) & 3)
         lo, hi = starts[slot] * PER, starts[slot + 1] * PER
         begin = pl.multiple_of(jnp.minimum((lo >> 4) << 4, ROWS - 256), 16)
         code = pattern_ref[ids_ref[slot]]
@@ -123,7 +149,7 @@
     zero = jnp.zeros((BLOCK, BLOCK), F32)
     for k in range(4):
         for j in range(4):
-            base = (k * 4 + j) * PIECE
+            out, base = outs[k], j * PIECE
             lo, hi, begin, keep0, keep1 = bounds(k, j)
             first = jnp.where(sub == k * 4 + j, lo, first)
             last = jnp.where(sub == k * 4 + j, hi, last)
@@ -141,11 +167,12 @@
     spread = jnp.where((lane >= first) & (lane < last), res, 0.0).astype(jnp.bfloat16)
     grad = jnp.dot(spread, cam_ref[...], preferred_element_type=F32)
     for i in range(SLOTS):
-        out[i * PIECE + 320 : i * PIECE + 321, :] = grad[i : i + 1, :]
+        base = (i % 4) * PIECE
+        outs[i // 4][base + 320 : base + 321, :] = grad[i : i + 1, :]
 
     for k in range(4):
         for j in range(4):
-            base = (k * 4 + j) * PIECE
+            out, base = outs[k], j * PIECE
             lo, hi, begin, keep0, keep1 = bounds(k, j)
 
             @pl.when(hi > begin + 256)
@@ -157,6 +184,12 @@
                 out[base + 128 : base + 256, :] += jnp.where(keep1, sums[:, 2 * BLOCK :], zero)
                 out[base + 256 : base + 320, :] += pair
                 out[base + 321 : base + 322, :] += diag
+
+
+def add_kernel(a_ref, b_ref, c_ref, d_ref, *outs):
+    for j in range(4):
+        rows = slice(j * PIECE, (j + 1) * PIECE)
+        outs[j][...] = (a_ref[rows, :] + b_ref[rows, :]) + (c_ref[rows, :] + d_ref[rows, :])
 
 
 def split3(value):
@@ -259,9 +292,9 @@
     sol_ref[:, BLOCK:] = near_dot(g1 - near_dot(y0, l10, across), w11, across)
 
 
-def last_kernel(parts_ref, inv_ref, sol_ref, damping_ref, red_ref, grad_ref, coup_ref):
+def last_kernel(a_ref, b_ref, c_ref, d_ref, inv_ref, sol_ref, damping_ref, red_ref, grad_ref, coup_ref):
     damping = damping_ref[0]
-    total = (parts_ref[0] + parts_ref[1]) + (parts_ref[2] + parts_ref[3])
+    total = (a_ref[...] + b_ref[...]) + (c_ref[...] + d_ref[...])
     cross = jnp.concatenate([total[:128], total[128:256]], axis=1)
     pair, grad, diag = total[256:320], total[320:321], total[321:322]
     row, col = iota((BLOCK, BLOCK), 0), iota((BLOCK, BLOCK), 1)
@@ -280,17 +313,16 @@
     grad_ref[...] = grad - exact_dot(sol_ref[...], coupling, ((1,), (1,)))
 
 
-LOCAL_SCRATCH = [
-    pltpu.SMEM((SLOTS + 1,), jnp.int32),
-    pltpu.VMEM((ROWS, BLOCK), jnp.bfloat16),
+SMALL_SCRATCH = [
     pltpu.VMEM((ROWS, TEX_W), jnp.bfloat16),
     pltpu.VMEM((1, ROWS), jnp.bfloat16),
     pltpu.SMEM((OBS,), jnp.int32),
     pltpu.SMEM((SLOTS,), jnp.int32),
     pltpu.SMEM((512,), jnp.int32),
-    pltpu.SemaphoreType.DMA((8,)),
-    pltpu.SemaphoreType.DMA((4,)),
+    pltpu.SemaphoreType.DMA((12,)),
 ]
+TEX_SCRATCH = [pltpu.SMEM((SLOTS + 1,), jnp.int32), *SMALL_SCRATCH]
+CAM_SCRATCH = [TEX_SCRATCH[0], pltpu.VMEM((ROWS, BLOCK), jnp.bfloat16), *SMALL_SCRATCH]
 PANEL = [pltpu.VMEM((BLOCK, TEX_W), F32), pltpu.VMEM((BLOCK, TEX_W), F32)]
 
 
@@ -306,6 +338,11 @@
     )
 
 
+def shift(value, axis, by):
+    n = lax.axis_size(axis)
+    return lax.ppermute(value, axis, [(i, (i + by) % n) for i in range(n)])
+
+
 def spread_sum(value, axes):
     count = lax.axis_size(axes)
     copies = jnp.broadcast_to(value[None], (count, *value.shape))
@@ -321,17 +358,20 @@
     res, obs = residual[0], obs_slot[0, 0]
     damping = damping.reshape(1)
 
-    cam_part, tex_part = call(
-        local_kernel, "local", [(16 * PIECE, BLOCK), (32, 16, BLOCK)], [HBM] * 6, LOCAL_SCRATCH, 60
-    )(cam, tex, res, obs, col_ids, block_pattern)
+    (tex_part,) = call(tex_kernel, "tex", [(32, 16, BLOCK)], [HBM] * 5, TEX_SCRATCH, 60)(
+        tex, res, obs, col_ids, block_pattern
+    )
+    pieces = call(cam_kernel, "cam", [(4 * PIECE, BLOCK)] * 4, [HBM] * 6, CAM_SCRATCH, 60)(
+        cam, tex, res, obs, col_ids, block_pattern
+    )
+    moved = [pieces[0]] + [shift(pieces[k], "x", k) for k in (1, 2, 3)]
+    pieces = call(add_kernel, "add", [(PIECE, BLOCK)] * 4, [VMEM] * 4)(*moved)
+    moved = [pieces[0]] + [shift(pieces[j], "yl", j) for j in (1, 2, 3)]
 
     share = jnp.sum(lax.all_to_all(tex_part, FAR, 0, 0), axis=0)
     share = spread_sum(share, NEAR)
     copies = jnp.broadcast_to(share[None], (32, *share.shape))
     tex_sums = lax.all_to_all(copies, FAR, 0, 0)
-
-    pieces = lax.psum_scatter(cam_part, "x", scatter_dimension=0, tiled=True)
-    parts = lax.all_to_all(pieces.reshape(4, PIECE, BLOCK), "yl", 0, 0)
 
     texture_factor, inverse, sol = call(
         panel_kernel, "panel", [(TEX_W, TEX_W), (TEX_W, TEX_W), (1, TEX_W)], [VMEM, SMEM], PANEL
@@ -340,8 +380,8 @@
         last_kernel,
         "last",
         [(BLOCK, BLOCK), (1, BLOCK), (BLOCK, TEX_W)],
-        [VMEM] * 3 + [SMEM],
-    )(parts, inverse, sol, damping)
+        [VMEM] * 6 + [SMEM],
+    )(*moved, inverse, sol, damping)
     return (reduced[None, None], gradient[None], coupling[None, None], texture_factor)
 
 

time: 101 us -> 85.1 us (0.84)
  the two profiles are of different devices: /device:TPU:1 before, /device:TPU:43 now
where the time goes in v4:
time: 85.1 us; the launch traced here: 84.6 us
  starting transfers between devices  40.7 us (48%)
  Pallas kernels  18.9 us (22%)
  blocking collectives  13.8 us (16%)
  waiting for transfers between devices  8.97 us (11%)
  between operations  1.42 us (2%)
    ppermute x6, starting transfers between devices, shift(): return lax.ppermute(value, axis, [(i, (i + by) % n) for i in range(n)])  20.1 us
    all_to_all x1, blocking collectives, spread_sum(): return jnp.sum(lax.all_to_all(copies, axes, 0, 0), axis=0)  13.8 us
    all_to_all x1, starting transfers between devices, shards(): share = jnp.sum(lax.all_to_all(tex_part, FAR, 0, 0), axis=0)  12.9 us
    pallas_call x1, Pallas kernels, shards(): call(panel_kernel, 'panel', [(TEX_W, TEX_W), (TEX_W, TEX_W), (1, TEX_W)],...  8.99 us
    ppermute x6, waiting for transfers between devices, shift(): return lax.ppermute(value, axis, [(i, (i + by) % n) for i in range(n)])  8.97 us
    all_to_all x1, starting transfers between devices, shards(): tex_sums = lax.all_to_all(copies, FAR, 0, 0)  7.75 us
    pallas_call x1, Pallas kernels, shards(): call(cam_kernel, 'cam', [(4 * PIECE, BLOCK)] * 4, [HBM] * 6, CAM_SCRATCH,...  4.68 us
    pallas_call x1, Pallas kernels, shards(): call(tex_kernel, 'tex', [(32, 16, BLOCK)], [HBM] * 5, TEX_SCRATCH, 60)  2.69 us
  transfers between devices with their start and end apart: 8, of which 2 were waited for; matrix products, arithmetic and copies ran while one was open for 1% of the time, Pallas kernels for 17%

profile of v4, /device:TPU:43, one launch (start us, length us, event | category | flops | bytes accessed | tf_op | source)
XLA Modules:
  0.0 84.6 jit_solution(15637455821052385192)
XLA Ops:
  0.6 2.7 %tex.1 = f32[32,16,128]{2,1,0:T(8,128)} custom-call(bf16[1536,256]{1,0:T(8,128)(2,1)} %bitcast.10, bf16[1,1536]{1,0:T(2,128)(2,1)} %bitcast.13, s32[192]{0:T(256)} %bitcast.15, s32[16]{0:T(128)} %ids_any.3, s32[512]{0:T(512)} %pattern_any.3), custom_call_target="tpu_custom_call" | custom-call | tf_op jit(solution)/shard_map/tex/pallas_call | solution.py:361
  3.3 12.9 %all-to-all-start = ((f32[32,16,128]{2,1,0:T(8,128)}), f32[32,16,128]{2,1,0:T(8,128)S(1)}, u32[]{:S(2)}, u32[]{:S(2)}) async-start(f32[32,16,128]{2,1,0:T(8,128)} %tex.1), calls=%async_computation | async-start | bytes 524288 | tf_op jit(solution)/shard_map/all_to_all | solution.py:371
  16.3 4.7 %cam.1 = (f32[1312,128]{1,0:T(8,128)}, f32[1312,128]{1,0:T(8,128)}, f32[1312,128]{1,0:T(8,128)}, f32[1312,128]{1,0:T(8,128)}) custom-call(bf16[1536,128]{1,0:T(8,128)(2,1)} %bitcast.12, bf16[1536,256]{1,0:T(8,128)(2,1)} %bitcast.11, bf16[1,1536]{1,0:T(2,128)(2,1)} %bitcast.14, s32[192]{0:T(256)} %bitcast.16, s32[16]{0:T(128)} %ids_any.3, s32[512]{0:T(512)} %pattern_any.3), custom_call_target="tpu_custom_call" | custom-call | tf_op jit(solution)/shard_map/cam/pallas_call | solution.py:364
  20.9 3.1 %collective-permute-start = (f32[1312,128]{1,0:T(8,128)}, f32[1312,128]{1,0:T(8,128)S(1)}, u32[]{:S(2)}, u32[]{:S(2)}) collective-permute-start(f32[1312,128]{1,0:T(8,128)} %get-tuple-element.19), channel_id=1, source_target_pairs={{0,32},{32,64},{64,96},{96,0},{1,33},{33,65},{65,97},{97,1},{2,34}... | collective-permute-start | bytes 2015240 | tf_op jit(solution)/shard_map/ppermute | solution.py:343
  24.0 2.8 %collective-permute-start.1 = (f32[1312,128]{1,0:T(8,128)}, f32[1312,128]{1,0:T(8,128)S(1)}, u32[]{:S(2)}, u32[]{:S(2)}) collective-permute-start(f32[1312,128]{1,0:T(8,128)} %get-tuple-element.20), channel_id=1, source_target_pairs={{0,64},{32,96},{64,0},{96,32},{1,65},{33,97},{65,1},{97,33},{2,66}... | collective-permute-start | bytes 2015240 | tf_op jit(solution)/shard_map/ppermute | solution.py:343
  26.8 3.8 %collective-permute-start.2 = (f32[1312,128]{1,0:T(8,128)}, f32[1312,128]{1,0:T(8,128)S(1)}, u32[]{:S(2)}, u32[]{:S(2)}) collective-permute-start(f32[1312,128]{1,0:T(8,128)} %get-tuple-element.21), channel_id=1, source_target_pairs={{0,96},{32,0},{64,32},{96,64},{1,97},{33,1},{65,33},{97,65},{2,98}... | collective-permute-start | bytes 2015240 | tf_op jit(solution)/shard_map/ppermute | solution.py:343
  30.6 0.0 all-to-all-done
  30.7 0.0 copy-start
  30.7 13.8 %all_to_all.15 = f32[16,16,128]{2,1,0:T(8,128)S(1)} all-to-all(f32[16,16,128]{2,1,0:T(8,128)S(1)} %broadcast_in_dim.10), channel_id=1, replica_groups=mesh['yl'=4,'x'=4,'yh'=2,'z'=8,'c'=2] {'yl','yh','c'}, dimensions={0} | all-to-all | bytes 262144 | tf_op jit(solution)/shard_map/all_to_all | solution.py:349
  44.5 0.7 broadcast_in_dim.22
  45.2 7.7 %all-to-all-start.2 = ((f32[32,16,128]{2,1,0:T(8,128)}), f32[32,16,128]{2,1,0:T(8,128)S(1)}, u32[]{:S(2)}, u32[]{:S(2)}) async-start(f32[32,16,128]{2,1,0:T(8,128)} %broadcast_in_dim.22), calls=%async_computation.2 | async-start | bytes 524288 | tf_op jit(solution)/shard_map/all_to_all | solution.py:374
  53.0 0.0 collective-permute-done.b_ref
  53.0 0.0 collective-permute-done.1.c_ref
  53.0 6.7 %collective-permute-done.2.d_ref = f32[1312,128]{1,0:T(8,128)S(1)} collective-permute-done((f32[1312,128]{1,0:T(8,128)}, f32[1312,128]{1,0:T(8,128)S(1)}, u32[]{:S(2)}, u32[]{:S(2)}) %collective-permute-start.2) | collective-permute-done | bytes 671776 | tf_op jit(solution)/shard_map/ppermute | solution.py:343
  59.7 0.0 copy-done
  59.7 0.8 add.1
  60.5 2.2 %collective-permute-start.3 = (f32[328,128]{1,0:T(8,128)}, f32[328,128]{1,0:T(8,128)S(1)}, u32[]{:S(2)}, u32[]{:S(2)}) collective-permute-start(f32[328,128]{1,0:T(8,128)} %get-tuple-element.23), channel_id=1, source_target_pairs={{0,128},{128,256},{256,384},{384,0},{1,129},{129,257},{257,385},{3... | collective-permute-start | bytes 503816 | tf_op jit(solution)/shard_map/ppermute | solution.py:343
  62.7 6.3 %collective-permute-start.4 = (f32[328,128]{1,0:T(8,128)S(1)}, f32[328,128]{1,0:T(8,128)S(1)}, u32[]{:S(2)}, u32[]{:S(2)}) collective-permute-start(f32[328,128]{1,0:T(8,128)S(1)} %get-tuple-element.24), channel_id=1, source_target_pairs={{0,256},{128,384},{256,0},{384,128},{1,257},{129,385},{257,1},{385... | collective-permute-start | bytes 503816 | tf_op jit(solution)/shard_map/ppermute | solution.py:343
  69.0 1.9 %collective-permute-start.5 = (f32[328,128]{1,0:T(8,128)S(1)}, f32[328,128]{1,0:T(8,128)S(1)}, u32[]{:S(2)}, u32[]{:S(2)}) collective-permute-start(f32[328,128]{1,0:T(8,128)S(1)} %get-tuple-element.25), channel_id=1, source_target_pairs={{0,384},{128,0},{256,128},{384,256},{1,385},{129,1},{257,129},{385... | collective-permute-start | bytes 503816 | tf_op jit(solution)/shard_map/ppermute | solution.py:343
  71.6 0.0 all-to-all-done.2.sums_ref
  71.6 9.0 %panel.1 = (f32[256,256]{1,0:T(8,128)}, f32[256,256]{1,0:T(8,128)S(1)}, f32[1,256]{1,0:T(1,128)S(1)}) custom-call(f32[32,16,128]{2,1,0:T(8,128)S(1)} %all-to-all-done.2.sums_ref, f32[1]{0:T(128)} %bitcast.8.damping_ref), custom_call_target="tpu_custom_call" | custom-call | tf_op jit(solution)/shard_map/panel/pallas_call | solution.py:376
  80.6 0.0 collective-permute-done.3.b_ref
  80.6 0.0 collective-permute-done.4.c_ref
  80.6 2.3 %collective-permute-done.5.d_ref = f32[328,128]{1,0:T(8,128)S(1)} collective-permute-done((f32[328,128]{1,0:T(8,128)S(1)}, f32[328,128]{1,0:T(8,128)S(1)}, u32[]{:S(2)}, u32[]{:S(2)}) %collective-permute-start.5) | collective-permute-done | bytes 167968 | tf_op jit(solution)/shard_map/ppermute | solution.py:343
  82.9 1.7 %last.1 = (f32[128,128]{1,0:T(8,128)}, f32[1,128]{1,0:T(1,128)}, f32[128,256]{1,0:T(8,128)}) custom-call(f32[328,128]{1,0:T(8,128)S(1)} %get-tuple-element.22.a_ref, f32[328,128]{1,0:T(8,128)S(1)} %collective-permute-done.3.b_ref, f32[328,128]{1,0:T(8,128)S(1)} %collective-permute-done.4.c_ref, f32[328,128]{1,0:T(8,128)S(1)} %collective-permute-done.5.d_ref, ...), custom_call_target="tpu_custom_call" | custom-call | tf_op jit(solution)/shard_map/last/pallas_call | solution.py:379
  (3 shorter events, 0.1 us)
Async XLA Ops:
  3.3 27.3 %all-to-all-start = ((f32[32,16,128]{2,1,0:T(8,128)}), f32[32,16,128]{2,1,0:T(8,128)S(1)}, u32[]{:S(2)}, u32[]{:S(2)}) async-start(f32[32,16,128]{2,1,0:T(8,128)} %tex.1), calls=%async_computation | async-start | bytes 524288 | tf_op jit(solution)/shard_map/all_to_all | solution.py:371
  20.9 32.0 %collective-permute-start = (f32[1312,128]{1,0:T(8,128)}, f32[1312,128]{1,0:T(8,128)S(1)}, u32[]{:S(2)}, u32[]{:S(2)}) collective-permute-start(f32[1312,128]{1,0:T(8,128)} %get-tuple-element.19), channel_id=1, source_target_pairs={{0,32},{32,64},{64,96},{96,0},{1,33},{33,65},{65,97},{97,1},{2,34}... | collective-permute-start | bytes 2015240 | tf_op jit(solution)/shard_map/ppermute | solution.py:343
  24.0 28.9 %collective-permute-start.1 = (f32[1312,128]{1,0:T(8,128)}, f32[1312,128]{1,0:T(8,128)S(1)}, u32[]{:S(2)}, u32[]{:S(2)}) collective-permute-start(f32[1312,128]{1,0:T(8,128)} %get-tuple-element.20), channel_id=1, source_target_pairs={{0,64},{32,96},{64,0},{96,32},{1,65},{33,97},{65,1},{97,33},{2,66}... | collective-permute-start | bytes 2015240 | tf_op jit(solution)/shard_map/ppermute | solution.py:343
  26.8 32.9 %collective-permute-start.2 = (f32[1312,128]{1,0:T(8,128)}, f32[1312,128]{1,0:T(8,128)S(1)}, u32[]{:S(2)}, u32[]{:S(2)}) collective-permute-start(f32[1312,128]{1,0:T(8,128)} %get-tuple-element.21), channel_id=1, source_target_pairs={{0,96},{32,0},{64,32},{96,64},{1,97},{33,1},{65,33},{97,65},{2,98}... | collective-permute-start | bytes 2015240 | tf_op jit(solution)/shard_map/ppermute | solution.py:343
  30.7 29.0 %copy-start = (f32[1312,128]{1,0:T(8,128)S(1)}, f32[1312,128]{1,0:T(8,128)}, u32[]{:S(2)}) copy-start(f32[1312,128]{1,0:T(8,128)} %get-tuple-element.18.a_ref) | copy-start | bytes 2015236
  45.2 26.4 %all-to-all-start.2 = ((f32[32,16,128]{2,1,0:T(8,128)}), f32[32,16,128]{2,1,0:T(8,128)S(1)}, u32[]{:S(2)}, u32[]{:S(2)}) async-start(f32[32,16,128]{2,1,0:T(8,128)} %broadcast_in_dim.22), calls=%async_computation.2 | async-start | bytes 524288 | tf_op jit(solution)/shard_map/all_to_all | solution.py:374
  60.5 20.1 %collective-permute-start.3 = (f32[328,128]{1,0:T(8,128)}, f32[328,128]{1,0:T(8,128)S(1)}, u32[]{:S(2)}, u32[]{:S(2)}) collective-permute-start(f32[328,128]{1,0:T(8,128)} %get-tuple-element.23), channel_id=1, source_target_pairs={{0,128},{128,256},{256,384},{384,0},{1,129},{129,257},{257,385},{3... | collective-permute-start | bytes 503816 | tf_op jit(solution)/shard_map/ppermute | solution.py:343
  62.7 17.9 %collective-permute-start.4 = (f32[328,128]{1,0:T(8,128)S(1)}, f32[328,128]{1,0:T(8,128)S(1)}, u32[]{:S(2)}, u32[]{:S(2)}) collective-permute-start(f32[328,128]{1,0:T(8,128)S(1)} %get-tuple-element.24), channel_id=1, source_target_pairs={{0,256},{128,384},{256,0},{384,128},{1,257},{129,385},{257,1},{385... | collective-permute-start | bytes 503816 | tf_op jit(solution)/shard_map/ppermute | solution.py:343
  69.0 13.9 %collective-permute-start.5 = (f32[328,128]{1,0:T(8,128)S(1)}, f32[328,128]{1,0:T(8,128)S(1)}, u32[]{:S(2)}, u32[]{:S(2)}) collective-permute-start(f32[328,128]{1,0:T(8,128)S(1)} %get-tuple-element.25), channel_id=1, source_target_pairs={{0,384},{128,0},{256,128},{384,256},{1,385},{129,1},{257,129},{385... | collective-permute-start | bytes 503816 | tf_op jit(solution)/shard_map/ppermute | solution.py:343

commit v5 on v4

--- a/solution.py
+++ b/solution.py
@@ -13,6 +13,8 @@
 OBS = 192
 PER = 8
 SLOTS = 16
+FAR_N = 16
+SHARE = TEX_W // FAR_N
 PIECE = 328
 F32 = jnp.float32
 VMEM = pl.BlockSpec(memory_space=pltpu.VMEM)
@@ -57,25 +59,7 @@
     return copies
 
 
-def tex_kernel(
-    tex_any, res_any, obs_any, ids_any, pattern_any, out_ref,
-    starts, tex_ref, res_ref, obs_ref, ids_ref, pattern_ref, sems,
-):
-    copies = fetch(
-        (
-            (obs_any, obs_ref),
-            (ids_any, ids_ref),
-            (pattern_any, pattern_ref),
-            (res_any, res_ref),
-            (tex_any, tex_ref),
-        ),
-        sems,
-    )
-    for copy in copies[:4]:
-        copy.wait()
-    find_starts(obs_ref, starts)
-    for copy in copies[4:]:
-        copy.wait()
+def tex_sums(tex_ref, res_ref, ids_ref, pattern_ref, starts, out_ref):
     obs_index = iota((OBS, BLOCK), 0)
     masks = []
     for bit in range(2):
@@ -91,12 +75,13 @@
     row, col = iota((BLOCK, BLOCK), 0), iota((BLOCK, BLOCK), 1)
     mixed = jnp.where(row >= col, h00, h11)
     diag = jnp.sum(jnp.where(row == col, h11, 0.0), axis=0, keepdims=True)
-    out_ref[:, 8:, :] = jnp.zeros((32, 8, BLOCK), F32)
-    out_ref[:16, :8, :] = mixed.reshape(16, 8, BLOCK)
-    out_ref[16:, :8, :] = h10.reshape(16, 8, BLOCK)
-    out_ref[0, 8:9, :] = grad[:, :BLOCK]
-    out_ref[1, 8:9, :] = grad[:, BLOCK:]
-    out_ref[2, 8:9, :] = diag
+    half = FAR_N // 2
+    out_ref[:, SHARE:, :] = jnp.zeros((FAR_N, 1, BLOCK), F32)
+    out_ref[:half, :SHARE, :] = mixed.reshape(half, SHARE, BLOCK)
+    out_ref[half:, :SHARE, :] = h10.reshape(half, SHARE, BLOCK)
+    out_ref[0, SHARE:, :] = grad[:, :BLOCK]
+    out_ref[1, SHARE:, :] = grad[:, BLOCK:]
+    out_ref[2, SHARE:, :] = diag
 
 
 def packed(hess):
@@ -107,8 +92,8 @@
     return pair, jnp.sum(jnp.where(row == lane - 64, low, 0.0), axis=0, keepdims=True)
 
 
-def cam_kernel(
-    cam_any, tex_any, res_any, obs_any, ids_any, pattern_any, out0, out1, out2, out3,
+def local_kernel(
+    cam_any, tex_any, res_any, obs_any, ids_any, pattern_any, out0, out1, out2, out3, tex_out,
     starts, cam_ref, tex_ref, res_ref, obs_ref, ids_ref, pattern_ref, sems,
 ):
     outs, my_x, my_yl = (out0, out1, out2, out3), lax.axis_index("x"), lax.axis_index("yl")
@@ -131,6 +116,7 @@
     last = jnp.zeros((SLOTS, BLOCK), jnp.int32)
     for copy in copies[4:]:
         copy.wait()
+    tex_sums(tex_ref, res_ref, ids_ref, pattern_ref, starts, tex_out)
 
     def bounds(k, j):
         slot = ((my_yl + j) & 3) * 4 + ((my_x + k) & 3)
@@ -186,10 +172,14 @@
                 out[base + 321 : base + 322, :] += diag
 
 
-def add_kernel(a_ref, b_ref, c_ref, d_ref, *outs):
+def near_kernel(a_ref, b_ref, c_ref, out_ref):
+    out_ref[...] = (a_ref[...] + b_ref[...]) + c_ref[...]
+
+
+def add_kernel(a_ref, b_ref, *outs):
     for j in range(4):
         rows = slice(j * PIECE, (j + 1) * PIECE)
-        outs[j][...] = (a_ref[rows, :] + b_ref[rows, :]) + (c_ref[rows, :] + d_ref[rows, :])
+        outs[j][...] = a_ref[rows, :] + b_ref[rows, :]
 
 
 def split3(value):
@@ -264,9 +254,9 @@
 def panel_kernel(sums_ref, damping_ref, factor_ref, inv_ref, sol_ref, ab, upper):
     damping = damping_ref[0]
     sums = sums_ref[...]
-    both = sums[:, :8, :].reshape(TEX_W, BLOCK)
+    both = sums[:, :SHARE, :].reshape(TEX_W, BLOCK)
     mixed, h10 = both[:BLOCK], both[BLOCK:]
-    g0, g1, diag = sums[0, 8:9, :], sums[1, 8:9, :], sums[2, 8:9, :]
+    g0, g1, diag = sums[0, SHARE:, :], sums[1, SHARE:, :], sums[2, SHARE:, :]
     row, col = iota((BLOCK, BLOCK), 0), iota((BLOCK, BLOCK), 1)
     flipped = mixed.T
     h00 = jnp.where(row >= col, mixed, flipped)
@@ -313,7 +303,9 @@
     grad_ref[...] = grad - exact_dot(sol_ref[...], coupling, ((1,), (1,)))
 
 
-SMALL_SCRATCH = [
+LOCAL_SCRATCH = [
+    pltpu.SMEM((SLOTS + 1,), jnp.int32),
+    pltpu.VMEM((ROWS, BLOCK), jnp.bfloat16),
     pltpu.VMEM((ROWS, TEX_W), jnp.bfloat16),
     pltpu.VMEM((1, ROWS), jnp.bfloat16),
     pltpu.SMEM((OBS,), jnp.int32),
@@ -321,14 +313,17 @@
     pltpu.SMEM((512,), jnp.int32),
     pltpu.SemaphoreType.DMA((12,)),
 ]
-TEX_SCRATCH = [pltpu.SMEM((SLOTS + 1,), jnp.int32), *SMALL_SCRATCH]
-CAM_SCRATCH = [TEX_SCRATCH[0], pltpu.VMEM((ROWS, BLOCK), jnp.bfloat16), *SMALL_SCRATCH]
+COST = {
+    name: pl.CostEstimate(flops=flops, bytes_accessed=0, transcendentals=0)
+    for name, flops in {"near": 6_000_000_000, "add": 1_000_000_000}.items()
+}
 PANEL = [pltpu.VMEM((BLOCK, TEX_W), F32), pltpu.VMEM((BLOCK, TEX_W), F32)]
 
 
 def call(kernel, name, outs, specs, scratch=(), room=24):
     return pl.pallas_call(
         kernel,
+        cost_estimate=COST.get(name),
         out_shape=[jax.ShapeDtypeStruct(s, F32) for s in outs],
         in_specs=specs,
         out_specs=[VMEM] * len(outs),
@@ -349,8 +344,8 @@
     return jnp.sum(lax.all_to_all(copies, axes, 0, 0), axis=0)
 
 
-FAR = ("x", "z")
-NEAR = ("yl", "yh", "c")
+FAR = ("z", "c")
+NEAR = ("yl", "x", "yh")
 
 
 def shards(jac_cam, jac_tex, residual, obs_slot, col_ids, block_pattern, damping):
@@ -358,19 +353,23 @@
     res, obs = residual[0], obs_slot[0, 0]
     damping = damping.reshape(1)
 
-    (tex_part,) = call(tex_kernel, "tex", [(32, 16, BLOCK)], [HBM] * 5, TEX_SCRATCH, 60)(
-        tex, res, obs, col_ids, block_pattern
-    )
-    pieces = call(cam_kernel, "cam", [(4 * PIECE, BLOCK)] * 4, [HBM] * 6, CAM_SCRATCH, 60)(
-        cam, tex, res, obs, col_ids, block_pattern
-    )
-    moved = [pieces[0]] + [shift(pieces[k], "x", k) for k in (1, 2, 3)]
-    pieces = call(add_kernel, "add", [(PIECE, BLOCK)] * 4, [VMEM] * 4)(*moved)
+    *pieces, tex_part = call(
+        local_kernel,
+        "local",
+        [(4 * PIECE, BLOCK)] * 4 + [(FAR_N, SHARE + 1, BLOCK)],
+        [HBM] * 6,
+        LOCAL_SCRATCH,
+        60,
+    )(cam, tex, res, obs, col_ids, block_pattern)
+    beside = [pieces[0]] + [shift(pieces[k], "x", k) for k in (1, 3)]
+    across = shift(pieces[2], "x", 2)
+    (beside,) = call(near_kernel, "near", [(4 * PIECE, BLOCK)], [VMEM] * 3)(*beside)
+    pieces = call(add_kernel, "add", [(PIECE, BLOCK)] * 4, [VMEM] * 2)(beside, across)
     moved = [pieces[0]] + [shift(pieces[j], "yl", j) for j in (1, 2, 3)]
 
     share = jnp.sum(lax.all_to_all(tex_part, FAR, 0, 0), axis=0)
     share = spread_sum(share, NEAR)
-    copies = jnp.broadcast_to(share[None], (32, *share.shape))
+    copies = jnp.broadcast_to(share[None], (FAR_N, *share.shape))
     tex_sums = lax.all_to_all(copies, FAR, 0, 0)
 
     texture_factor, inverse, sol = call(

time: 85.1 us -> 86.9 us (1.021)
  the two profiles are of different devices: /device:TPU:43 before, /device:TPU:1 now
where the time goes in v5:
time: 86.9 us; the launch traced here: 86.2 us
  starting transfers between devices  47.4 us (55%)
  waiting for transfers between devices  18.6 us (21%)
  Pallas kernels  16.3 us (19%)
  local copies, waits for them, and re-layouts  2.35 us (3%)
  between operations  1.43 us (2%)
    ppermute x6, starting transfers between devices, shift(): return lax.ppermute(value, axis, [(i, (i + by) % n) for i in range(n)])  21.8 us
    all_to_all x1, starting transfers between devices, shards(): share = jnp.sum(lax.all_to_all(tex_part, FAR, 0, 0), axis=0)  12 us
    all_to_all x1, waiting for transfers between devices, spread_sum(): return jnp.sum(lax.all_to_all(copies, axes, 0, 0), axis=0)  11.9 us
    pallas_call x1, Pallas kernels, shards(): call(panel_kernel, 'panel', [(TEX_W, TEX_W), (TEX_W, TEX_W), (1, TEX_W)],...  8.98 us
    all_to_all x1, starting transfers between devices, spread_sum(): return jnp.sum(lax.all_to_all(copies, axes, 0, 0), axis=0)  8.48 us
    all_to_all x1, waiting for transfers between devices, shards(): share = jnp.sum(lax.all_to_all(tex_part, FAR, 0, 0), axis=0)  6.72 us
    pallas_call x1, Pallas kernels, shards(): call(local_kernel, 'local', [(4 * PIECE, BLOCK)] * 4 + [(FAR_N, SHARE + 1...  5.46 us
    all_to_all x1, starting transfers between devices, shards(): tex_sums = lax.all_to_all(copies, FAR, 0, 0)  5.09 us
  transfers between devices with their start and end apart: 9, of which 2 were waited for; matrix products, arithmetic and copies ran while one was open for 2% of the time, Pallas kernels for 11%

profile of v5, /device:TPU:1, one launch (start us, length us, event | category | flops | bytes accessed | tf_op | source)
XLA Modules:
  0.0 86.2 jit_solution(4829162399985335605)
XLA Ops:
  0.6 5.5 %local.1 = (f32[1312,128]{1,0:T(8,128)}, f32[1312,128]{1,0:T(8,128)}, f32[1312,128]{1,0:T(8,128)}, f32[1312,128]{1,0:T(8,128)}, f32[16,17,128]{2,1,0:T(8,128)}) custom-call(bf16[1536,128]{1,0:T(8,128)(2,1)} %bitcast.11, bf16[1536,256]{1,0:T(8,128)(2,1)} %bitcast.10, bf16[1,1536]{1,0:T(2,128)(2,1)} %bitcast.12, s32[192]{0:T(256)} %bitcast.13, s32[16]{0:T(128)} %ids_any.1, ...), custom_call_target="tpu_custom_call" | custom-call | tf_op jit(solution)/shard_map/local/pallas_call | solution.py:356
  6.1 3.9 %collective-permute-start = (f32[1312,128]{1,0:T(8,128)}, f32[1312,128]{1,0:T(8,128)S(1)}, u32[]{:S(2)}, u32[]{:S(2)}) collective-permute-start(f32[1312,128]{1,0:T(8,128)} %get-tuple-element.20), channel_id=1, source_target_pairs={{0,32},{32,64},{64,96},{96,0},{1,33},{33,65},{65,97},{97,1},{2,34}... | collective-permute-start | bytes 2015240 | tf_op jit(solution)/shard_map/ppermute | solution.py:338
  10.0 2.9 %collective-permute-start.1 = (f32[1312,128]{1,0:T(8,128)}, f32[1312,128]{1,0:T(8,128)S(1)}, u32[]{:S(2)}, u32[]{:S(2)}) collective-permute-start(f32[1312,128]{1,0:T(8,128)} %get-tuple-element.21), channel_id=1, source_target_pairs={{0,96},{32,0},{64,32},{96,64},{1,97},{33,1},{65,33},{97,65},{2,98}... | collective-permute-start | bytes 2015240 | tf_op jit(solution)/shard_map/ppermute | solution.py:338
  13.0 12.0 %all-to-all-start = ((f32[16,17,128]{2,1,0:T(8,128)}), f32[16,17,128]{2,1,0:T(8,128)S(1)}, u32[]{:S(2)}, u32[]{:S(2)}) async-start(f32[16,17,128]{2,1,0:T(8,128)} %get-tuple-element.27), calls=%async_computation | async-start | bytes 393216 | tf_op jit(solution)/shard_map/all_to_all | solution.py:370
  25.0 0.0 copy-start
  25.0 3.6 %collective-permute-start.2 = (f32[1312,128]{1,0:T(8,128)}, f32[1312,128]{1,0:T(8,128)S(1)}, u32[]{:S(2)}, u32[]{:S(2)}) collective-permute-start(f32[1312,128]{1,0:T(8,128)} %get-tuple-element.22), channel_id=1, source_target_pairs={{0,64},{32,96},{64,0},{96,32},{1,65},{33,97},{65,1},{97,33},{2,66}... | collective-permute-start | bytes 2015240 | tf_op jit(solution)/shard_map/ppermute | solution.py:338
  28.6 6.7 %all-to-all-done = f32[16,17,128]{2,1,0:T(8,128)S(1)} async-done(((f32[16,17,128]{2,1,0:T(8,128)}), f32[16,17,128]{2,1,0:T(8,128)S(1)}, u32[]{:S(2)}, u32[]{:S(2)}) %all-to-all-start) | async-done | bytes 139296 | tf_op jit(solution)/shard_map/all_to_all | solution.py:370
  35.3 0.8 broadcast_in_dim.10
  36.1 8.5 %all-to-all-start.1 = ((f32[32,17,128]{2,1,0:T(8,128)}), f32[32,17,128]{2,1,0:T(8,128)S(1)}, u32[]{:S(2)}, u32[]{:S(2)}) async-start(f32[32,17,128]{2,1,0:T(8,128)} %broadcast_in_dim.10), calls=%async_computation.1 | async-start | bytes 786432 | tf_op jit(solution)/shard_map/all_to_all | solution.py:344
  44.6 0.0 collective-permute-done.b_ref
  44.6 0.0 collective-permute-done.1.c_ref
  44.6 0.0 copy-done
  44.6 0.1 near.1.a_ref
  44.7 0.0 copy-start.1
  44.8 0.9 copy-done.1
  45.6 11.9 %all-to-all-done.1 = f32[32,17,128]{2,1,0:T(8,128)S(1)} async-done(((f32[32,17,128]{2,1,0:T(8,128)}), f32[32,17,128]{2,1,0:T(8,128)S(1)}, u32[]{:S(2)}, u32[]{:S(2)}) %all-to-all-start.1) | async-done | bytes 278560 | tf_op jit(solution)/shard_map/all_to_all | solution.py:344
  57.5 0.0 copy-start.2
  57.6 0.7 broadcast_in_dim.22
  58.3 5.1 %all-to-all-start.2 = ((f32[16,17,128]{2,1,0:T(8,128)}), f32[16,17,128]{2,1,0:T(8,128)S(1)}, u32[]{:S(2)}, u32[]{:S(2)}) async-start(f32[16,17,128]{2,1,0:T(8,128)} %broadcast_in_dim.22), calls=%async_computation.2 | async-start | bytes 393216 | tf_op jit(solution)/shard_map/all_to_all | solution.py:373
  63.4 0.0 collective-permute-done.2.b_ref
  63.4 0.0 copy-done.2
  63.4 0.1 add.1
  63.4 5.1 %collective-permute-start.3 = (f32[328,128]{1,0:T(8,128)S(1)}, f32[328,128]{1,0:T(8,128)S(1)}, u32[]{:S(2)}, u32[]{:S(2)}) collective-permute-start(f32[328,128]{1,0:T(8,128)S(1)} %get-tuple-element.24), channel_id=1, source_target_pairs={{0,128},{128,256},{256,384},{384,0},{1,129},{129,257},{257,385},{3... | collective-permute-start | bytes 503816 | tf_op jit(solution)/shard_map/ppermute | solution.py:338
  68.5 2.1 %collective-permute-start.4 = (f32[328,128]{1,0:T(8,128)S(1)}, f32[328,128]{1,0:T(8,128)S(1)}, u32[]{:S(2)}, u32[]{:S(2)}) collective-permute-start(f32[328,128]{1,0:T(8,128)S(1)} %get-tuple-element.25), channel_id=1, source_target_pairs={{0,256},{128,384},{256,0},{384,128},{1,257},{129,385},{257,1},{385... | collective-permute-start | bytes 503816 | tf_op jit(solution)/shard_map/ppermute | solution.py:338
  70.6 4.3 %collective-permute-start.5 = (f32[328,128]{1,0:T(8,128)S(1)}, f32[328,128]{1,0:T(8,128)S(1)}, u32[]{:S(2)}, u32[]{:S(2)}) collective-permute-start(f32[328,128]{1,0:T(8,128)S(1)} %get-tuple-element.26), channel_id=1, source_target_pairs={{0,384},{128,0},{256,128},{384,256},{1,385},{129,1},{257,129},{385... | collective-permute-start | bytes 503816 | tf_op jit(solution)/shard_map/ppermute | solution.py:338
  75.5 0.0 all-to-all-done.2.sums_ref
  75.5 9.0 %panel.1 = (f32[256,256]{1,0:T(8,128)}, f32[256,256]{1,0:T(8,128)S(1)}, f32[1,256]{1,0:T(1,128)S(1)}) custom-call(f32[16,17,128]{2,1,0:T(8,128)S(1)} %all-to-all-done.2.sums_ref, f32[1]{0:T(128)} %bitcast.8.damping_ref), custom_call_target="tpu_custom_call" | custom-call | tf_op jit(solution)/shard_map/panel/pallas_call | solution.py:375
  84.5 0.0 collective-permute-done.3.b_ref
  84.5 0.0 collective-permute-done.4.c_ref
  84.5 0.0 collective-permute-done.5.d_ref
  84.5 1.7 %last.1 = (f32[128,128]{1,0:T(8,128)}, f32[1,128]{1,0:T(1,128)}, f32[128,256]{1,0:T(8,128)}) custom-call(f32[328,128]{1,0:T(8,128)S(1)} %get-tuple-element.23.a_ref, f32[328,128]{1,0:T(8,128)S(1)} %collective-permute-done.3.b_ref, f32[328,128]{1,0:T(8,128)S(1)} %collective-permute-done.4.c_ref, f32[328,128]{1,0:T(8,128)S(1)} %collective-permute-done.5.d_ref, ...), custom_call_target="tpu_custom_call" | custom-call | tf_op jit(solution)/shard_map/last/pallas_call | solution.py:378
  (2 shorter events, 0.1 us)
Async XLA Ops:
  6.1 38.5 %collective-permute-start = (f32[1312,128]{1,0:T(8,128)}, f32[1312,128]{1,0:T(8,128)S(1)}, u32[]{:S(2)}, u32[]{:S(2)}) collective-permute-start(f32[1312,128]{1,0:T(8,128)} %get-tuple-element.20), channel_id=1, source_target_pairs={{0,32},{32,64},{64,96},{96,0},{1,33},{33,65},{65,97},{97,1},{2,34}... | collective-permute-start | bytes 2015240 | tf_op jit(solution)/shard_map/ppermute | solution.py:338
  10.0 34.6 %collective-permute-start.1 = (f32[1312,128]{1,0:T(8,128)}, f32[1312,128]{1,0:T(8,128)S(1)}, u32[]{:S(2)}, u32[]{:S(2)}) collective-permute-start(f32[1312,128]{1,0:T(8,128)} %get-tuple-element.21), channel_id=1, source_target_pairs={{0,96},{32,0},{64,32},{96,64},{1,97},{33,1},{65,33},{97,65},{2,98}... | collective-permute-start | bytes 2015240 | tf_op jit(solution)/shard_map/ppermute | solution.py:338
  13.0 22.3 %all-to-all-start = ((f32[16,17,128]{2,1,0:T(8,128)}), f32[16,17,128]{2,1,0:T(8,128)S(1)}, u32[]{:S(2)}, u32[]{:S(2)}) async-start(f32[16,17,128]{2,1,0:T(8,128)} %get-tuple-element.27), calls=%async_computation | async-start | bytes 393216 | tf_op jit(solution)/shard_map/all_to_all | solution.py:370
  25.0 19.6 %copy-start = (f32[1312,128]{1,0:T(8,128)S(1)}, f32[1312,128]{1,0:T(8,128)}, u32[]{:S(2)}) copy-start(f32[1312,128]{1,0:T(8,128)} %get-tuple-element.19.a_ref) | copy-start | bytes 2015236
  25.0 38.4 %collective-permute-start.2 = (f32[1312,128]{1,0:T(8,128)}, f32[1312,128]{1,0:T(8,128)S(1)}, u32[]{:S(2)}, u32[]{:S(2)}) collective-permute-start(f32[1312,128]{1,0:T(8,128)} %get-tuple-element.22), channel_id=1, source_target_pairs={{0,64},{32,96},{64,0},{96,32},{1,65},{33,97},{65,1},{97,33},{2,66}... | collective-permute-start | bytes 2015240 | tf_op jit(solution)/shard_map/ppermute | solution.py:338
  36.1 21.4 %all-to-all-start.1 = ((f32[32,17,128]{2,1,0:T(8,128)}), f32[32,17,128]{2,1,0:T(8,128)S(1)}, u32[]{:S(2)}, u32[]{:S(2)}) async-start(f32[32,17,128]{2,1,0:T(8,128)} %broadcast_in_dim.10), calls=%async_computation.1 | async-start | bytes 786432 | tf_op jit(solution)/shard_map/all_to_all | solution.py:344
  44.7 0.9 %copy-start.1 = (f32[1312,128]{1,0:T(8,128)}, f32[1312,128]{1,0:T(8,128)S(1)}, u32[]{:S(2)}) copy-start(f32[1312,128]{1,0:T(8,128)S(1)} %near.1.a_ref) | copy-start | bytes 2015236
  57.5 5.8 %copy-start.2 = (f32[1312,128]{1,0:T(8,128)S(1)}, f32[1312,128]{1,0:T(8,128)}, u32[]{:S(2)}) copy-start(f32[1312,128]{1,0:T(8,128)} %copy-done.1) | copy-start | bytes 2015236
  58.3 17.2 %all-to-all-start.2 = ((f32[16,17,128]{2,1,0:T(8,128)}), f32[16,17,128]{2,1,0:T(8,128)S(1)}, u32[]{:S(2)}, u32[]{:S(2)}) async-start(f32[16,17,128]{2,1,0:T(8,128)} %broadcast_in_dim.22), calls=%async_computation.2 | async-start | bytes 393216 | tf_op jit(solution)/shard_map/all_to_all | solution.py:373
  63.4 21.1 %collective-permute-start.3 = (f32[328,128]{1,0:T(8,128)S(1)}, f32[328,128]{1,0:T(8,128)S(1)}, u32[]{:S(2)}, u32[]{:S(2)}) collective-permute-start(f32[328,128]{1,0:T(8,128)S(1)} %get-tuple-element.24), channel_id=1, source_target_pairs={{0,128},{128,256},{256,384},{384,0},{1,129},{129,257},{257,385},{3... | collective-permute-start | bytes 503816 | tf_op jit(solution)/shard_map/ppermute | solution.py:338
  68.5 16.0 %collective-permute-start.4 = (f32[328,128]{1,0:T(8,128)S(1)}, f32[328,128]{1,0:T(8,128)S(1)}, u32[]{:S(2)}, u32[]{:S(2)}) collective-permute-start(f32[328,128]{1,0:T(8,128)S(1)} %get-tuple-element.25), channel_id=1, source_target_pairs={{0,256},{128,384},{256,0},{384,128},{1,257},{129,385},{257,1},{385... | collective-permute-start | bytes 503816 | tf_op jit(solution)/shard_map/ppermute | solution.py:338
  70.6 13.9 %collective-permute-start.5 = (f32[328,128]{1,0:T(8,128)S(1)}, f32[328,128]{1,0:T(8,128)S(1)}, u32[]{:S(2)}, u32[]{:S(2)}) collective-permute-start(f32[328,128]{1,0:T(8,128)S(1)} %get-tuple-element.26), channel_id=1, source_target_pairs={{0,384},{128,0},{256,128},{384,256},{1,385},{129,1},{257,129},{385... | collective-permute-start | bytes 503816 | tf_op jit(solution)/shard_map/ppermute | solution.py:338

commit v6 on v5

--- a/solution.py
+++ b/solution.py
@@ -13,7 +13,7 @@
 OBS = 192
 PER = 8
 SLOTS = 16
-FAR_N = 16
+FAR_N = 32
 SHARE = TEX_W // FAR_N
 PIECE = 328
 F32 = jnp.float32
@@ -76,12 +76,12 @@
     mixed = jnp.where(row >= col, h00, h11)
     diag = jnp.sum(jnp.where(row == col, h11, 0.0), axis=0, keepdims=True)
     half = FAR_N // 2
-    out_ref[:, SHARE:, :] = jnp.zeros((FAR_N, 1, BLOCK), F32)
+    out_ref[:, SHARE:, :] = jnp.zeros((FAR_N, SHARE, BLOCK), F32)
     out_ref[:half, :SHARE, :] = mixed.reshape(half, SHARE, BLOCK)
     out_ref[half:, :SHARE, :] = h10.reshape(half, SHARE, BLOCK)
-    out_ref[0, SHARE:, :] = grad[:, :BLOCK]
-    out_ref[1, SHARE:, :] = grad[:, BLOCK:]
-    out_ref[2, SHARE:, :] = diag
+    out_ref[0, SHARE : SHARE + 1, :] = grad[:, :BLOCK]
+    out_ref[1, SHARE : SHARE + 1, :] = grad[:, BLOCK:]
+    out_ref[2, SHARE : SHARE + 1, :] = diag
 
 
 def packed(hess):
@@ -256,7 +256,7 @@
     sums = sums_ref[...]
     both = sums[:, :SHARE, :].reshape(TEX_W, BLOCK)
     mixed, h10 = both[:BLOCK], both[BLOCK:]
-    g0, g1, diag = sums[0, SHARE:, :], sums[1, SHARE:, :], sums[2, SHARE:, :]
+    g0, g1, diag = sums[0, SHARE : SHARE + 1, :], sums[1, SHARE : SHARE + 1, :], sums[2, SHARE : SHARE + 1, :]
     row, col = iota((BLOCK, BLOCK), 0), iota((BLOCK, BLOCK), 1)
     flipped = mixed.T
     h00 = jnp.where(row >= col, mixed, flipped)
@@ -344,8 +344,8 @@
     return jnp.sum(lax.all_to_all(copies, axes, 0, 0), axis=0)
 
 
-FAR = ("z", "c")
-NEAR = ("yl", "x", "yh")
+FAR = ("x", "z")
+NEAR = ("yl", "yh", "c")
 
 
 def shards(jac_cam, jac_tex, residual, obs_slot, col_ids, block_pattern, damping):
@@ -356,7 +356,7 @@
     *pieces, tex_part = call(
         local_kernel,
         "local",
-        [(4 * PIECE, BLOCK)] * 4 + [(FAR_N, SHARE + 1, BLOCK)],
+        [(4 * PIECE, BLOCK)] * 4 + [(FAR_N, 2 * SHARE, BLOCK)],
         [HBM] * 6,
         LOCAL_SCRATCH,
         60,

time: 86.9 us -> 85.6 us (0.985)
  waiting for transfers between devices: 18.6 us -> 15.7 us
  starting transfers between devices: 47.4 us -> 49.3 us
  local copies, waits for them, and re-layouts: 2.35 us -> 1.39 us
    ppermute x6, waiting for transfers between devices: 0.02 us -> 6.64 us  [shift(): return lax.ppermute(value, axis, [(i, (i + by) % n) for i in range(n)])]
    all_to_all x1, waiting for transfers between devices: 11.9 us -> 5.91 us  [spread_sum(): return jnp.sum(lax.all_to_all(copies, axes, 0, 0), axis=0)]
    all_to_all x1, waiting for transfers between devices: 6.72 us -> 3.19 us  [shards(): share = jnp.sum(lax.all_to_all(tex_part, FAR, 0, 0), axis=0)]
    all_to_all x1, starting transfers between devices: 8.48 us -> 10.4 us  [spread_sum(): return jnp.sum(lax.all_to_all(copies, axes, 0, 0), axis=0)]
    all_to_all x1, starting transfers between devices: 12 us -> 13.7 us  [shards(): share = jnp.sum(lax.all_to_all(tex_part, FAR, 0, 0), axis=0)]
    ppermute x6, starting transfers between devices: 21.8 us -> 20.8 us  [shift(): return lax.ppermute(value, axis, [(i, (i + by) % n) for i in range(n)])]
  transfers between devices with their start and end apart: 9 -> 9, of which waited for: 2 -> 3; matrix products, arithmetic and copies ran while one was open for 2% -> 2% of each run, Pallas kernels for 11% -> 11%
where the time goes in v6:
time: 85.6 us; the launch traced here: 84.2 us
  starting transfers between devices  49.3 us (58%)
  Pallas kernels  16.3 us (19%)
  waiting for transfers between devices  15.7 us (18%)
  between operations  1.42 us (2%)
  local copies, waits for them, and re-layouts  1.39 us (2%)
    ppermute x6, starting transfers between devices, shift(): return lax.ppermute(value, axis, [(i, (i + by) % n) for i in range(n)])  20.8 us
    all_to_all x1, starting transfers between devices, shards(): share = jnp.sum(lax.all_to_all(tex_part, FAR, 0, 0), axis=0)  13.7 us
    all_to_all x1, starting transfers between devices, spread_sum(): return jnp.sum(lax.all_to_all(copies, axes, 0, 0), axis=0)  10.4 us
    pallas_call x1, Pallas kernels, shards(): call(panel_kernel, 'panel', [(TEX_W, TEX_W), (TEX_W, TEX_W), (1, TEX_W)],...  8.98 us
    ppermute x6, waiting for transfers between devices, shift(): return lax.ppermute(value, axis, [(i, (i + by) % n) for i in range(n)])  6.64 us
    all_to_all x1, waiting for transfers between devices, spread_sum(): return jnp.sum(lax.all_to_all(copies, axes, 0, 0), axis=0)  5.91 us
    pallas_call x1, Pallas kernels, shards(): call(local_kernel, 'local', [(4 * PIECE, BLOCK)] * 4 + [(FAR_N, 2 * SHARE...  5.46 us
    all_to_all x1, starting transfers between devices, shards(): tex_sums = lax.all_to_all(copies, FAR, 0, 0)  4.27 us
  transfers between devices with their start and end apart: 9, of which 3 were waited for; matrix products, arithmetic and copies ran while one was open for 2% of the time, Pallas kernels for 11%

profile of v6, /device:TPU:1, one launch (start us, length us, event | category | flops | bytes accessed | tf_op | source)
XLA Modules:
  0.0 84.2 jit_solution(11007199243175099654)
XLA Ops:
  0.6 5.5 %local.1 = (f32[1312,128]{1,0:T(8,128)}, f32[1312,128]{1,0:T(8,128)}, f32[1312,128]{1,0:T(8,128)}, f32[1312,128]{1,0:T(8,128)}, f32[32,16,128]{2,1,0:T(8,128)}) custom-call(bf16[1536,128]{1,0:T(8,128)(2,1)} %bitcast.11, bf16[1536,256]{1,0:T(8,128)(2,1)} %bitcast.10, bf16[1,1536]{1,0:T(2,128)(2,1)} %bitcast.12, s32[192]{0:T(256)} %bitcast.13, s32[16]{0:T(128)} %ids_any.1, ...), custom_call_target="tpu_custom_call" | custom-call | tf_op jit(solution)/shard_map/local/pallas_call | solution.py:356
  6.1 13.7 %all-to-all-start = ((f32[32,16,128]{2,1,0:T(8,128)}), f32[32,16,128]{2,1,0:T(8,128)S(1)}, u32[]{:S(2)}, u32[]{:S(2)}) async-start(f32[32,16,128]{2,1,0:T(8,128)} %get-tuple-element.27), calls=%async_computation | async-start | bytes 524288 | tf_op jit(solution)/shard_map/all_to_all | solution.py:370
  19.9 3.1 %collective-permute-start = (f32[1312,128]{1,0:T(8,128)}, f32[1312,128]{1,0:T(8,128)S(1)}, u32[]{:S(2)}, u32[]{:S(2)}) collective-permute-start(f32[1312,128]{1,0:T(8,128)} %get-tuple-element.20), channel_id=1, source_target_pairs={{0,32},{32,64},{64,96},{96,0},{1,33},{33,65},{65,97},{97,1},{2,34}... | collective-permute-start | bytes 2015240 | tf_op jit(solution)/shard_map/ppermute | solution.py:338
  23.0 3.4 %collective-permute-start.1 = (f32[1312,128]{1,0:T(8,128)}, f32[1312,128]{1,0:T(8,128)S(1)}, u32[]{:S(2)}, u32[]{:S(2)}) collective-permute-start(f32[1312,128]{1,0:T(8,128)} %get-tuple-element.21), channel_id=1, source_target_pairs={{0,96},{32,0},{64,32},{96,64},{1,97},{33,1},{65,33},{97,65},{2,98}... | collective-permute-start | bytes 2015240 | tf_op jit(solution)/shard_map/ppermute | solution.py:338
  26.4 3.2 %all-to-all-done = f32[32,16,128]{2,1,0:T(8,128)S(1)} async-done(((f32[32,16,128]{2,1,0:T(8,128)}), f32[32,16,128]{2,1,0:T(8,128)S(1)}, u32[]{:S(2)}, u32[]{:S(2)}) %all-to-all-start) | async-done | bytes 262176 | tf_op jit(solution)/shard_map/all_to_all | solution.py:370
  29.6 0.0 copy-start
  29.6 0.7 broadcast_in_dim.10
  30.3 10.4 %all-to-all-start.1 = ((f32[16,16,128]{2,1,0:T(8,128)}), f32[16,16,128]{2,1,0:T(8,128)S(1)}, u32[]{:S(2)}, u32[]{:S(2)}) async-start(f32[16,16,128]{2,1,0:T(8,128)} %broadcast_in_dim.10), calls=%async_computation.1 | async-start | bytes 262144 | tf_op jit(solution)/shard_map/all_to_all | solution.py:344
  40.7 3.1 %collective-permute-start.2 = (f32[1312,128]{1,0:T(8,128)}, f32[1312,128]{1,0:T(8,128)S(1)}, u32[]{:S(2)}, u32[]{:S(2)}) collective-permute-start(f32[1312,128]{1,0:T(8,128)} %get-tuple-element.22), channel_id=1, source_target_pairs={{0,64},{32,96},{64,0},{96,32},{1,65},{33,97},{65,1},{97,33},{2,66}... | collective-permute-start | bytes 2015240 | tf_op jit(solution)/shard_map/ppermute | solution.py:338
  43.8 5.9 %all-to-all-done.1 = f32[16,16,128]{2,1,0:T(8,128)S(1)} async-done(((f32[16,16,128]{2,1,0:T(8,128)}), f32[16,16,128]{2,1,0:T(8,128)S(1)}, u32[]{:S(2)}, u32[]{:S(2)}) %all-to-all-start.1) | async-done | bytes 131104 | tf_op jit(solution)/shard_map/all_to_all | solution.py:344
  49.8 0.7 broadcast_in_dim.22
  50.5 4.3 %all-to-all-start.2 = ((f32[32,16,128]{2,1,0:T(8,128)}), f32[32,16,128]{2,1,0:T(8,128)S(1)}, u32[]{:S(2)}, u32[]{:S(2)}) async-start(f32[32,16,128]{2,1,0:T(8,128)} %broadcast_in_dim.22), calls=%async_computation.2 | async-start | bytes 524288 | tf_op jit(solution)/shard_map/all_to_all | solution.py:373
  54.8 0.0 collective-permute-done.b_ref
  54.8 0.0 collective-permute-done.1.c_ref
  54.8 0.0 copy-done
  54.8 0.1 near.1.a_ref
  54.9 6.6 %collective-permute-done.2.b_ref = f32[1312,128]{1,0:T(8,128)S(1)} collective-permute-done((f32[1312,128]{1,0:T(8,128)}, f32[1312,128]{1,0:T(8,128)S(1)}, u32[]{:S(2)}, u32[]{:S(2)}) %collective-permute-start.2) | collective-permute-done | bytes 671776 | tf_op jit(solution)/shard_map/ppermute | solution.py:338
  61.5 0.1 add.1
  61.6 2.9 %collective-permute-start.3 = (f32[328,128]{1,0:T(8,128)S(1)}, f32[328,128]{1,0:T(8,128)S(1)}, u32[]{:S(2)}, u32[]{:S(2)}) collective-permute-start(f32[328,128]{1,0:T(8,128)S(1)} %get-tuple-element.24), channel_id=1, source_target_pairs={{0,128},{128,256},{256,384},{384,0},{1,129},{129,257},{257,385},{3... | collective-permute-start | bytes 503816 | tf_op jit(solution)/shard_map/ppermute | solution.py:338
  64.6 5.5 %collective-permute-start.4 = (f32[328,128]{1,0:T(8,128)S(1)}, f32[328,128]{1,0:T(8,128)S(1)}, u32[]{:S(2)}, u32[]{:S(2)}) collective-permute-start(f32[328,128]{1,0:T(8,128)S(1)} %get-tuple-element.25), channel_id=1, source_target_pairs={{0,256},{128,384},{256,0},{384,128},{1,257},{129,385},{257,1},{385... | collective-permute-start | bytes 503816 | tf_op jit(solution)/shard_map/ppermute | solution.py:338
  70.0 2.8 %collective-permute-start.5 = (f32[328,128]{1,0:T(8,128)S(1)}, f32[328,128]{1,0:T(8,128)S(1)}, u32[]{:S(2)}, u32[]{:S(2)}) collective-permute-start(f32[328,128]{1,0:T(8,128)S(1)} %get-tuple-element.26), channel_id=1, source_target_pairs={{0,384},{128,0},{256,128},{384,256},{1,385},{129,1},{257,129},{385... | collective-permute-start | bytes 503816 | tf_op jit(solution)/shard_map/ppermute | solution.py:338
  73.5 0.0 all-to-all-done.2.sums_ref
  73.5 9.0 %panel.1 = (f32[256,256]{1,0:T(8,128)}, f32[256,256]{1,0:T(8,128)S(1)}, f32[1,256]{1,0:T(1,128)S(1)}) custom-call(f32[32,16,128]{2,1,0:T(8,128)S(1)} %all-to-all-done.2.sums_ref, f32[1]{0:T(128)} %bitcast.8.damping_ref), custom_call_target="tpu_custom_call" | custom-call | tf_op jit(solution)/shard_map/panel/pallas_call | solution.py:375
  82.5 0.0 collective-permute-done.3.b_ref
  82.5 0.0 collective-permute-done.4.c_ref
  82.5 0.0 collective-permute-done.5.d_ref
  82.5 1.7 %last.1 = (f32[128,128]{1,0:T(8,128)}, f32[1,128]{1,0:T(1,128)}, f32[128,256]{1,0:T(8,128)}) custom-call(f32[328,128]{1,0:T(8,128)S(1)} %get-tuple-element.23.a_ref, f32[328,128]{1,0:T(8,128)S(1)} %collective-permute-done.3.b_ref, f32[328,128]{1,0:T(8,128)S(1)} %collective-permute-done.4.c_ref, f32[328,128]{1,0:T(8,128)S(1)} %collective-permute-done.5.d_ref, ...), custom_call_target="tpu_custom_call" | custom-call | tf_op jit(solution)/shard_map/last/pallas_call | solution.py:378
  (2 shorter events, 0.1 us)
Async XLA Ops:
  6.1 23.4 %all-to-all-start = ((f32[32,16,128]{2,1,0:T(8,128)}), f32[32,16,128]{2,1,0:T(8,128)S(1)}, u32[]{:S(2)}, u32[]{:S(2)}) async-start(f32[32,16,128]{2,1,0:T(8,128)} %get-tuple-element.27), calls=%async_computation | async-start | bytes 524288 | tf_op jit(solution)/shard_map/all_to_all | solution.py:370
  19.9 34.9 %collective-permute-start = (f32[1312,128]{1,0:T(8,128)}, f32[1312,128]{1,0:T(8,128)S(1)}, u32[]{:S(2)}, u32[]{:S(2)}) collective-permute-start(f32[1312,128]{1,0:T(8,128)} %get-tuple-element.20), channel_id=1, source_target_pairs={{0,32},{32,64},{64,96},{96,0},{1,33},{33,65},{65,97},{97,1},{2,34}... | collective-permute-start | bytes 2015240 | tf_op jit(solution)/shard_map/ppermute | solution.py:338
  23.0 31.8 %collective-permute-start.1 = (f32[1312,128]{1,0:T(8,128)}, f32[1312,128]{1,0:T(8,128)S(1)}, u32[]{:S(2)}, u32[]{:S(2)}) collective-permute-start(f32[1312,128]{1,0:T(8,128)} %get-tuple-element.21), channel_id=1, source_target_pairs={{0,96},{32,0},{64,32},{96,64},{1,97},{33,1},{65,33},{97,65},{2,98}... | collective-permute-start | bytes 2015240 | tf_op jit(solution)/shard_map/ppermute | solution.py:338
  29.6 25.2 %copy-start = (f32[1312,128]{1,0:T(8,128)S(1)}, f32[1312,128]{1,0:T(8,128)}, u32[]{:S(2)}) copy-start(f32[1312,128]{1,0:T(8,128)} %get-tuple-element.19.a_ref) | copy-start | bytes 2015236
  30.3 19.5 %all-to-all-start.1 = ((f32[16,16,128]{2,1,0:T(8,128)}), f32[16,16,128]{2,1,0:T(8,128)S(1)}, u32[]{:S(2)}, u32[]{:S(2)}) async-start(f32[16,16,128]{2,1,0:T(8,128)} %broadcast_in_dim.10), calls=%async_computation.1 | async-start | bytes 262144 | tf_op jit(solution)/shard_map/all_to_all | solution.py:344
  40.7 20.8 %collective-permute-start.2 = (f32[1312,128]{1,0:T(8,128)}, f32[1312,128]{1,0:T(8,128)S(1)}, u32[]{:S(2)}, u32[]{:S(2)}) collective-permute-start(f32[1312,128]{1,0:T(8,128)} %get-tuple-element.22), channel_id=1, source_target_pairs={{0,64},{32,96},{64,0},{96,32},{1,65},{33,97},{65,1},{97,33},{2,66}... | collective-permute-start | bytes 2015240 | tf_op jit(solution)/shard_map/ppermute | solution.py:338
  50.5 23.0 %all-to-all-start.2 = ((f32[32,16,128]{2,1,0:T(8,128)}), f32[32,16,128]{2,1,0:T(8,128)S(1)}, u32[]{:S(2)}, u32[]{:S(2)}) async-start(f32[32,16,128]{2,1,0:T(8,128)} %broadcast_in_dim.22), calls=%async_computation.2 | async-start | bytes 524288 | tf_op jit(solution)/shard_map/all_to_all | solution.py:373
  61.6 20.9 %collective-permute-start.3 = (f32[328,128]{1,0:T(8,128)S(1)}, f32[328,128]{1,0:T(8,128)S(1)}, u32[]{:S(2)}, u32[]{:S(2)}) collective-permute-start(f32[328,128]{1,0:T(8,128)S(1)} %get-tuple-element.24), channel_id=1, source_target_pairs={{0,128},{128,256},{256,384},{384,0},{1,129},{129,257},{257,385},{3... | collective-permute-start | bytes 503816 | tf_op jit(solution)/shard_map/ppermute | solution.py:338
  64.6 17.9 %collective-permute-start.4 = (f32[328,128]{1,0:T(8,128)S(1)}, f32[328,128]{1,0:T(8,128)S(1)}, u32[]{:S(2)}, u32[]{:S(2)}) collective-permute-start(f32[328,128]{1,0:T(8,128)S(1)} %get-tuple-element.25), channel_id=1, source_target_pairs={{0,256},{128,384},{256,0},{384,128},{1,257},{129,385},{257,1},{385... | collective-permute-start | bytes 503816 | tf_op jit(solution)/shard_map/ppermute | solution.py:338
  70.0 12.4 %collective-permute-start.5 = (f32[328,128]{1,0:T(8,128)S(1)}, f32[328,128]{1,0:T(8,128)S(1)}, u32[]{:S(2)}, u32[]{:S(2)}) collective-permute-start(f32[328,128]{1,0:T(8,128)S(1)} %get-tuple-element.26), channel_id=1, source_target_pairs={{0,384},{128,0},{256,128},{384,256},{1,385},{129,1},{257,129},{385... | collective-permute-start | bytes 503816 | tf_op jit(solution)/shard_map/ppermute | solution.py:338

commit v7 on v6

--- a/solution.py
+++ b/solution.py
@@ -15,7 +15,7 @@
 SLOTS = 16
 FAR_N = 32
 SHARE = TEX_W // FAR_N
-PIECE = 328
+BODY = 320
 F32 = jnp.float32
 VMEM = pl.BlockSpec(memory_space=pltpu.VMEM)
 HBM = pl.BlockSpec(memory_space=pltpu.HBM)
@@ -24,12 +24,6 @@
 
 def col_dot(left, right):
     return lax.dot_general(left, right, (((0,), (0,)), ((), ())), preferred_element_type=F32)
-
-
-def exact_dot(left, right, dims=((1,), (0,))):
-    return lax.dot_general(
-        left, right, (dims, ((), ())), precision=lax.Precision.HIGHEST, preferred_element_type=F32
-    )
 
 
 def iota(shape, dim):
@@ -76,7 +70,7 @@
     mixed = jnp.where(row >= col, h00, h11)
     diag = jnp.sum(jnp.where(row == col, h11, 0.0), axis=0, keepdims=True)
     half = FAR_N // 2
-    out_ref[:, SHARE:, :] = jnp.zeros((FAR_N, SHARE, BLOCK), F32)
+    out_ref[:, SHARE:, :] = jnp.zeros((FAR_N, 8, BLOCK), F32)
     out_ref[:half, :SHARE, :] = mixed.reshape(half, SHARE, BLOCK)
     out_ref[half:, :SHARE, :] = h10.reshape(half, SHARE, BLOCK)
     out_ref[0, SHARE : SHARE + 1, :] = grad[:, :BLOCK]
@@ -135,7 +129,7 @@
     zero = jnp.zeros((BLOCK, BLOCK), F32)
     for k in range(4):
         for j in range(4):
-            out, base = outs[k], j * PIECE
+            out, base, tail = outs[k], j * BODY, 4 * BODY + 2 * j
             lo, hi, begin, keep0, keep1 = bounds(k, j)
             first = jnp.where(sub == k * 4 + j, lo, first)
             last = jnp.where(sub == k * 4 + j, hi, last)
@@ -144,7 +138,7 @@
             out[base : base + 128, :] = jnp.where(keep0, sums[:, BLOCK : 2 * BLOCK], zero)
             out[base + 128 : base + 256, :] = jnp.where(keep1, sums[:, 2 * BLOCK :], zero)
             out[base + 256 : base + 320, :] = pair
-            out[base + 320 : base + 328, :] = jnp.broadcast_to(diag, (8, BLOCK))
+            out[tail + 1 : tail + 2, :] = diag
 
     lane = iota((SLOTS, ROWS), 1)
     first = jnp.tile(first, (1, ROWS // BLOCK))
@@ -153,12 +147,12 @@
     spread = jnp.where((lane >= first) & (lane < last), res, 0.0).astype(jnp.bfloat16)
     grad = jnp.dot(spread, cam_ref[...], preferred_element_type=F32)
     for i in range(SLOTS):
-        base = (i % 4) * PIECE
-        outs[i // 4][base + 320 : base + 321, :] = grad[i : i + 1, :]
+        tail = 4 * BODY + 2 * (i % 4)
+        outs[i // 4][tail : tail + 1, :] = grad[i : i + 1, :]
 
     for k in range(4):
         for j in range(4):
-            out, base = outs[k], j * PIECE
+            out, base, tail = outs[k], j * BODY, 4 * BODY + 2 * j
             lo, hi, begin, keep0, keep1 = bounds(k, j)
 
             @pl.when(hi > begin + 256)
@@ -169,17 +163,17 @@
                 out[base : base + 128, :] += jnp.where(keep0, sums[:, BLOCK : 2 * BLOCK], zero)
                 out[base + 128 : base + 256, :] += jnp.where(keep1, sums[:, 2 * BLOCK :], zero)
                 out[base + 256 : base + 320, :] += pair
-                out[base + 321 : base + 322, :] += diag
-
-
-def near_kernel(a_ref, b_ref, c_ref, out_ref):
-    out_ref[...] = (a_ref[...] + b_ref[...]) + c_ref[...]
-
-
-def add_kernel(a_ref, b_ref, *outs):
+                out[tail + 1 : tail + 2, :] += diag
+
+
+def add_kernel(a_ref, b_ref, c_ref, d_ref, *outs):
     for j in range(4):
-        rows = slice(j * PIECE, (j + 1) * PIECE)
-        outs[j][...] = a_ref[rows, :] + b_ref[rows, :]
+        for rows, put in (
+            (slice(j * BODY, (j + 1) * BODY), slice(0, BODY)),
+            (slice(4 * BODY + 2 * j, 4 * BODY + 2 * j + 2), slice(BODY, BODY + 2)),
+        ):
+            outs[j][put, :] = (a_ref[rows, :] + b_ref[rows, :]) + (c_ref[rows, :] + d_ref[rows, :])
+        outs[j][BODY + 2 :, :] = jnp.zeros((6, BLOCK), F32)
 
 
 def split3(value):
@@ -297,10 +291,10 @@
     lower = jnp.where(row > col, lower, 0.0)
     main = jnp.where(row == col, jnp.where(row < 64, square, diag), 0.0)
     hess = lower + lower.T + main + damping * main
-    coupling = exact_dot(cross, inv_ref[...], ((1,), (1,)))
+    coupling = near_dot(cross, inv_ref[...], ((1,), (1,)))
     coup_ref[...] = coupling
-    red_ref[...] = hess - exact_dot(coupling, coupling, ((1,), (1,)))
-    grad_ref[...] = grad - exact_dot(sol_ref[...], coupling, ((1,), (1,)))
+    red_ref[...] = hess - near_dot(coupling, coupling, ((1,), (1,)))
+    grad_ref[...] = grad - near_dot(sol_ref[...], coupling, ((1,), (1,)))
 
 
 LOCAL_SCRATCH = [
@@ -313,10 +307,7 @@
     pltpu.SMEM((512,), jnp.int32),
     pltpu.SemaphoreType.DMA((12,)),
 ]
-COST = {
-    name: pl.CostEstimate(flops=flops, bytes_accessed=0, transcendentals=0)
-    for name, flops in {"near": 6_000_000_000, "add": 1_000_000_000}.items()
-}
+COST = {}
 PANEL = [pltpu.VMEM((BLOCK, TEX_W), F32), pltpu.VMEM((BLOCK, TEX_W), F32)]
 
 
@@ -356,16 +347,14 @@
     *pieces, tex_part = call(
         local_kernel,
         "local",
-        [(4 * PIECE, BLOCK)] * 4 + [(FAR_N, 2 * SHARE, BLOCK)],
+        [(4 * BODY + 8, BLOCK)] * 4 + [(FAR_N, SHARE + 8, BLOCK)],
         [HBM] * 6,
         LOCAL_SCRATCH,
         60,
     )(cam, tex, res, obs, col_ids, block_pattern)
-    beside = [pieces[0]] + [shift(pieces[k], "x", k) for k in (1, 3)]
-    across = shift(pieces[2], "x", 2)
-    (beside,) = call(near_kernel, "near", [(4 * PIECE, BLOCK)], [VMEM] * 3)(*beside)
-    pieces = call(add_kernel, "add", [(PIECE, BLOCK)] * 4, [VMEM] * 2)(beside, across)
-    moved = [pieces[0]] + [shift(pieces[j], "yl", j) for j in (1, 2, 3)]
+    moved = [pieces[0]] + [shift(pieces[k], "x", k) for k in (2, 1, 3)]
+    pieces = call(add_kernel, "add", [(BODY + 8, BLOCK)] * 4, [VMEM] * 4)(*moved)
+    parts = [pieces[0]] + [shift(pieces[j], "yl", j) for j in (1, 2, 3)]
 
     share = jnp.sum(lax.all_to_all(tex_part, FAR, 0, 0), axis=0)
     share = spread_sum(share, NEAR)
@@ -380,7 +369,7 @@
         "last",
         [(BLOCK, BLOCK), (1, BLOCK), (BLOCK, TEX_W)],
         [VMEM] * 6 + [SMEM],
-    )(*moved, inverse, sol, damping)
+    )(*parts, inverse, sol, damping)
     return (reduced[None, None], gradient[None], coupling[None, None], texture_factor)
 
 

time: 85.6 us -> 79.6 us (0.930)
  blocking collectives: 0 us -> 18.4 us
  waiting for transfers between devices: 15.7 us -> 0.02 us
  starting transfers between devices: 49.3 us -> 41.4 us
    all_to_all x0 -> x1, blocking collectives: none -> 18.4 us  [spread_sum(): return jnp.sum(lax.all_to_all(copies, axes, 0, 0), axis=0)]
    all_to_all x1 -> x0, starting transfers between devices: 10.4 us -> none  [spread_sum(): return jnp.sum(lax.all_to_all(copies, axes, 0, 0), axis=0)]
    ppermute x6, waiting for transfers between devices: 6.64 us -> 0.02 us  [shift(): return lax.ppermute(value, axis, [(i, (i + by) % n) for i in range(n)])]
    all_to_all x1 -> x0, waiting for transfers between devices: 5.91 us -> none  [spread_sum(): return jnp.sum(lax.all_to_all(copies, axes, 0, 0), axis=0)]
    all_to_all x1, waiting for transfers between devices: 3.19 us -> 0.01 us  [shards(): share = jnp.sum(lax.all_to_all(tex_part, FAR, 0, 0), axis=0)]
    all_to_all x1, starting transfers between devices: 4.27 us -> 6.56 us  [shards(): tex_sums = lax.all_to_all(copies, FAR, 0, 0)]
    pallas_call x3 -> x2, Pallas kernels: 5.63 us -> 6.29 us  [the longest x1 5.45 us: shards(): call(local_kernel, 'local', [(4 * BODY + 8, BLOCK)] * 4 + [(FAR_N, SHARE...]
  transfers between devices with their start and end apart: 9 -> 8, of which waited for: 3 -> 0; matrix products, arithmetic and copies ran while one was open for 2% -> 1% of each run, Pallas kernels for 11% -> 13%
where the time goes in v7:
time: 79.6 us; the launch traced here: 78.6 us
  starting transfers between devices  41.4 us (52%)
  blocking collectives  18.4 us (23%)
  Pallas kernels  16.6 us (21%)
  between operations  1.43 us (2%)
    ppermute x6, starting transfers between devices, shift(): return lax.ppermute(value, axis, [(i, (i + by) % n) for i in range(n)])  21.1 us
    all_to_all x1, blocking collectives, spread_sum(): return jnp.sum(lax.all_to_all(copies, axes, 0, 0), axis=0)  18.4 us
    all_to_all x1, starting transfers between devices, shards(): share = jnp.sum(lax.all_to_all(tex_part, FAR, 0, 0), axis=0)  13.7 us
    pallas_call x1, Pallas kernels, shards(): call(panel_kernel, 'panel', [(TEX_W, TEX_W), (TEX_W, TEX_W), (1, TEX_W)],...  8.98 us
    all_to_all x1, starting transfers between devices, shards(): tex_sums = lax.all_to_all(copies, FAR, 0, 0)  6.56 us
    pallas_call x1, Pallas kernels, shards(): call(local_kernel, 'local', [(4 * BODY + 8, BLOCK)] * 4 + [(FAR_N, SHARE...  5.45 us
  transfers between devices with their start and end apart: 8, of which 0 were waited for; matrix products, arithmetic and copies ran while one was open for 1% of the time, Pallas kernels for 13%

profile of v7, /device:TPU:1, one launch (start us, length us, event | category | flops | bytes accessed | tf_op | source)
XLA Modules:
  0.0 78.6 jit_solution(6466298632389248516)
XLA Ops:
  0.6 5.4 %local.1 = (f32[1288,128]{1,0:T(8,128)}, f32[1288,128]{1,0:T(8,128)}, f32[1288,128]{1,0:T(8,128)}, f32[1288,128]{1,0:T(8,128)}, f32[32,16,128]{2,1,0:T(8,128)}) custom-call(bf16[1536,128]{1,0:T(8,128)(2,1)} %bitcast.11, bf16[1536,256]{1,0:T(8,128)(2,1)} %bitcast.10, bf16[1,1536]{1,0:T(2,128)(2,1)} %bitcast.12, s32[192]{0:T(256)} %bitcast.13, s32[16]{0:T(128)} %ids_any.1, ...), custom_call_target="tpu_custom_call" | custom-call | tf_op jit(solution)/shard_map/local/pallas_call | solution.py:347
  6.1 13.7 %all-to-all-start = ((f32[32,16,128]{2,1,0:T(8,128)}), f32[32,16,128]{2,1,0:T(8,128)S(1)}, u32[]{:S(2)}, u32[]{:S(2)}) async-start(f32[32,16,128]{2,1,0:T(8,128)} %get-tuple-element.27), calls=%async_computation | async-start | bytes 524288 | tf_op jit(solution)/shard_map/all_to_all | solution.py:359
  19.8 4.6 %collective-permute-start = (f32[1288,128]{1,0:T(8,128)}, f32[1288,128]{1,0:T(8,128)S(1)}, u32[]{:S(2)}, u32[]{:S(2)}) collective-permute-start(f32[1288,128]{1,0:T(8,128)} %get-tuple-element.20), channel_id=1, source_target_pairs={{0,64},{32,96},{64,0},{96,32},{1,65},{33,97},{65,1},{97,33},{2,66}... | collective-permute-start | bytes 1978376 | tf_op jit(solution)/shard_map/ppermute | solution.py:329
  24.5 2.2 %collective-permute-start.1 = (f32[1288,128]{1,0:T(8,128)}, f32[1288,128]{1,0:T(8,128)S(1)}, u32[]{:S(2)}, u32[]{:S(2)}) collective-permute-start(f32[1288,128]{1,0:T(8,128)} %get-tuple-element.21), channel_id=1, source_target_pairs={{0,32},{32,64},{64,96},{96,0},{1,33},{33,65},{65,97},{97,1},{2,34}... | collective-permute-start | bytes 1978376 | tf_op jit(solution)/shard_map/ppermute | solution.py:329
  26.7 4.3 %collective-permute-start.2 = (f32[1288,128]{1,0:T(8,128)}, f32[1288,128]{1,0:T(8,128)S(1)}, u32[]{:S(2)}, u32[]{:S(2)}) collective-permute-start(f32[1288,128]{1,0:T(8,128)} %get-tuple-element.22), channel_id=1, source_target_pairs={{0,96},{32,0},{64,32},{96,64},{1,97},{33,1},{65,33},{97,65},{2,98}... | collective-permute-start | bytes 1978376 | tf_op jit(solution)/shard_map/ppermute | solution.py:329
  31.0 0.0 all-to-all-done
  31.0 0.0 copy-start
  31.1 18.4 %all_to_all.15 = f32[16,16,128]{2,1,0:T(8,128)S(1)} all-to-all(f32[16,16,128]{2,1,0:T(8,128)S(1)} %broadcast_in_dim.10), channel_id=1, replica_groups=mesh['yl'=4,'x'=4,'yh'=2,'z'=8,'c'=2] {'yl','yh','c'}, dimensions={0} | all-to-all | bytes 262144 | tf_op jit(solution)/shard_map/all_to_all | solution.py:335
  49.5 0.7 broadcast_in_dim.22
  50.2 6.6 %all-to-all-start.2 = ((f32[32,16,128]{2,1,0:T(8,128)}), f32[32,16,128]{2,1,0:T(8,128)S(1)}, u32[]{:S(2)}, u32[]{:S(2)}) async-start(f32[32,16,128]{2,1,0:T(8,128)} %broadcast_in_dim.22), calls=%async_computation.2 | async-start | bytes 524288 | tf_op jit(solution)/shard_map/all_to_all | solution.py:362
  56.8 0.0 collective-permute-done.b_ref
  56.8 0.0 collective-permute-done.1.c_ref
  56.8 0.0 collective-permute-done.2.d_ref
  56.8 0.0 copy-done
  56.8 0.8 %add.1 = (f32[328,128]{1,0:T(8,128)S(1)}, f32[328,128]{1,0:T(8,128)}, f32[328,128]{1,0:T(8,128)S(1)}, f32[328,128]{1,0:T(8,128)S(1)}) custom-call(f32[1288,128]{1,0:T(8,128)S(1)} %copy-done, f32[1288,128]{1,0:T(8,128)S(1)} %collective-permute-done.b_ref, f32[1288,128]{1,0:T(8,128)S(1)} %collective-permute-done.1.c_ref, ...), custom_call_target="tpu_custom_call" | custom-call | tf_op jit(solution)/shard_map/add/pallas_call | solution.py:356
  57.6 2.8 %collective-permute-start.3 = (f32[328,128]{1,0:T(8,128)}, f32[328,128]{1,0:T(8,128)S(1)}, u32[]{:S(2)}, u32[]{:S(2)}) collective-permute-start(f32[328,128]{1,0:T(8,128)} %get-tuple-element.24), channel_id=1, source_target_pairs={{0,128},{128,256},{256,384},{384,0},{1,129},{129,257},{257,385},{3... | collective-permute-start | bytes 503816 | tf_op jit(solution)/shard_map/ppermute | solution.py:329
  60.5 4.3 %collective-permute-start.4 = (f32[328,128]{1,0:T(8,128)S(1)}, f32[328,128]{1,0:T(8,128)S(1)}, u32[]{:S(2)}, u32[]{:S(2)}) collective-permute-start(f32[328,128]{1,0:T(8,128)S(1)} %get-tuple-element.25), channel_id=1, source_target_pairs={{0,256},{128,384},{256,0},{384,128},{1,257},{129,385},{257,1},{385... | collective-permute-start | bytes 503816 | tf_op jit(solution)/shard_map/ppermute | solution.py:329
  64.7 2.9 %collective-permute-start.5 = (f32[328,128]{1,0:T(8,128)S(1)}, f32[328,128]{1,0:T(8,128)S(1)}, u32[]{:S(2)}, u32[]{:S(2)}) collective-permute-start(f32[328,128]{1,0:T(8,128)S(1)} %get-tuple-element.26), channel_id=1, source_target_pairs={{0,384},{128,0},{256,128},{384,256},{1,385},{129,1},{257,129},{385... | collective-permute-start | bytes 503816 | tf_op jit(solution)/shard_map/ppermute | solution.py:329
  68.3 0.0 all-to-all-done.2.sums_ref
  68.3 9.0 %panel.1 = (f32[256,256]{1,0:T(8,128)}, f32[256,256]{1,0:T(8,128)S(1)}, f32[1,256]{1,0:T(1,128)S(1)}) custom-call(f32[32,16,128]{2,1,0:T(8,128)S(1)} %all-to-all-done.2.sums_ref, f32[1]{0:T(128)} %bitcast.8.damping_ref), custom_call_target="tpu_custom_call" | custom-call | tf_op jit(solution)/shard_map/panel/pallas_call | solution.py:364
  77.3 0.0 collective-permute-done.3.b_ref
  77.3 0.0 collective-permute-done.4.c_ref
  77.3 0.0 collective-permute-done.5.d_ref
  77.3 1.3 %last.1 = (f32[128,128]{1,0:T(8,128)}, f32[1,128]{1,0:T(1,128)}, f32[128,256]{1,0:T(8,128)}) custom-call(f32[328,128]{1,0:T(8,128)S(1)} %get-tuple-element.23.a_ref, f32[328,128]{1,0:T(8,128)S(1)} %collective-permute-done.3.b_ref, f32[328,128]{1,0:T(8,128)S(1)} %collective-permute-done.4.c_ref, f32[328,128]{1,0:T(8,128)S(1)} %collective-permute-done.5.d_ref, ...), custom_call_target="tpu_custom_call" | custom-call | tf_op jit(solution)/shard_map/last/pallas_call | solution.py:367
  (3 shorter events, 0.1 us)
Async XLA Ops:
  6.1 24.9 %all-to-all-start = ((f32[32,16,128]{2,1,0:T(8,128)}), f32[32,16,128]{2,1,0:T(8,128)S(1)}, u32[]{:S(2)}, u32[]{:S(2)}) async-start(f32[32,16,128]{2,1,0:T(8,128)} %get-tuple-element.27), calls=%async_computation | async-start | bytes 524288 | tf_op jit(solution)/shard_map/all_to_all | solution.py:359
  19.8 37.0 %collective-permute-start = (f32[1288,128]{1,0:T(8,128)}, f32[1288,128]{1,0:T(8,128)S(1)}, u32[]{:S(2)}, u32[]{:S(2)}) collective-permute-start(f32[1288,128]{1,0:T(8,128)} %get-tuple-element.20), channel_id=1, source_target_pairs={{0,64},{32,96},{64,0},{96,32},{1,65},{33,97},{65,1},{97,33},{2,66}... | collective-permute-start | bytes 1978376 | tf_op jit(solution)/shard_map/ppermute | solution.py:329
  24.5 32.3 %collective-permute-start.1 = (f32[1288,128]{1,0:T(8,128)}, f32[1288,128]{1,0:T(8,128)S(1)}, u32[]{:S(2)}, u32[]{:S(2)}) collective-permute-start(f32[1288,128]{1,0:T(8,128)} %get-tuple-element.21), channel_id=1, source_target_pairs={{0,32},{32,64},{64,96},{96,0},{1,33},{33,65},{65,97},{97,1},{2,34}... | collective-permute-start | bytes 1978376 | tf_op jit(solution)/shard_map/ppermute | solution.py:329
  26.7 30.1 %collective-permute-start.2 = (f32[1288,128]{1,0:T(8,128)}, f32[1288,128]{1,0:T(8,128)S(1)}, u32[]{:S(2)}, u32[]{:S(2)}) collective-permute-start(f32[1288,128]{1,0:T(8,128)} %get-tuple-element.22), channel_id=1, source_target_pairs={{0,96},{32,0},{64,32},{96,64},{1,97},{33,1},{65,33},{97,65},{2,98}... | collective-permute-start | bytes 1978376 | tf_op jit(solution)/shard_map/ppermute | solution.py:329
  31.0 25.8 %copy-start = (f32[1288,128]{1,0:T(8,128)S(1)}, f32[1288,128]{1,0:T(8,128)}, u32[]{:S(2)}) copy-start(f32[1288,128]{1,0:T(8,128)} %get-tuple-element.19.a_ref) | copy-start | bytes 1978372
  50.2 18.1 %all-to-all-start.2 = ((f32[32,16,128]{2,1,0:T(8,128)}), f32[32,16,128]{2,1,0:T(8,128)S(1)}, u32[]{:S(2)}, u32[]{:S(2)}) async-start(f32[32,16,128]{2,1,0:T(8,128)} %broadcast_in_dim.22), calls=%async_computation.2 | async-start | bytes 524288 | tf_op jit(solution)/shard_map/all_to_all | solution.py:362
  57.6 19.7 %collective-permute-start.3 = (f32[328,128]{1,0:T(8,128)}, f32[328,128]{1,0:T(8,128)S(1)}, u32[]{:S(2)}, u32[]{:S(2)}) collective-permute-start(f32[328,128]{1,0:T(8,128)} %get-tuple-element.24), channel_id=1, source_target_pairs={{0,128},{128,256},{256,384},{384,0},{1,129},{129,257},{257,385},{3... | collective-permute-start | bytes 503816 | tf_op jit(solution)/shard_map/ppermute | solution.py:329
  60.5 16.8 %collective-permute-start.4 = (f32[328,128]{1,0:T(8,128)S(1)}, f32[328,128]{1,0:T(8,128)S(1)}, u32[]{:S(2)}, u32[]{:S(2)}) collective-permute-start(f32[328,128]{1,0:T(8,128)S(1)} %get-tuple-element.25), channel_id=1, source_target_pairs={{0,256},{128,384},{256,0},{384,128},{1,257},{129,385},{257,1},{385... | collective-permute-start | bytes 503816 | tf_op jit(solution)/shard_map/ppermute | solution.py:329
  64.7 12.6 %collective-permute-start.5 = (f32[328,128]{1,0:T(8,128)S(1)}, f32[328,128]{1,0:T(8,128)S(1)}, u32[]{:S(2)}, u32[]{:S(2)}) collective-permute-start(f32[328,128]{1,0:T(8,128)S(1)} %get-tuple-element.26), channel_id=1, source_target_pairs={{0,384},{128,0},{256,128},{384,256},{1,385},{129,1},{257,129},{385... | collective-permute-start | bytes 503816 | tf_op jit(solution)/shard_map/ppermute | solution.py:329

commit v8 on v7

--- a/solution.py
+++ b/solution.py
@@ -15,6 +15,7 @@
 SLOTS = 16
 FAR_N = 32
 SHARE = TEX_W // FAR_N
+WINDOW = 304
 BODY = 320
 F32 = jnp.float32
 VMEM = pl.BlockSpec(memory_space=pltpu.VMEM)
@@ -44,9 +45,11 @@
 def fetch(pairs, sems):
     copies = []
     for src, dst in pairs:
-        step = dst.shape[0] // 4 if dst.shape[0] == ROWS else dst.shape[0]
-        for n in range(0, dst.shape[0], step):
-            part = pl.ds(n, step)
+        if dst.shape[0] != ROWS:
+            copies.append(pltpu.make_async_copy(src, dst, sems.at[len(copies)]))
+            continue
+        for n in range(0, ROWS, ROWS // 4):
+            part = pl.ds(n, ROWS // 4)
             copies.append(pltpu.make_async_copy(src.at[part], dst.at[part], sems.at[len(copies)]))
     for copy in copies:
         copy.start()
@@ -88,9 +91,9 @@
 
 def local_kernel(
     cam_any, tex_any, res_any, obs_any, ids_any, pattern_any, out0, out1, out2, out3, tex_out,
-    starts, cam_ref, tex_ref, res_ref, obs_ref, ids_ref, pattern_ref, sems,
+    starts, cam_ref, tex_ref, res_ref, obs_ref, ids_ref, pattern_ref, sems, outs, tex_sums_ref, out_sems,
 ):
-    outs, my_x, my_yl = (out0, out1, out2, out3), lax.axis_index("x"), lax.axis_index("yl")
+    dests, my_x, my_yl = (out0, out1, out2, out3), lax.axis_index("x"), lax.axis_index("yl")
     copies = fetch(
         (
             (obs_any, obs_ref),
@@ -110,12 +113,14 @@
     last = jnp.zeros((SLOTS, BLOCK), jnp.int32)
     for copy in copies[4:]:
         copy.wait()
-    tex_sums(tex_ref, res_ref, ids_ref, pattern_ref, starts, tex_out)
+    tex_sums(tex_ref, res_ref, ids_ref, pattern_ref, starts, tex_sums_ref)
+    leave = [pltpu.make_async_copy(tex_sums_ref, tex_out, out_sems.at[4])]
+    leave[0].start()
 
     def bounds(k, j):
         slot = ((my_yl + j) & 3) * 4 + ((my_x + k) & 3)
         lo, hi = starts[slot] * PER, starts[slot + 1] * PER
-        begin = pl.multiple_of(jnp.minimum((lo >> 4) << 4, ROWS - 256), 16)
+        begin = pl.multiple_of(jnp.minimum((lo >> 4) << 4, ROWS - WINDOW), 16)
         code = pattern_ref[ids_ref[slot]]
         return lo, hi, begin, (code & 1) == 1, (code >> 1) == 1
 
@@ -126,53 +131,45 @@
         keep = ((where >= lo) & (where < hi)).astype(F32).astype(jnp.bfloat16)
         return col_dot(cam * keep, both)
 
-    zero = jnp.zeros((BLOCK, BLOCK), F32)
-    for k in range(4):
-        for j in range(4):
-            out, base, tail = outs[k], j * BODY, 4 * BODY + 2 * j
-            lo, hi, begin, keep0, keep1 = bounds(k, j)
-            first = jnp.where(sub == k * 4 + j, lo, first)
-            last = jnp.where(sub == k * 4 + j, hi, last)
-            sums = part(begin, lo, hi, 256)
-            pair, diag = packed(sums[:, :BLOCK])
-            out[base : base + 128, :] = jnp.where(keep0, sums[:, BLOCK : 2 * BLOCK], zero)
-            out[base + 128 : base + 256, :] = jnp.where(keep1, sums[:, 2 * BLOCK :], zero)
-            out[base + 256 : base + 320, :] = pair
-            out[tail + 1 : tail + 2, :] = diag
-
+    for i in range(SLOTS):
+        lo, hi, *_ = bounds(i // 4, i % 4)
+        first = jnp.where(sub == i, lo, first)
+        last = jnp.where(sub == i, hi, last)
     lane = iota((SLOTS, ROWS), 1)
     first = jnp.tile(first, (1, ROWS // BLOCK))
     last = jnp.tile(last, (1, ROWS // BLOCK))
     res = jnp.broadcast_to(res_ref[...].astype(F32), (SLOTS, ROWS))
     spread = jnp.where((lane >= first) & (lane < last), res, 0.0).astype(jnp.bfloat16)
     grad = jnp.dot(spread, cam_ref[...], preferred_element_type=F32)
-    for i in range(SLOTS):
-        tail = 4 * BODY + 2 * (i % 4)
-        outs[i // 4][tail : tail + 1, :] = grad[i : i + 1, :]
-
-    for k in range(4):
+    zero = jnp.zeros((BLOCK, BLOCK), F32)
+    for k in (2, 1, 3, 0):
         for j in range(4):
-            out, base, tail = outs[k], j * BODY, 4 * BODY + 2 * j
+            out, base, tail = outs.at[k], j * BODY, 4 * BODY + 2 * j
             lo, hi, begin, keep0, keep1 = bounds(k, j)
-
-            @pl.when(hi > begin + 256)
-            def _():
-                second = pl.multiple_of(jnp.minimum(begin + 256, ROWS - 48), 16)
-                sums = part(second, begin + 256, hi, 48)
-                pair, diag = packed(sums[:, :BLOCK])
-                out[base : base + 128, :] += jnp.where(keep0, sums[:, BLOCK : 2 * BLOCK], zero)
-                out[base + 128 : base + 256, :] += jnp.where(keep1, sums[:, 2 * BLOCK :], zero)
-                out[base + 256 : base + 320, :] += pair
-                out[tail + 1 : tail + 2, :] += diag
-
-
-def add_kernel(a_ref, b_ref, c_ref, d_ref, *outs):
+            sums = part(begin, lo, hi, WINDOW)
+            pair, diag = packed(sums[:, :BLOCK])
+            out[base : base + 128, :] = jnp.where(keep0, sums[:, BLOCK : 2 * BLOCK], zero)
+            out[base + 128 : base + 256, :] = jnp.where(keep1, sums[:, 2 * BLOCK :], zero)
+            out[base + 256 : base + 320, :] = pair
+            out[tail + 1 : tail + 2, :] = diag
+            out[tail : tail + 1, :] = grad[4 * k + j : 4 * k + j + 1, :]
+        leave.append(pltpu.make_async_copy(outs.at[k], dests[k], out_sems.at[k]))
+        leave[-1].start()
+    for copy in leave:
+        copy.wait()
+
+
+def near_kernel(a_ref, b_ref, out_ref):
+    out_ref[...] = a_ref[...] + b_ref[...]
+
+
+def add_kernel(a_ref, b_ref, c_ref, *outs):
     for j in range(4):
         for rows, put in (
             (slice(j * BODY, (j + 1) * BODY), slice(0, BODY)),
             (slice(4 * BODY + 2 * j, 4 * BODY + 2 * j + 2), slice(BODY, BODY + 2)),
         ):
-            outs[j][put, :] = (a_ref[rows, :] + b_ref[rows, :]) + (c_ref[rows, :] + d_ref[rows, :])
+            outs[j][put, :] = (a_ref[rows, :] + b_ref[rows, :]) + c_ref[rows, :]
         outs[j][BODY + 2 :, :] = jnp.zeros((6, BLOCK), F32)
 
 
@@ -306,18 +303,24 @@
     pltpu.SMEM((SLOTS,), jnp.int32),
     pltpu.SMEM((512,), jnp.int32),
     pltpu.SemaphoreType.DMA((12,)),
+    pltpu.VMEM((4, 4 * BODY + 8, BLOCK), F32),
+    pltpu.VMEM((FAR_N, 2 * SHARE, BLOCK), F32),
+    pltpu.SemaphoreType.DMA((5,)),
 ]
-COST = {}
+COST = {
+    name: pl.CostEstimate(flops=flops, bytes_accessed=0, transcendentals=0)
+    for name, flops in {"near": 300000000, "add": 500000000}.items()
+}
 PANEL = [pltpu.VMEM((BLOCK, TEX_W), F32), pltpu.VMEM((BLOCK, TEX_W), F32)]
 
 
-def call(kernel, name, outs, specs, scratch=(), room=24):
+def call(kernel, name, outs, specs, scratch=(), room=24, out_spec=VMEM):
     return pl.pallas_call(
         kernel,
         cost_estimate=COST.get(name),
         out_shape=[jax.ShapeDtypeStruct(s, F32) for s in outs],
         in_specs=specs,
-        out_specs=[VMEM] * len(outs),
+        out_specs=[out_spec] * len(outs),
         scratch_shapes=scratch,
         name=name,
         compiler_params=pltpu.CompilerParams(vmem_limit_bytes=room * 2**20),
@@ -351,9 +354,11 @@
         [HBM] * 6,
         LOCAL_SCRATCH,
         60,
+        HBM,
     )(cam, tex, res, obs, col_ids, block_pattern)
-    moved = [pieces[0]] + [shift(pieces[k], "x", k) for k in (2, 1, 3)]
-    pieces = call(add_kernel, "add", [(BODY + 8, BLOCK)] * 4, [VMEM] * 4)(*moved)
+    far, right, left = (shift(pieces[k], "x", k) for k in (2, 1, 3))
+    (near,) = call(near_kernel, "near", [(4 * BODY + 8, BLOCK)], [VMEM] * 2)(pieces[0], far)
+    pieces = call(add_kernel, "add", [(BODY + 8, BLOCK)] * 4, [VMEM] * 3)(near, right, left)
     parts = [pieces[0]] + [shift(pieces[j], "yl", j) for j in (1, 2, 3)]
 
     share = jnp.sum(lax.all_to_all(tex_part, FAR, 0, 0), axis=0)

time: 79.6 us -> 77.9 us (0.979)
  Pallas kernels: 16.6 us -> 15.3 us
  transfers between devices with their start and end apart: 8 -> 8, of which waited for: 0 -> 0; matrix products, arithmetic and copies ran while one was open for 1% -> 1% of each run, Pallas kernels for 13% -> 12%
where the time goes in v8:
time: 77.9 us; the launch traced here: 77.3 us
  starting transfers between devices  41.4 us (53%)
  blocking collectives  18.4 us (24%)
  Pallas kernels  15.3 us (20%)
  between operations  1.43 us (2%)
    ppermute x6, starting transfers between devices, shift(): return lax.ppermute(value, axis, [(i, (i + by) % n) for i in range(n)])  21.1 us
    all_to_all x1, blocking collectives, spread_sum(): return jnp.sum(lax.all_to_all(copies, axes, 0, 0), axis=0)  18.4 us
    all_to_all x1, starting transfers between devices, shards(): share = jnp.sum(lax.all_to_all(tex_part, FAR, 0, 0), axis=0)  13.7 us
    pallas_call x1, Pallas kernels, shards(): call(panel_kernel, 'panel', [(TEX_W, TEX_W), (TEX_W, TEX_W), (1, TEX_W)],...  8.98 us
    all_to_all x1, starting transfers between devices, shards(): tex_sums = lax.all_to_all(copies, FAR, 0, 0)  6.54 us
    pallas_call x1, Pallas kernels, shards(): call(local_kernel, 'local', [(4 * BODY + 8, BLOCK)] * 4 + [(FAR_N, SHARE...  4.74 us
  transfers between devices with their start and end apart: 8, of which 0 were waited for; matrix products, arithmetic and copies ran while one was open for 1% of the time, Pallas kernels for 12%

profile of v8, /device:TPU:1, one launch (start us, length us, event | category | flops | bytes accessed | tf_op | source)
XLA Modules:
  0.0 77.3 jit_solution(10665800215829074095)
XLA Ops:
  0.6 4.7 %local.1 = (f32[1288,128]{1,0:T(8,128)}, f32[1288,128]{1,0:T(8,128)}, f32[1288,128]{1,0:T(8,128)}, f32[1288,128]{1,0:T(8,128)}, f32[32,16,128]{2,1,0:T(8,128)}) custom-call(bf16[1536,128]{1,0:T(8,128)(2,1)} %bitcast.11, bf16[1536,256]{1,0:T(8,128)(2,1)} %bitcast.10, bf16[1,1536]{1,0:T(2,128)(2,1)} %bitcast.12, s32[192]{0:T(256)} %bitcast.13, s32[16]{0:T(128)} %ids_any.1, ...), custom_call_target="tpu_custom_call" | custom-call | tf_op jit(solution)/shard_map/local/pallas_call | solution.py:350
  5.4 13.7 %all-to-all-start = ((f32[32,16,128]{2,1,0:T(8,128)}), f32[32,16,128]{2,1,0:T(8,128)S(1)}, u32[]{:S(2)}, u32[]{:S(2)}) async-start(f32[32,16,128]{2,1,0:T(8,128)} %get-tuple-element.27), calls=%async_computation | async-start | bytes 524288 | tf_op jit(solution)/shard_map/all_to_all | solution.py:364
  19.1 4.6 %collective-permute-start = (f32[1288,128]{1,0:T(8,128)}, f32[1288,128]{1,0:T(8,128)S(1)}, u32[]{:S(2)}, u32[]{:S(2)}) collective-permute-start(f32[1288,128]{1,0:T(8,128)} %get-tuple-element.20), channel_id=1, source_target_pairs={{0,64},{32,96},{64,0},{96,32},{1,65},{33,97},{65,1},{97,33},{2,66}... | collective-permute-start | bytes 1978376 | tf_op jit(solution)/shard_map/ppermute | solution.py:332
  23.8 2.2 %collective-permute-start.1 = (f32[1288,128]{1,0:T(8,128)}, f32[1288,128]{1,0:T(8,128)S(1)}, u32[]{:S(2)}, u32[]{:S(2)}) collective-permute-start(f32[1288,128]{1,0:T(8,128)} %get-tuple-element.21), channel_id=1, source_target_pairs={{0,32},{32,64},{64,96},{96,0},{1,33},{33,65},{65,97},{97,1},{2,34}... | collective-permute-start | bytes 1978376 | tf_op jit(solution)/shard_map/ppermute | solution.py:332
  26.0 4.3 %collective-permute-start.2 = (f32[1288,128]{1,0:T(8,128)}, f32[1288,128]{1,0:T(8,128)S(1)}, u32[]{:S(2)}, u32[]{:S(2)}) collective-permute-start(f32[1288,128]{1,0:T(8,128)} %get-tuple-element.22), channel_id=1, source_target_pairs={{0,96},{32,0},{64,32},{96,64},{1,97},{33,1},{65,33},{97,65},{2,98}... | collective-permute-start | bytes 1978376 | tf_op jit(solution)/shard_map/ppermute | solution.py:332
  30.3 0.0 all-to-all-done
  30.3 0.0 copy-start
  30.3 18.4 %all_to_all.15 = f32[16,16,128]{2,1,0:T(8,128)S(1)} all-to-all(f32[16,16,128]{2,1,0:T(8,128)S(1)} %broadcast_in_dim.10), channel_id=1, replica_groups=mesh['yl'=4,'x'=4,'yh'=2,'z'=8,'c'=2] {'yl','yh','c'}, dimensions={0} | all-to-all | bytes 262144 | tf_op jit(solution)/shard_map/all_to_all | solution.py:338
  48.8 0.7 broadcast_in_dim.22
  49.5 6.5 %all-to-all-start.2 = ((f32[32,16,128]{2,1,0:T(8,128)}), f32[32,16,128]{2,1,0:T(8,128)S(1)}, u32[]{:S(2)}, u32[]{:S(2)}) async-start(f32[32,16,128]{2,1,0:T(8,128)} %broadcast_in_dim.22), calls=%async_computation.2 | async-start | bytes 524288 | tf_op jit(solution)/shard_map/all_to_all | solution.py:367
  56.0 0.0 collective-permute-done.b_ref
  56.0 0.0 copy-done
  56.0 0.1 near.1.a_ref
  56.1 0.0 collective-permute-done.1.b_ref
  56.1 0.0 collective-permute-done.2.c_ref
  56.2 0.1 add.1
  56.3 2.8 %collective-permute-start.3 = (f32[328,128]{1,0:T(8,128)S(1)}, f32[328,128]{1,0:T(8,128)S(1)}, u32[]{:S(2)}, u32[]{:S(2)}) collective-permute-start(f32[328,128]{1,0:T(8,128)S(1)} %get-tuple-element.24), channel_id=1, source_target_pairs={{0,128},{128,256},{256,384},{384,0},{1,129},{129,257},{257,385},{3... | collective-permute-start | bytes 503816 | tf_op jit(solution)/shard_map/ppermute | solution.py:332
  59.1 4.2 %collective-permute-start.4 = (f32[328,128]{1,0:T(8,128)S(1)}, f32[328,128]{1,0:T(8,128)S(1)}, u32[]{:S(2)}, u32[]{:S(2)}) collective-permute-start(f32[328,128]{1,0:T(8,128)S(1)} %get-tuple-element.25), channel_id=1, source_target_pairs={{0,256},{128,384},{256,0},{384,128},{1,257},{129,385},{257,1},{385... | collective-permute-start | bytes 503816 | tf_op jit(solution)/shard_map/ppermute | solution.py:332
  63.3 3.0 %collective-permute-start.5 = (f32[328,128]{1,0:T(8,128)S(1)}, f32[328,128]{1,0:T(8,128)S(1)}, u32[]{:S(2)}, u32[]{:S(2)}) collective-permute-start(f32[328,128]{1,0:T(8,128)S(1)} %get-tuple-element.26), channel_id=1, source_target_pairs={{0,384},{128,0},{256,128},{384,256},{1,385},{129,1},{257,129},{385... | collective-permute-start | bytes 503816 | tf_op jit(solution)/shard_map/ppermute | solution.py:332
  66.9 0.0 all-to-all-done.2.sums_ref
  66.9 9.0 %panel.1 = (f32[256,256]{1,0:T(8,128)}, f32[256,256]{1,0:T(8,128)S(1)}, f32[1,256]{1,0:T(1,128)S(1)}) custom-call(f32[32,16,128]{2,1,0:T(8,128)S(1)} %all-to-all-done.2.sums_ref, f32[1]{0:T(128)} %bitcast.8.damping_ref), custom_call_target="tpu_custom_call" | custom-call | tf_op jit(solution)/shard_map/panel/pallas_call | solution.py:369
  75.9 0.0 collective-permute-done.3.b_ref
  75.9 0.0 collective-permute-done.4.c_ref
  75.9 0.0 collective-permute-done.5.d_ref
  75.9 1.3 %last.1 = (f32[128,128]{1,0:T(8,128)}, f32[1,128]{1,0:T(1,128)}, f32[128,256]{1,0:T(8,128)}) custom-call(f32[328,128]{1,0:T(8,128)S(1)} %get-tuple-element.23.a_ref, f32[328,128]{1,0:T(8,128)S(1)} %collective-permute-done.3.b_ref, f32[328,128]{1,0:T(8,128)S(1)} %collective-permute-done.4.c_ref, f32[328,128]{1,0:T(8,128)S(1)} %collective-permute-done.5.d_ref, ...), custom_call_target="tpu_custom_call" | custom-call | tf_op jit(solution)/shard_map/last/pallas_call | solution.py:372
  (3 shorter events, 0.1 us)
Async XLA Ops:
  5.4 24.9 %all-to-all-start = ((f32[32,16,128]{2,1,0:T(8,128)}), f32[32,16,128]{2,1,0:T(8,128)S(1)}, u32[]{:S(2)}, u32[]{:S(2)}) async-start(f32[32,16,128]{2,1,0:T(8,128)} %get-tuple-element.27), calls=%async_computation | async-start | bytes 524288 | tf_op jit(solution)/shard_map/all_to_all | solution.py:364
  19.1 36.9 %collective-permute-start = (f32[1288,128]{1,0:T(8,128)}, f32[1288,128]{1,0:T(8,128)S(1)}, u32[]{:S(2)}, u32[]{:S(2)}) collective-permute-start(f32[1288,128]{1,0:T(8,128)} %get-tuple-element.20), channel_id=1, source_target_pairs={{0,64},{32,96},{64,0},{96,32},{1,65},{33,97},{65,1},{97,33},{2,66}... | collective-permute-start | bytes 1978376 | tf_op jit(solution)/shard_map/ppermute | solution.py:332
  23.8 32.4 %collective-permute-start.1 = (f32[1288,128]{1,0:T(8,128)}, f32[1288,128]{1,0:T(8,128)S(1)}, u32[]{:S(2)}, u32[]{:S(2)}) collective-permute-start(f32[1288,128]{1,0:T(8,128)} %get-tuple-element.21), channel_id=1, source_target_pairs={{0,32},{32,64},{64,96},{96,0},{1,33},{33,65},{65,97},{97,1},{2,34}... | collective-permute-start | bytes 1978376 | tf_op jit(solution)/shard_map/ppermute | solution.py:332
  26.0 30.2 %collective-permute-start.2 = (f32[1288,128]{1,0:T(8,128)}, f32[1288,128]{1,0:T(8,128)S(1)}, u32[]{:S(2)}, u32[]{:S(2)}) collective-permute-start(f32[1288,128]{1,0:T(8,128)} %get-tuple-element.22), channel_id=1, source_target_pairs={{0,96},{32,0},{64,32},{96,64},{1,97},{33,1},{65,33},{97,65},{2,98}... | collective-permute-start | bytes 1978376 | tf_op jit(solution)/shard_map/ppermute | solution.py:332
  30.3 25.7 %copy-start = (f32[1288,128]{1,0:T(8,128)S(1)}, f32[1288,128]{1,0:T(8,128)}, u32[]{:S(2)}) copy-start(f32[1288,128]{1,0:T(8,128)} %get-tuple-element.19.a_ref) | copy-start | bytes 1978372
  49.5 17.5 %all-to-all-start.2 = ((f32[32,16,128]{2,1,0:T(8,128)}), f32[32,16,128]{2,1,0:T(8,128)S(1)}, u32[]{:S(2)}, u32[]{:S(2)}) async-start(f32[32,16,128]{2,1,0:T(8,128)} %broadcast_in_dim.22), calls=%async_computation.2 | async-start | bytes 524288 | tf_op jit(solution)/shard_map/all_to_all | solution.py:367
  56.3 19.6 %collective-permute-start.3 = (f32[328,128]{1,0:T(8,128)S(1)}, f32[328,128]{1,0:T(8,128)S(1)}, u32[]{:S(2)}, u32[]{:S(2)}) collective-permute-start(f32[328,128]{1,0:T(8,128)S(1)} %get-tuple-element.24), channel_id=1, source_target_pairs={{0,128},{128,256},{256,384},{384,0},{1,129},{129,257},{257,385},{3... | collective-permute-start | bytes 503816 | tf_op jit(solution)/shard_map/ppermute | solution.py:332
  59.1 16.8 %collective-permute-start.4 = (f32[328,128]{1,0:T(8,128)S(1)}, f32[328,128]{1,0:T(8,128)S(1)}, u32[]{:S(2)}, u32[]{:S(2)}) collective-permute-start(f32[328,128]{1,0:T(8,128)S(1)} %get-tuple-element.25), channel_id=1, source_target_pairs={{0,256},{128,384},{256,0},{384,128},{1,257},{129,385},{257,1},{385... | collective-permute-start | bytes 503816 | tf_op jit(solution)/shard_map/ppermute | solution.py:332
  63.3 12.6 %collective-permute-start.5 = (f32[328,128]{1,0:T(8,128)S(1)}, f32[328,128]{1,0:T(8,128)S(1)}, u32[]{:S(2)}, u32[]{:S(2)}) collective-permute-start(f32[328,128]{1,0:T(8,128)S(1)} %get-tuple-element.26), channel_id=1, source_target_pairs={{0,384},{128,0},{256,128},{384,256},{1,385},{129,1},{257,129},{385... | collective-permute-start | bytes 503816 | tf_op jit(solution)/shard_map/ppermute | solution.py:332

commit v9 on v8

--- a/solution.py
+++ b/solution.py
@@ -204,13 +204,14 @@
     ab[:, :BLOCK] = block
     ab[:, BLOCK:] = (row == col).astype(F32)
     cur = [block[:8], ab[:8, BLOCK:]]
+    heads = [lanes(cur[0], k) for k in range(8)]
     for b in range(16):
         more = b < 15
-        heads = [lanes(cur[0], 8 * b + k) for k in range(8)]
         if more:
             rows = slice(8 * (b + 1), 8 * (b + 2))
             below = [ab[rows, :BLOCK], ab[rows, BLOCK:]]
             tails = [lanes(below[0], 8 * b + k) for k in range(8)]
+            later = [lanes(below[0], 8 * (b + 1) + k) for k in range(8)]
         for j in range(8):
             scale = lax.rsqrt(subs(heads[j], j))
             head = jnp.where(sub > j, heads[j] * scale, 0.0)
@@ -223,6 +224,8 @@
                     tails[k] = tails[k] - tail * pick
             if more and j == 7:
                 tail = tails[j] * scale
+            if more:
+                later = [value - tail * subs(tail, k) for k, value in enumerate(later)]
             for part in range(2):
                 pivot = subs(cur[part], j) * scale
                 cur[part] = jnp.where(sub == j, pivot, cur[part] - head * pivot)
@@ -238,7 +241,7 @@
             )
             ab[8 * (b + 2) :, :] -= update[8 * (b + 2) :, :]
         if more:
-            cur = below
+            cur, heads = below, later
     return jnp.where(row >= col, upper[:, :BLOCK].T, 0.0), upper[:, BLOCK:]
 
 
@@ -359,7 +362,7 @@
     far, right, left = (shift(pieces[k], "x", k) for k in (2, 1, 3))
     (near,) = call(near_kernel, "near", [(4 * BODY + 8, BLOCK)], [VMEM] * 2)(pieces[0], far)
     pieces = call(add_kernel, "add", [(BODY + 8, BLOCK)] * 4, [VMEM] * 3)(near, right, left)
-    parts = [pieces[0]] + [shift(pieces[j], "yl", j) for j in (1, 2, 3)]
+    parts = [pieces[0]] + [shift(pieces[j], "yl", j) for j in (2, 1, 3)]
 
     share = jnp.sum(lax.all_to_all(tex_part, FAR, 0, 0), axis=0)
     share = spread_sum(share, NEAR)

time: 77.9 us -> 77.9 us (level)
  Pallas kernels: 15.3 us -> 13.8 us
  starting transfers between devices: 41.4 us -> 42.3 us
    pallas_call x1, Pallas kernels: 8.98 us -> 7.54 us  [shards(): call(panel_kernel, 'panel', [(TEX_W, TEX_W), (TEX_W, TEX_W), (1, TEX_W)],...]
    ppermute x6, starting transfers between devices: 21.1 us -> 22 us  [shift(): return lax.ppermute(value, axis, [(i, (i + by) % n) for i in range(n)])]
  transfers between devices with their start and end apart: 8 -> 8, of which waited for: 0 -> 1; matrix products, arithmetic and copies ran while one was open for 1% -> 1% of each run, Pallas kernels for 12% -> 10%
where the time goes in v9:
time: 77.9 us; the launch traced here: 77.4 us
  starting transfers between devices  42.3 us (54%)
  blocking collectives  18.4 us (24%)
  Pallas kernels  13.8 us (18%)
  between operations  1.43 us (2%)
    ppermute x6, starting transfers between devices, shift(): return lax.ppermute(value, axis, [(i, (i + by) % n) for i in range(n)])  22 us
    all_to_all x1, blocking collectives, spread_sum(): return jnp.sum(lax.all_to_all(copies, axes, 0, 0), axis=0)  18.4 us
    all_to_all x1, starting transfers between devices, shards(): share = jnp.sum(lax.all_to_all(tex_part, FAR, 0, 0), axis=0)  13.7 us
    pallas_call x1, Pallas kernels, shards(): call(panel_kernel, 'panel', [(TEX_W, TEX_W), (TEX_W, TEX_W), (1, TEX_W)],...  7.54 us
    all_to_all x1, starting transfers between devices, shards(): tex_sums = lax.all_to_all(copies, FAR, 0, 0)  6.55 us
    pallas_call x1, Pallas kernels, shards(): call(local_kernel, 'local', [(4 * BODY + 8, BLOCK)] * 4 + [(FAR_N, SHARE...  4.71 us
  transfers between devices with their start and end apart: 8, of which 1 were waited for; matrix products, arithmetic and copies ran while one was open for 1% of the time, Pallas kernels for 10%

profile of v9, /device:TPU:1, one launch (start us, length us, event | category | flops | bytes accessed | tf_op | source)
XLA Modules:
  0.0 77.4 jit_solution(4250748673871470253)
XLA Ops:
  0.6 4.7 %local.1 = (f32[1288,128]{1,0:T(8,128)}, f32[1288,128]{1,0:T(8,128)}, f32[1288,128]{1,0:T(8,128)}, f32[1288,128]{1,0:T(8,128)}, f32[32,16,128]{2,1,0:T(8,128)}) custom-call(bf16[1536,128]{1,0:T(8,128)(2,1)} %bitcast.11, bf16[1536,256]{1,0:T(8,128)(2,1)} %bitcast.10, bf16[1,1536]{1,0:T(2,128)(2,1)} %bitcast.12, s32[192]{0:T(256)} %bitcast.13, s32[16]{0:T(128)} %ids_any.1, ...), custom_call_target="tpu_custom_call" | custom-call | tf_op jit(solution)/shard_map/local/pallas_call | solution.py:353
  5.4 13.7 %all-to-all-start = ((f32[32,16,128]{2,1,0:T(8,128)}), f32[32,16,128]{2,1,0:T(8,128)S(1)}, u32[]{:S(2)}, u32[]{:S(2)}) async-start(f32[32,16,128]{2,1,0:T(8,128)} %get-tuple-element.27), calls=%async_computation | async-start | bytes 524288 | tf_op jit(solution)/shard_map/all_to_all | solution.py:367
  19.1 4.6 %collective-permute-start = (f32[1288,128]{1,0:T(8,128)}, f32[1288,128]{1,0:T(8,128)S(1)}, u32[]{:S(2)}, u32[]{:S(2)}) collective-permute-start(f32[1288,128]{1,0:T(8,128)} %get-tuple-element.20), channel_id=1, source_target_pairs={{0,64},{32,96},{64,0},{96,32},{1,65},{33,97},{65,1},{97,33},{2,66}... | collective-permute-start | bytes 1978376 | tf_op jit(solution)/shard_map/ppermute | solution.py:335
  23.8 2.2 %collective-permute-start.1 = (f32[1288,128]{1,0:T(8,128)}, f32[1288,128]{1,0:T(8,128)S(1)}, u32[]{:S(2)}, u32[]{:S(2)}) collective-permute-start(f32[1288,128]{1,0:T(8,128)} %get-tuple-element.21), channel_id=1, source_target_pairs={{0,32},{32,64},{64,96},{96,0},{1,33},{33,65},{65,97},{97,1},{2,34}... | collective-permute-start | bytes 1978376 | tf_op jit(solution)/shard_map/ppermute | solution.py:335
  26.0 4.3 %collective-permute-start.2 = (f32[1288,128]{1,0:T(8,128)}, f32[1288,128]{1,0:T(8,128)S(1)}, u32[]{:S(2)}, u32[]{:S(2)}) collective-permute-start(f32[1288,128]{1,0:T(8,128)} %get-tuple-element.22), channel_id=1, source_target_pairs={{0,96},{32,0},{64,32},{96,64},{1,97},{33,1},{65,33},{97,65},{2,98}... | collective-permute-start | bytes 1978376 | tf_op jit(solution)/shard_map/ppermute | solution.py:335
  30.3 0.0 all-to-all-done
  30.3 0.0 copy-start
  30.3 18.4 %all_to_all.15 = f32[16,16,128]{2,1,0:T(8,128)S(1)} all-to-all(f32[16,16,128]{2,1,0:T(8,128)S(1)} %broadcast_in_dim.10), channel_id=1, replica_groups=mesh['yl'=4,'x'=4,'yh'=2,'z'=8,'c'=2] {'yl','yh','c'}, dimensions={0} | all-to-all | bytes 262144 | tf_op jit(solution)/shard_map/all_to_all | solution.py:341
  48.8 0.7 broadcast_in_dim.22
  49.5 6.5 %all-to-all-start.2 = ((f32[32,16,128]{2,1,0:T(8,128)}), f32[32,16,128]{2,1,0:T(8,128)S(1)}, u32[]{:S(2)}, u32[]{:S(2)}) async-start(f32[32,16,128]{2,1,0:T(8,128)} %broadcast_in_dim.22), calls=%async_computation.2 | async-start | bytes 524288 | tf_op jit(solution)/shard_map/all_to_all | solution.py:370
  56.0 0.0 collective-permute-done.b_ref
  56.0 0.0 copy-done
  56.0 0.1 near.1.a_ref
  56.1 0.0 collective-permute-done.1.b_ref
  56.1 0.0 collective-permute-done.2.c_ref
  56.2 0.1 add.1
  56.3 3.8 %collective-permute-start.3 = (f32[328,128]{1,0:T(8,128)S(1)}, f32[328,128]{1,0:T(8,128)S(1)}, u32[]{:S(2)}, u32[]{:S(2)}) collective-permute-start(f32[328,128]{1,0:T(8,128)S(1)} %get-tuple-element.24), channel_id=1, source_target_pairs={{0,256},{128,384},{256,0},{384,128},{1,257},{129,385},{257,1},{385... | collective-permute-start | bytes 503816 | tf_op jit(solution)/shard_map/ppermute | solution.py:335
  60.1 3.2 %collective-permute-start.4 = (f32[328,128]{1,0:T(8,128)S(1)}, f32[328,128]{1,0:T(8,128)S(1)}, u32[]{:S(2)}, u32[]{:S(2)}) collective-permute-start(f32[328,128]{1,0:T(8,128)S(1)} %get-tuple-element.25), channel_id=1, source_target_pairs={{0,128},{128,256},{256,384},{384,0},{1,129},{129,257},{257,385},{3... | collective-permute-start | bytes 503816 | tf_op jit(solution)/shard_map/ppermute | solution.py:335
  63.3 3.9 %collective-permute-start.5 = (f32[328,128]{1,0:T(8,128)S(1)}, f32[328,128]{1,0:T(8,128)S(1)}, u32[]{:S(2)}, u32[]{:S(2)}) collective-permute-start(f32[328,128]{1,0:T(8,128)S(1)} %get-tuple-element.26), channel_id=1, source_target_pairs={{0,384},{128,0},{256,128},{384,256},{1,385},{129,1},{257,129},{385... | collective-permute-start | bytes 503816 | tf_op jit(solution)/shard_map/ppermute | solution.py:335
  67.8 0.0 all-to-all-done.2.sums_ref
  67.8 7.5 %panel.1 = (f32[256,256]{1,0:T(8,128)}, f32[256,256]{1,0:T(8,128)S(1)}, f32[1,256]{1,0:T(1,128)S(1)}) custom-call(f32[32,16,128]{2,1,0:T(8,128)S(1)} %all-to-all-done.2.sums_ref, f32[1]{0:T(128)} %bitcast.8.damping_ref), custom_call_target="tpu_custom_call" | custom-call | tf_op jit(solution)/shard_map/panel/pallas_call | solution.py:372
  75.4 0.0 collective-permute-done.3.b_ref
  75.4 0.0 collective-permute-done.4.c_ref
  75.4 0.7 collective-permute-done.5.d_ref
  76.1 1.3 %last.1 = (f32[128,128]{1,0:T(8,128)}, f32[1,128]{1,0:T(1,128)}, f32[128,256]{1,0:T(8,128)}) custom-call(f32[328,128]{1,0:T(8,128)S(1)} %get-tuple-element.23.a_ref, f32[328,128]{1,0:T(8,128)S(1)} %collective-permute-done.3.b_ref, f32[328,128]{1,0:T(8,128)S(1)} %collective-permute-done.4.c_ref, f32[328,128]{1,0:T(8,128)S(1)} %collective-permute-done.5.d_ref, ...), custom_call_target="tpu_custom_call" | custom-call | tf_op jit(solution)/shard_map/last/pallas_call | solution.py:375
  (3 shorter events, 0.1 us)
Async XLA Ops:
  5.4 24.9 %all-to-all-start = ((f32[32,16,128]{2,1,0:T(8,128)}), f32[32,16,128]{2,1,0:T(8,128)S(1)}, u32[]{:S(2)}, u32[]{:S(2)}) async-start(f32[32,16,128]{2,1,0:T(8,128)} %get-tuple-element.27), calls=%async_computation | async-start | bytes 524288 | tf_op jit(solution)/shard_map/all_to_all | solution.py:367
  19.1 36.9 %collective-permute-start = (f32[1288,128]{1,0:T(8,128)}, f32[1288,128]{1,0:T(8,128)S(1)}, u32[]{:S(2)}, u32[]{:S(2)}) collective-permute-start(f32[1288,128]{1,0:T(8,128)} %get-tuple-element.20), channel_id=1, source_target_pairs={{0,64},{32,96},{64,0},{96,32},{1,65},{33,97},{65,1},{97,33},{2,66}... | collective-permute-start | bytes 1978376 | tf_op jit(solution)/shard_map/ppermute | solution.py:335
  23.8 32.4 %collective-permute-start.1 = (f32[1288,128]{1,0:T(8,128)}, f32[1288,128]{1,0:T(8,128)S(1)}, u32[]{:S(2)}, u32[]{:S(2)}) collective-permute-start(f32[1288,128]{1,0:T(8,128)} %get-tuple-element.21), channel_id=1, source_target_pairs={{0,32},{32,64},{64,96},{96,0},{1,33},{33,65},{65,97},{97,1},{2,34}... | collective-permute-start | bytes 1978376 | tf_op jit(solution)/shard_map/ppermute | solution.py:335
  26.0 30.2 %collective-permute-start.2 = (f32[1288,128]{1,0:T(8,128)}, f32[1288,128]{1,0:T(8,128)S(1)}, u32[]{:S(2)}, u32[]{:S(2)}) collective-permute-start(f32[1288,128]{1,0:T(8,128)} %get-tuple-element.22), channel_id=1, source_target_pairs={{0,96},{32,0},{64,32},{96,64},{1,97},{33,1},{65,33},{97,65},{2,98}... | collective-permute-start | bytes 1978376 | tf_op jit(solution)/shard_map/ppermute | solution.py:335
  30.3 25.7 %copy-start = (f32[1288,128]{1,0:T(8,128)S(1)}, f32[1288,128]{1,0:T(8,128)}, u32[]{:S(2)}) copy-start(f32[1288,128]{1,0:T(8,128)} %get-tuple-element.19.a_ref) | copy-start | bytes 1978372
  49.5 18.4 %all-to-all-start.2 = ((f32[32,16,128]{2,1,0:T(8,128)}), f32[32,16,128]{2,1,0:T(8,128)S(1)}, u32[]{:S(2)}, u32[]{:S(2)}) async-start(f32[32,16,128]{2,1,0:T(8,128)} %broadcast_in_dim.22), calls=%async_computation.2 | async-start | bytes 524288 | tf_op jit(solution)/shard_map/all_to_all | solution.py:370
  56.3 19.1 %collective-permute-start.3 = (f32[328,128]{1,0:T(8,128)S(1)}, f32[328,128]{1,0:T(8,128)S(1)}, u32[]{:S(2)}, u32[]{:S(2)}) collective-permute-start(f32[328,128]{1,0:T(8,128)S(1)} %get-tuple-element.24), channel_id=1, source_target_pairs={{0,256},{128,384},{256,0},{384,128},{1,257},{129,385},{257,1},{385... | collective-permute-start | bytes 503816 | tf_op jit(solution)/shard_map/ppermute | solution.py:335
  60.1 15.3 %collective-permute-start.4 = (f32[328,128]{1,0:T(8,128)S(1)}, f32[328,128]{1,0:T(8,128)S(1)}, u32[]{:S(2)}, u32[]{:S(2)}) collective-permute-start(f32[328,128]{1,0:T(8,128)S(1)} %get-tuple-element.25), channel_id=1, source_target_pairs={{0,128},{128,256},{256,384},{384,0},{1,129},{129,257},{257,385},{3... | collective-permute-start | bytes 503816 | tf_op jit(solution)/shard_map/ppermute | solution.py:335
  63.3 12.8 %collective-permute-start.5 = (f32[328,128]{1,0:T(8,128)S(1)}, f32[328,128]{1,0:T(8,128)S(1)}, u32[]{:S(2)}, u32[]{:S(2)}) collective-permute-start(f32[328,128]{1,0:T(8,128)S(1)} %get-tuple-element.26), channel_id=1, source_target_pairs={{0,384},{128,0},{256,128},{384,256},{1,385},{129,1},{257,129},{385... | collective-permute-start | bytes 503816 | tf_op jit(solution)/shard_map/ppermute | solution.py:335

commit v10 on v9

--- a/solution.py
+++ b/solution.py
@@ -105,9 +105,10 @@
         ),
         sems,
     )
-    for copy in copies[:4]:
+    copies[0].wait()
+    find_starts(obs_ref, starts)
+    for copy in copies[1:4]:
         copy.wait()
-    find_starts(obs_ref, starts)
     sub = iota((SLOTS, BLOCK), 0)
     first = jnp.zeros((SLOTS, BLOCK), jnp.int32)
     last = jnp.zeros((SLOTS, BLOCK), jnp.int32)

time: 77.9 us -> 77.9 us (level)
  no operation moved by 1% of the time
where the time goes in v10:
time: 77.9 us; the launch traced here: 77.4 us
  starting transfers between devices  42.3 us (54%)
  blocking collectives  18.4 us (24%)
  Pallas kernels  13.8 us (18%)
  between operations  1.43 us (2%)
    ppermute x6, starting transfers between devices, shift(): return lax.ppermute(value, axis, [(i, (i + by) % n) for i in range(n)])  22 us
    all_to_all x1, blocking collectives, spread_sum(): return jnp.sum(lax.all_to_all(copies, axes, 0, 0), axis=0)  18.4 us
    all_to_all x1, starting transfers between devices, shards(): share = jnp.sum(lax.all_to_all(tex_part, FAR, 0, 0), axis=0)  13.7 us
    pallas_call x1, Pallas kernels, shards(): call(panel_kernel, 'panel', [(TEX_W, TEX_W), (TEX_W, TEX_W), (1, TEX_W)],...  7.54 us
    all_to_all x1, starting transfers between devices, shards(): tex_sums = lax.all_to_all(copies, FAR, 0, 0)  6.55 us
    pallas_call x1, Pallas kernels, shards(): call(local_kernel, 'local', [(4 * BODY + 8, BLOCK)] * 4 + [(FAR_N, SHARE...  4.72 us
  transfers between devices with their start and end apart: 8, of which 1 were waited for; matrix products, arithmetic and copies ran while one was open for 1% of the time, Pallas kernels for 10%

profile of v10, /device:TPU:1, one launch (start us, length us, event | category | flops | bytes accessed | tf_op | source)
XLA Modules:
  0.0 77.4 jit_solution(11949953365889922716)
XLA Ops:
  0.6 4.7 %local.1 = (f32[1288,128]{1,0:T(8,128)}, f32[1288,128]{1,0:T(8,128)}, f32[1288,128]{1,0:T(8,128)}, f32[1288,128]{1,0:T(8,128)}, f32[32,16,128]{2,1,0:T(8,128)}) custom-call(bf16[1536,128]{1,0:T(8,128)(2,1)} %bitcast.11, bf16[1536,256]{1,0:T(8,128)(2,1)} %bitcast.10, bf16[1,1536]{1,0:T(2,128)(2,1)} %bitcast.12, s32[192]{0:T(256)} %bitcast.13, s32[16]{0:T(128)} %ids_any.1, ...), custom_call_target="tpu_custom_call" | custom-call | tf_op jit(solution)/shard_map/local/pallas_call | solution.py:354
  5.4 13.7 %all-to-all-start = ((f32[32,16,128]{2,1,0:T(8,128)}), f32[32,16,128]{2,1,0:T(8,128)S(1)}, u32[]{:S(2)}, u32[]{:S(2)}) async-start(f32[32,16,128]{2,1,0:T(8,128)} %get-tuple-element.27), calls=%async_computation | async-start | bytes 524288 | tf_op jit(solution)/shard_map/all_to_all | solution.py:368
  19.1 4.6 %collective-permute-start = (f32[1288,128]{1,0:T(8,128)}, f32[1288,128]{1,0:T(8,128)S(1)}, u32[]{:S(2)}, u32[]{:S(2)}) collective-permute-start(f32[1288,128]{1,0:T(8,128)} %get-tuple-element.20), channel_id=1, source_target_pairs={{0,64},{32,96},{64,0},{96,32},{1,65},{33,97},{65,1},{97,33},{2,66}... | collective-permute-start | bytes 1978376 | tf_op jit(solution)/shard_map/ppermute | solution.py:336
  23.8 2.2 %collective-permute-start.1 = (f32[1288,128]{1,0:T(8,128)}, f32[1288,128]{1,0:T(8,128)S(1)}, u32[]{:S(2)}, u32[]{:S(2)}) collective-permute-start(f32[1288,128]{1,0:T(8,128)} %get-tuple-element.21), channel_id=1, source_target_pairs={{0,32},{32,64},{64,96},{96,0},{1,33},{33,65},{65,97},{97,1},{2,34}... | collective-permute-start | bytes 1978376 | tf_op jit(solution)/shard_map/ppermute | solution.py:336
  26.0 4.3 %collective-permute-start.2 = (f32[1288,128]{1,0:T(8,128)}, f32[1288,128]{1,0:T(8,128)S(1)}, u32[]{:S(2)}, u32[]{:S(2)}) collective-permute-start(f32[1288,128]{1,0:T(8,128)} %get-tuple-element.22), channel_id=1, source_target_pairs={{0,96},{32,0},{64,32},{96,64},{1,97},{33,1},{65,33},{97,65},{2,98}... | collective-permute-start | bytes 1978376 | tf_op jit(solution)/shard_map/ppermute | solution.py:336
  30.3 0.0 all-to-all-done
  30.3 0.0 copy-start
  30.3 18.4 %all_to_all.15 = f32[16,16,128]{2,1,0:T(8,128)S(1)} all-to-all(f32[16,16,128]{2,1,0:T(8,128)S(1)} %broadcast_in_dim.10), channel_id=1, replica_groups=mesh['yl'=4,'x'=4,'yh'=2,'z'=8,'c'=2] {'yl','yh','c'}, dimensions={0} | all-to-all | bytes 262144 | tf_op jit(solution)/shard_map/all_to_all | solution.py:342
  48.8 0.7 broadcast_in_dim.22
  49.5 6.6 %all-to-all-start.2 = ((f32[32,16,128]{2,1,0:T(8,128)}), f32[32,16,128]{2,1,0:T(8,128)S(1)}, u32[]{:S(2)}, u32[]{:S(2)}) async-start(f32[32,16,128]{2,1,0:T(8,128)} %broadcast_in_dim.22), calls=%async_computation.2 | async-start | bytes 524288 | tf_op jit(solution)/shard_map/all_to_all | solution.py:371
  56.0 0.0 collective-permute-done.b_ref
  56.1 0.0 copy-done
  56.1 0.1 near.1.a_ref
  56.1 0.0 collective-permute-done.1.b_ref
  56.2 0.0 collective-permute-done.2.c_ref
  56.2 0.1 add.1
  56.3 3.8 %collective-permute-start.3 = (f32[328,128]{1,0:T(8,128)S(1)}, f32[328,128]{1,0:T(8,128)S(1)}, u32[]{:S(2)}, u32[]{:S(2)}) collective-permute-start(f32[328,128]{1,0:T(8,128)S(1)} %get-tuple-element.24), channel_id=1, source_target_pairs={{0,256},{128,384},{256,0},{384,128},{1,257},{129,385},{257,1},{385... | collective-permute-start | bytes 503816 | tf_op jit(solution)/shard_map/ppermute | solution.py:336
  60.1 3.2 %collective-permute-start.4 = (f32[328,128]{1,0:T(8,128)S(1)}, f32[328,128]{1,0:T(8,128)S(1)}, u32[]{:S(2)}, u32[]{:S(2)}) collective-permute-start(f32[328,128]{1,0:T(8,128)S(1)} %get-tuple-element.25), channel_id=1, source_target_pairs={{0,128},{128,256},{256,384},{384,0},{1,129},{129,257},{257,385},{3... | collective-permute-start | bytes 503816 | tf_op jit(solution)/shard_map/ppermute | solution.py:336
  63.3 3.9 %collective-permute-start.5 = (f32[328,128]{1,0:T(8,128)S(1)}, f32[328,128]{1,0:T(8,128)S(1)}, u32[]{:S(2)}, u32[]{:S(2)}) collective-permute-start(f32[328,128]{1,0:T(8,128)S(1)} %get-tuple-element.26), channel_id=1, source_target_pairs={{0,384},{128,0},{256,128},{384,256},{1,385},{129,1},{257,129},{385... | collective-permute-start | bytes 503816 | tf_op jit(solution)/shard_map/ppermute | solution.py:336
  67.8 0.0 all-to-all-done.2.sums_ref
  67.8 7.5 %panel.1 = (f32[256,256]{1,0:T(8,128)}, f32[256,256]{1,0:T(8,128)S(1)}, f32[1,256]{1,0:T(1,128)S(1)}) custom-call(f32[32,16,128]{2,1,0:T(8,128)S(1)} %all-to-all-done.2.sums_ref, f32[1]{0:T(128)} %bitcast.8.damping_ref), custom_call_target="tpu_custom_call" | custom-call | tf_op jit(solution)/shard_map/panel/pallas_call | solution.py:373
  75.4 0.0 collective-permute-done.3.b_ref
  75.4 0.0 collective-permute-done.4.c_ref
  75.4 0.7 collective-permute-done.5.d_ref
  76.1 1.3 %last.1 = (f32[128,128]{1,0:T(8,128)}, f32[1,128]{1,0:T(1,128)}, f32[128,256]{1,0:T(8,128)}) custom-call(f32[328,128]{1,0:T(8,128)S(1)} %get-tuple-element.23.a_ref, f32[328,128]{1,0:T(8,128)S(1)} %collective-permute-done.3.b_ref, f32[328,128]{1,0:T(8,128)S(1)} %collective-permute-done.4.c_ref, f32[328,128]{1,0:T(8,128)S(1)} %collective-permute-done.5.d_ref, ...), custom_call_target="tpu_custom_call" | custom-call | tf_op jit(solution)/shard_map/last/pallas_call | solution.py:376
  (3 shorter events, 0.1 us)
Async XLA Ops:
  5.4 24.9 %all-to-all-start = ((f32[32,16,128]{2,1,0:T(8,128)}), f32[32,16,128]{2,1,0:T(8,128)S(1)}, u32[]{:S(2)}, u32[]{:S(2)}) async-start(f32[32,16,128]{2,1,0:T(8,128)} %get-tuple-element.27), calls=%async_computation | async-start | bytes 524288 | tf_op jit(solution)/shard_map/all_to_all | solution.py:368
  19.1 36.9 %collective-permute-start = (f32[1288,128]{1,0:T(8,128)}, f32[1288,128]{1,0:T(8,128)S(1)}, u32[]{:S(2)}, u32[]{:S(2)}) collective-permute-start(f32[1288,128]{1,0:T(8,128)} %get-tuple-element.20), channel_id=1, source_target_pairs={{0,64},{32,96},{64,0},{96,32},{1,65},{33,97},{65,1},{97,33},{2,66}... | collective-permute-start | bytes 1978376 | tf_op jit(solution)/shard_map/ppermute | solution.py:336
  23.8 32.4 %collective-permute-start.1 = (f32[1288,128]{1,0:T(8,128)}, f32[1288,128]{1,0:T(8,128)S(1)}, u32[]{:S(2)}, u32[]{:S(2)}) collective-permute-start(f32[1288,128]{1,0:T(8,128)} %get-tuple-element.21), channel_id=1, source_target_pairs={{0,32},{32,64},{64,96},{96,0},{1,33},{33,65},{65,97},{97,1},{2,34}... | collective-permute-start | bytes 1978376 | tf_op jit(solution)/shard_map/ppermute | solution.py:336
  26.0 30.2 %collective-permute-start.2 = (f32[1288,128]{1,0:T(8,128)}, f32[1288,128]{1,0:T(8,128)S(1)}, u32[]{:S(2)}, u32[]{:S(2)}) collective-permute-start(f32[1288,128]{1,0:T(8,128)} %get-tuple-element.22), channel_id=1, source_target_pairs={{0,96},{32,0},{64,32},{96,64},{1,97},{33,1},{65,33},{97,65},{2,98}... | collective-permute-start | bytes 1978376 | tf_op jit(solution)/shard_map/ppermute | solution.py:336
  30.3 25.7 %copy-start = (f32[1288,128]{1,0:T(8,128)S(1)}, f32[1288,128]{1,0:T(8,128)}, u32[]{:S(2)}) copy-start(f32[1288,128]{1,0:T(8,128)} %get-tuple-element.19.a_ref) | copy-start | bytes 1978372
  49.5 18.4 %all-to-all-start.2 = ((f32[32,16,128]{2,1,0:T(8,128)}), f32[32,16,128]{2,1,0:T(8,128)S(1)}, u32[]{:S(2)}, u32[]{:S(2)}) async-start(f32[32,16,128]{2,1,0:T(8,128)} %broadcast_in_dim.22), calls=%async_computation.2 | async-start | bytes 524288 | tf_op jit(solution)/shard_map/all_to_all | solution.py:371
  56.3 19.1 %collective-permute-start.3 = (f32[328,128]{1,0:T(8,128)S(1)}, f32[328,128]{1,0:T(8,128)S(1)}, u32[]{:S(2)}, u32[]{:S(2)}) collective-permute-start(f32[328,128]{1,0:T(8,128)S(1)} %get-tuple-element.24), channel_id=1, source_target_pairs={{0,256},{128,384},{256,0},{384,128},{1,257},{129,385},{257,1},{385... | collective-permute-start | bytes 503816 | tf_op jit(solution)/shard_map/ppermute | solution.py:336
  60.1 15.3 %collective-permute-start.4 = (f32[328,128]{1,0:T(8,128)S(1)}, f32[328,128]{1,0:T(8,128)S(1)}, u32[]{:S(2)}, u32[]{:S(2)}) collective-permute-start(f32[328,128]{1,0:T(8,128)S(1)} %get-tuple-element.25), channel_id=1, source_target_pairs={{0,128},{128,256},{256,384},{384,0},{1,129},{129,257},{257,385},{3... | collective-permute-start | bytes 503816 | tf_op jit(solution)/shard_map/ppermute | solution.py:336
  63.3 12.8 %collective-permute-start.5 = (f32[328,128]{1,0:T(8,128)S(1)}, f32[328,128]{1,0:T(8,128)S(1)}, u32[]{:S(2)}, u32[]{:S(2)}) collective-permute-start(f32[328,128]{1,0:T(8,128)S(1)} %get-tuple-element.26), channel_id=1, source_target_pairs={{0,384},{128,0},{256,128},{384,256},{1,385},{129,1},{257,129},{385... | collective-permute-start | bytes 503816 | tf_op jit(solution)/shard_map/ppermute | solution.py:336
